TPU v7x, 32 devices: a whole 2x2x4 slice. The times are simulated.
32 devices in a mesh: dp: 8 (over y, x, core), red: 4 (over z).
Axes of the slice: x: 2, y: 2, z: 4, core: 2. Of those that a mesh axis runs over, the one named last changes fastest.
Arguments:
- frames: bfloat16 [512, 48, 1536], P(('dp', 'red')), may hold values from -36 to 36
- cotangent: bfloat16 [512, 48, 1536], P(('dp', 'red')), may hold values from -6 to 6
- w_in: bfloat16 [1536, 3072], P('red'), may hold values from -0.15625 to 0.15625
- kernel: float32 [31, 1536], replicated, may hold values from -1 to 1
- gain: float32 [1536], replicated, may hold values from 0.25 to 1.75
- lengths: int32 [512], replicated, may hold values from 1 to 47, as said below
Outputs:
- module_output: bfloat16 [512, 48, 1536], P(('dp', 'red'))
- frame_gradient: bfloat16 [512, 48, 1536], P(('dp', 'red'))
- grad_w_in: float32 [1536, 3072], P('red')
- grad_kernel: float32 [31, 1536], replicated
- grad_gain: float32 [1536], replicated
Inputs may be any that keep to these rules, and one draw needn't show every extreme that they name: The slots of each device, in order, form 8 groups of 2 slots. The q-th slot of group j on the device with dp index i and red index r and the q-th slot of group j on the device with dp index (2 j + 1 - i) mod 8 and the same red index have lengths that sum to exactly 48. The slots of dp index 0 all hold at least three quarters of 48 frames, rounded up.
All inputs are finite; a program needn't handle non-finite values.
Results may differ from a plain program's by a relative error of at most 0.0054.
Values may be sent and summed in bfloat16 or wider, within the bound.
No kernel may reach another device: no remote copies, remote signals or barrier semaphores. Data moves between devices by JAX's collectives and lax.ppermute only.
A program may use at most 128 MiB of HBM per device.

v0:
```python
import jax
import jax.numpy as jnp
from jax import lax
from jax.sharding import PartitionSpec as P

EPSILON = 1e-05


def normalize(widened_frames):
    center = widened_frames - jnp.mean(widened_frames, axis=-1, keepdims=True)
    inv_std = lax.rsqrt(jnp.mean(center * center, axis=-1, keepdims=True) + EPSILON)
    return (center * inv_std, inv_std)


def block_pass(frames, cotangent, valid_frame_mask, segment, weights, kernel, gain):
    row_count, length, model_width = frames.shape
    tap_count = kernel.shape[0]
    reach = tap_count // 2
    widened_frames = frames.astype(jnp.float32)
    normed, inv_std = normalize(widened_frames)
    scaled = (normed * gain).astype(jnp.bfloat16)
    flat_in = scaled.reshape(row_count * length, model_width)
    hidden = jnp.dot(flat_in, weights, preferred_element_type=jnp.float32)
    hidden = hidden.reshape(row_count, length, 2 * model_width)
    value_portion = hidden[..., :model_width]
    gate_sigmoid = jax.nn.sigmoid(hidden[..., model_width:])
    frame_validity = valid_frame_mask.astype(jnp.float32)[..., None]
    gated_linear_output = value_portion * gate_sigmoid * frame_validity
    padded = jnp.pad(gated_linear_output, ((0, 0), (reach, reach), (0, 0)))
    seg_pad = jnp.pad(segment, ((0, 0), (reach, reach)), constant_values=-1)
    convolved_frames = jnp.zeros_like(gated_linear_output)
    for offset in range(tap_count):
        window = padded[:, offset : offset + length]
        same_seg = (seg_pad[:, offset : offset + length] == segment).astype(jnp.float32)[..., None]
        convolved_frames = convolved_frames + kernel[offset] * (window * same_seg)
    swish_activation = jax.nn.sigmoid(convolved_frames)
    module_output = (
        (widened_frames + convolved_frames * swish_activation) * frame_validity
    ).astype(jnp.bfloat16)
    incoming_gradient = cotangent.astype(jnp.float32) * frame_validity
    grad_conv = incoming_gradient * (
        swish_activation * (1.0 + convolved_frames * (1.0 - swish_activation))
    )
    grad_pad = jnp.pad(grad_conv, ((0, 0), (reach, reach), (0, 0)))
    gated_linear_gradient = jnp.zeros_like(gated_linear_output)
    kernel_terms = []
    for offset in range(tap_count):
        window = padded[:, offset : offset + length]
        same_seg = (seg_pad[:, offset : offset + length] == segment).astype(jnp.float32)[..., None]
        kernel_terms.append(jnp.sum(grad_conv * window * same_seg, axis=(0, 1)))
        back_start = 2 * reach - offset
        back_same = (seg_pad[:, back_start : back_start + length] == segment).astype(jnp.float32)[
            ..., None
        ]
        gated_linear_gradient = gated_linear_gradient + kernel[offset] * (
            grad_pad[:, back_start : back_start + length] * back_same
        )
    gated_linear_gradient = gated_linear_gradient * frame_validity
    grad_hidden = jnp.concatenate(
        [
            gated_linear_gradient * gate_sigmoid,
            gated_linear_gradient * value_portion * gate_sigmoid * (1.0 - gate_sigmoid),
        ],
        axis=-1,
    ).astype(jnp.bfloat16)
    flat_grad = grad_hidden.reshape(row_count * length, 2 * model_width)
    grad_scaled = lax.dot_general(
        flat_grad, weights, (((1,), (1,)), ((), ())), preferred_element_type=jnp.float32
    )
    grad_scaled = grad_scaled.reshape(row_count, length, model_width)
    gain_term = jnp.sum(grad_scaled * normed, axis=(0, 1))
    grad_normed = grad_scaled * gain
    frame_gradient = incoming_gradient + inv_std * (
        grad_normed
        - jnp.mean(grad_normed, axis=-1, keepdims=True)
        - normed * jnp.mean(grad_normed * normed, axis=-1, keepdims=True)
    )
    frame_gradient = (frame_gradient * frame_validity).astype(jnp.bfloat16)
    return (module_output, frame_gradient, flat_in, flat_grad, jnp.stack(kernel_terms), gain_term)


def local(frames, cotangent, w_in, kernel, gain, lengths):
    dp_size = lax.axis_size("dp")
    red_size = lax.axis_size("red")
    dp_index = lax.axis_index("dp")
    red_index = lax.axis_index("red")
    local_utts, length, model_width = frames.shape
    weights = lax.all_gather(w_in, "red", axis=0, tiled=True)
    positions = jnp.arange(length, dtype=jnp.int32)
    by_owner = lengths.reshape(dp_size, red_size, local_utts)
    own_lengths = lax.dynamic_slice(by_owner, (dp_index, red_index, 0), (1, 1, local_utts)).reshape(
        local_utts
    )
    valid_frame_mask = positions[None, :] < own_lengths[:, None]
    segment = jnp.where(valid_frame_mask, 0, 1).astype(jnp.int32)
    module_output, frame_gradient, flat_in, flat_grad, kernel_part, gain_part = block_pass(
        frames, cotangent, valid_frame_mask, segment, weights, kernel, gain
    )
    grad_scale = lax.rsqrt(jnp.sum(lengths).astype(jnp.float32))
    block_rows = model_width // (dp_size * red_size)
    ordered = flat_in.reshape(-1, red_size, dp_size, block_rows)
    ordered = jnp.transpose(ordered, (0, 2, 1, 3)).reshape(-1, model_width)
    owned_rows = lax.psum_scatter(
        lax.dot_general(
            ordered, flat_grad, (((0,), (0,)), ((), ())), preferred_element_type=jnp.float32
        ),
        ("dp", "red"),
        scatter_dimension=0,
        tiled=True,
    )
    grad_weights = lax.all_gather(owned_rows, "dp", axis=0, tiled=True)
    kernel_total, gain_total = lax.psum((kernel_part, gain_part), ("dp", "red"))
    return (
        module_output,
        frame_gradient,
        grad_weights * grad_scale,
        kernel_total * grad_scale,
        gain_total * grad_scale,
    )


def solution(mesh):
    placed = (
        P(("dp", "red"), None, None),
        P(("dp", "red"), None, None),
        P("red", None),
        P(),
        P(),
        P(),
    )
    return jax.shard_map(
        local,
        mesh=mesh,
        in_specs=placed,
        out_specs=(
            P(("dp", "red"), None, None),
            P(("dp", "red"), None, None),
            P("red", None),
            P(),
            P(),
        ),
        check_vma=False,
    )
```

profile of v0, /device:TPU:0, one launch (start us, length us, event | category | flops | bytes accessed | tf_op | source)
XLA Modules:
  0.0 677.3 jit_solution(7808285599320160932)
XLA Ops:
  7.2 0.0 all-gather.3.cloned.1.call-start
  7.2 0.7 all-gather.3.cloned.1.call-update
  7.9 0.0 reduce-scatter.2.cloned.1.call-start
  8.0 0.8 reshape.138
  8.7 2.1 convert_reduce_fusion
  10.8 0.8 fusion.18
  11.6 0.6 copy-done.17
  12.2 2.2 fusion.10
  14.4 9.5 %reshape_reshape.3 = bf16[768,4,8,48]{3,2,1,0:T(8,128)(2,1)} reshape(bf16[16,48,1536]{2,1,0:T(8,128)(2,1)} %fusion.10) | data formatting | bytes 4718592 | tf_op jit(solution)/shard_map/reshape;reshape | solution.py:101
  23.8 8.2 %copy.11 = bf16[768,8,4,48]{0,3,2,1:T(8,128)(2,1)} copy(bf16[768,8,4,48]{3,1,2,0:T(8,128)(2,1)} %bitcast.17) | data formatting | bytes 4718592 | tf_op jit(solution)/shard_map/transpose | solution.py:102
  32.1 0.2 slice_reduce_fusion.29
  32.3 0.3 slice_reduce_fusion.30
  32.7 0.1 fusion.122
  32.7 0.1 fusion.151
  32.8 0.1 fusion.133
  32.9 0.1 fusion.142
  33.0 0.1 fusion.124
  33.1 146.0 %all-gather.3.cloned.1.call-done = bf16[1536,3072]{1,0:T(8,128)(2,1)} async-done(((bf16[384,3072]{1,0:T(8,128)(2,1)}), bf16[1536,3072]{1,0:T(8,128)(2,1)}) %all-gather.3.cloned.1.call-update) | async-done | bytes 9437200 | tf_op jit(solution)/shard_map/all_gather | solution.py:88
  179.1 10.7 %fusion.2 = f32[16,48,3072]{2,1,0:T(8,128)S(1)} fusion(bf16[16,48,1536]{2,1,0:T(8,128)(2,1)} %fusion.10, bf16[1536,3072]{1,0:T(8,128)(2,1)} %all-gather.3.cloned.1.call-done), kind=kOutput, calls=%fused_computation.62 | convolution fusion | flops 7247757312 | bytes 21233664 | tf_op jit(solution)/shard_map/dot_general | solution.py:23
  189.9 1.3 multiply_multiply_fusion.1
  191.2 2.7 copy-done.3
  193.9 49.3 %multiply_reduce_fusion = (f32[1536]{0:T(1024)}, f32[1536]{0:T(1024)}, f32[1536]{0:T(1024)}, f32[1536]{0:T(1024)}, f32[1536]{0:T(1024)}, /*index=5*/f32[1536]{0:...) fusion(f32[16,48,1536]{2,1,0:T(8,128)S(1)} %multiply_multiply_f, ...), kind=kLoop, calls=%fused_computation.186 | loop fusion | flops 150981120 | bytes 16856064 | tf_op jit(solution)/shard_map/reduce_sum | solution.py:50
  243.2 28.6 %multiply_convert_fusion.1 = (bf16[16,48,1536]{2,1,0:T(8,128)(2,1)S(1)}, f32[16,48,1536]{2,1,0:T(8,128)}) fusion(f32[16,48,3072]{2,1,0:T(8,128)} %copy-done.3, f32[16,48]{1,0:T(8,128)S(1)} %get-tuple-element.106, f32[16,48]{1,0:T(8,128)S(1)} %get-tuple-element.76, f32[1536]{0:T(1024)} %copy-done.15, f32[16,48]{1,0:T(8,128)S(1)} %get-tuple-element.77, ...), kind=kLoop, calls=%fused_computation.218 | loop fusion | flops 114425856 | bytes 16800768 | tf_op jit(solution)/shard_map/convert.4
  271.8 6.9 %multiply_convert_fusion = bf16[16,48,1536]{2,1,0:T(8,128)(2,1)S(1)} fusion(f32[16,48,1536]{2,1,0:T(8,128)} %get-tuple-element.73, f32[16,48,3072]{2,1,0:T(8,128)} %copy-done.3), kind=kLoop, calls=%fused_computation.217 | loop fusion | flops 9437184 | bytes 16515072 | tf_op jit(solution)/shard_map/convert.5
  278.7 1.4 copy-done.7
  280.1 10.8 %fusion.118 = f32[1536,3072]{1,0:T(8,128)} fusion(bf16[768,1536]{0,1:T(8,128)(2,1)S(1)} %bitcast.20, bf16[768,1536]{1,0:T(8,128)(2,1)S(1)} %bitcast.19, bf16[768,1536]{1,0:T(8,128)(2,1)S(1)} %bitcast.18), kind=kOutput, calls=%fused_computation.182 | convolution fusion | flops 7257194496 | bytes 25952256 | tf_op jit(solution)/shard_map/dot_general | solution.py:104
  291.0 0.0 reduce-scatter.2.cloned.1.call-update
  291.0 0.0 all-reduce.5.cloned.1.call-start
  291.1 0.6 copy-done.29
  291.6 0.0 copy-done.28
  291.6 0.0 copy-done.27
  291.8 11.0 %multiply_reduce_fusion.27 = (f32[1536]{0:T(1024)S(1)}, f32[1536]{0:T(1024)S(1)}, f32[1536]{0:T(1024)S(1)}, f32[1536]{0:T(1024)S(1)}) fusion(f32[16,48,1536]{2,1,0:T(8,128)} %copy-done.1, f32[16,48,1536]{2,1,0:T(8,128)} %copy-done, f32[16,48]{1,0:T(8,128)S(1)} %get-tuple-element.79, f32[16,48]{1,0:T(8,128)S(1)} %get-tuple-element.78, ...), kind=kLoop, calls=%fused_computation.213 | loop fusion | flops 14149632 | bytes 9474048 | tf_op jit(solution)/shard_map/reduce_sum | solution.py:50
  302.9 24.8 %multiply_reduce_fusion.9 = (f32[1536]{0:T(1024)S(1)}, f32[1536]{0:T(1024)S(1)}, f32[1536]{0:T(1024)S(1)}, f32[1536]{0:T(1024)S(1)}, f32[1536]{0:T(1024)S(1)}, /...) fusion(f32[16,48,1536]{2,1,0:T(8,128)S(1)} %copy-done.2, ...), kind=kLoop, calls=%fused_computation.195 | loop fusion | flops 30657024 | bytes 9517056 | tf_op jit(solution)/shard_map/reduce_sum | solution.py:50
  327.7 8.8 %multiply_reduce_fusion.18 = (f32[1536]{0:T(1024)S(1)}, f32[1536]{0:T(1024)S(1)}, f32[1536]{0:T(1024)S(1)}, f32[1536]{0:T(1024)S(1)}, f32[1536]{0:T(1024)S(1)}, ...) fusion(f32[16,48,1536]{2,1,0:T(8,128)S(1)} %copy-done.2, ...), kind=kLoop, calls=%fused_computation.204 | loop fusion | flops 31836672 | bytes 9520128 | tf_op jit(solution)/shard_map/reduce_sum | solution.py:50
  336.7 2.8 stack.127
  339.5 0.0 all-reduce.5.cloned.1.call-update
  339.5 0.0 all-gather.5.cloned.1.call-start
  339.6 156.5 %reduce-scatter.2.cloned.1.call-done = f32[48,3072]{1,0:T(8,128)} async-done(((f32[1536,3072]{1,0:T(8,128)}), f32[48,3072]{1,0:T(8,128)}) %reduce-scatter.2.cloned.1.call-update) | async-done | bytes 589840 | tf_op jit(solution)/shard_map/reduce_scatter | solution.py:103
  496.1 0.0 all-gather.5.cloned.1.call-update
  496.1 0.7 reduce_sum.337
  497.5 14.5 %fusion.17 = (f32[1536]{0:T(1024)S(1)}, f32[16,48]{1,0:T(8,128)S(1)}, f32[16,48]{1,0:T(8,128)S(1)}, f32[16,48,1536]{2,1,0:T(8,128)}) fusion(bf16[16,48,1536]{2,1,0:T(8,128)(2,1)S(1)} %copy-done.4, f32[16,48]{1,0:T(8,128)S(1)} %copy-done.18, f32[16,48]{1,0:T(8,128)S(1)} %broadcast_multiply_fusion.5, f32[1536]{0:T(1024)S(1)} %copy-done.20, ...), kind=kOutput, calls=%fused_computation.80 | convolution fusion | flops 7267808256 | bytes 21258240 | tf_op jit(solution)/shard_map/dot_general | solution.py:67
  512.0 39.1 %psum.15 = f32[1536]{0:T(1024)S(1)} all-reduce(f32[1536]{0:T(1024)S(1)} %get-tuple-element.36), channel_id=1, replica_groups=mesh['dp'=8,'red'=4] {'dp','red'}, use_global_device_ids=true, to_apply=%region_39.40 | all-reduce | flops 1536 | bytes 12288 | tf_op jit(solution)/shard_map/psum | solution.py:112
  551.2 0.6 broadcast_multiply_fusion.2
  551.8 7.8 %fusion.16 = (bf16[16,48,1536]{2,1,0:T(8,128)(2,1)}, bf16[16,48,1536]{2,1,0:T(8,128)(2,1)}) fusion(bf16[16,48,1536]{2,1,0:T(8,128)(2,1)S(1)} %copy-done.4, bf16[16,48,1536]{2,1,0:T(8,128)(2,1)} %param.7, f32[16,48,1536]{2,1,0:T(8,128)} %get-tuple-element.107, f32[16,48]{1,0:T(8,128)S(1)} %get-tuple-element.108, f32[16,48]{1,0:T(8,128)S(1)} %get-tuple-element.109, ...), kind=kLoop, calls=%fused_computation.79 | loop fusion | flops 23592960 | bytes 18895872 | tf_op jit(solution)/shard_map/convert_element_type | solution.py:78
  559.6 64.5 %all-reduce.5.cloned.1.call-done = f32[31,1536]{1,0:T(8,128)} async-done(((f32[31,1536]{1,0:T(8,128)}), f32[31,1536]{1,0:T(8,128)}) %all-reduce.5.cloned.1.call-update) | async-done | bytes 190480 | tf_op jit(solution)/shard_map/psum | solution.py:112
  624.1 1.6 broadcast_multiply_fusion.1
  625.7 40.0 %all-gather.5.cloned.1.call-done = f32[384,3072]{1,0:T(8,128)} async-done(((f32[48,3072]{1,0:T(8,128)}), f32[384,3072]{1,0:T(8,128)}) %all-gather.5.cloned.1.call-update) | async-done | bytes 4718608 | tf_op jit(solution)/shard_map/all_gather | solution.py:111
  665.7 5.1 broadcast_multiply_fusion
  (96 shorter events, 0.4 us)
Async XLA Ops:
  7.2 3.6 copy-start.4
  7.2 5.0 copy-start.19
  7.2 171.9 %all-gather.3.cloned.1.call-start = ((), (), s32[]{:S(2)}) async-start(), calls=%async_computation.1 | async-start | bytes 11796480 | tf_op jit(solution)/shard_map/all_gather | solution.py:88
  7.9 488.2 %reduce-scatter.2.cloned.1.call-start = ((), (), s32[]{:S(2)}) async-start(), calls=%async_computation.2 | async-start | bytes 19464192 | tf_op jit(solution)/shard_map/reduce_scatter | solution.py:103
  11.6 0.6 copy-start.17
  23.8 8.2 %copy-start.9 = (f32[31,1536]{1,0:T(8,128)S(1)}, f32[31,1536]{1,0:T(8,128)}, u32[]{:S(2)}) copy-start(f32[31,1536]{1,0:T(8,128)} %param.9) | copy-start | bytes 571396
  32.3 161.6 %copy-start.10 = (f32[1536]{0:T(1024)}, f32[1536]{0:T(1024)S(1)}, u32[]{:S(2)}) copy-start(f32[1536]{0:T(1024)S(1)} %get-tuple-element.63) | copy-start | bytes 18436
  32.3 161.6 %copy-start.11 = (f32[1536]{0:T(1024)}, f32[1536]{0:T(1024)S(1)}, u32[]{:S(2)}) copy-start(f32[1536]{0:T(1024)S(1)} %get-tuple-element.64) | copy-start | bytes 18436
  32.3 161.5 %copy-start.12 = (f32[1536]{0:T(1024)}, f32[1536]{0:T(1024)S(1)}, u32[]{:S(2)}) copy-start(f32[1536]{0:T(1024)S(1)} %get-tuple-element.65) | copy-start | bytes 18436
  32.3 161.5 %copy-start.13 = (f32[1536]{0:T(1024)}, f32[1536]{0:T(1024)S(1)}, u32[]{:S(2)}) copy-start(f32[1536]{0:T(1024)S(1)} %get-tuple-element.66) | copy-start | bytes 18436
  32.3 161.5 %copy-start.14 = (f32[1536]{0:T(1024)}, f32[1536]{0:T(1024)S(1)}, u32[]{:S(2)}) copy-start(f32[1536]{0:T(1024)S(1)} %get-tuple-element.67) | copy-start | bytes 18436
  32.3 161.5 %copy-start.15 = (f32[1536]{0:T(1024)}, f32[1536]{0:T(1024)S(1)}, u32[]{:S(2)}) copy-start(f32[1536]{0:T(1024)S(1)} %get-tuple-element.68) | copy-start | bytes 18436
  32.3 161.5 %copy-start.16 = (f32[1536]{0:T(1024)}, f32[1536]{0:T(1024)S(1)}, u32[]{:S(2)}) copy-start(f32[1536]{0:T(1024)S(1)} %get-tuple-element.69) | copy-start | bytes 18436
  189.8 4.0 copy-start.3
  189.8 4.0 copy-start.5
  193.8 49.3 %copy-start = (f32[16,48,1536]{2,1,0:T(8,128)}, f32[16,48,1536]{2,1,0:T(8,128)S(1)}, u32[]{:S(2)}) copy-start(f32[16,48,1536]{2,1,0:T(8,128)S(1)} %multiply_multiply_fusion.1) | copy-start | bytes 14155780
  243.2 28.6 %copy-start.1 = (f32[16,48,1536]{2,1,0:T(8,128)}, f32[16,48,1536]{2,1,0:T(8,128)S(1)}, u32[]{:S(2)}) copy-start(f32[16,48,1536]{2,1,0:T(8,128)S(1)} %get-tuple-element.70) | copy-start | bytes 14155780
  271.8 6.9 %copy-start.6 = (bf16[16,48,1536]{2,1,0:T(8,128)(2,1)}, bf16[16,48,1536]{2,1,0:T(8,128)(2,1)S(1)}, u32[]{:S(2)}) copy-start(bf16[16,48,1536]{2,1,0:T(8,128)(2,1)S(1)} %get-tuple-element.72) | copy-start | bytes 7077892
  271.8 8.3 %copy-start.8 = (bf16[768,8,4,48]{0,3,2,1:T(8,128)(2,1)S(1)}, bf16[768,8,4,48]{0,3,2,1:T(8,128)(2,1)}, u32[]{:S(2)}) copy-start(bf16[768,8,4,48]{0,3,2,1:T(8,128)(2,1)} %copy.11) | copy-start | bytes 7077892
  278.7 1.4 copy-start.7
  290.9 0.7 copy-start.29
  290.9 0.7 copy-start.28
  290.9 0.7 copy-start.27
  290.9 0.7 copy-start.26
  290.9 0.8 copy-start.25
  290.9 0.8 copy-start.24
  291.0 0.8 copy-start.23
  291.0 0.8 copy-start.22
  291.0 0.8 copy-start.21
  291.0 333.1 %all-reduce.5.cloned.1.call-start = ((), (), s32[]{:S(2)}) async-start(), calls=%async_computation.4 | async-start | bytes 393216 | tf_op jit(solution)/shard_map/psum | solution.py:112
  291.8 11.1 %copy-start.2 = (f32[16,48,1536]{2,1,0:T(8,128)S(1)}, f32[16,48,1536]{2,1,0:T(8,128)}, u32[]{:S(2)}) copy-start(f32[16,48,1536]{2,1,0:T(8,128)} %copy-done.1) | copy-start | bytes 14155780
  291.8 35.9 %slice-start = ((s8[4718592]{0:T(1024)(128)(4,1)}), s8[524288]{0:T(1024)(128)(4,1)S(1)}, s32[]{:S(2)}) async-start(s8[4718592]{0:T(1024)(128)(4,1)} %bitcast.15), calls=%async_computation.5 | async-start | bytes 1048576
  302.9 24.8 %slice-start.1 = ((s8[4718592]{0:T(1024)(128)(4,1)}), s8[4194304]{0:T(1024)(128)(4,1)S(1)}, s32[]{:S(2)}) async-start(s8[4718592]{0:T(1024)(128)(4,1)} %bitcast.15), calls=%async_computation.6 | async-start | bytes 8388608
  327.7 168.4 %copy-start.30 = (s32[512]{0:T(512)S(1)}, s32[512]{0:T(512)}, u32[]{:S(2)}) copy-start(s32[512]{0:T(512)} %param.11) | copy-start | bytes 6148
  327.7 169.8 %copy-start.18 = (f32[16,48]{1,0:T(8,128)S(1)}, f32[16,48]{1,0:T(8,128)}, u32[]{:S(2)}) copy-start(f32[16,48]{1,0:T(8,128)} %copy-done.17) | copy-start | bytes 9220
  327.7 169.8 %copy-start.20 = (f32[1536]{0:T(1024)S(1)}, f32[1536]{0:T(1024)}, u32[]{:S(2)}) copy-start(f32[1536]{0:T(1024)} %param.10) | copy-start | bytes 18436
  339.5 326.2 %all-gather.5.cloned.1.call-start = ((), (), s32[]{:S(2)}) async-start(), calls=%async_computation.3 | async-start | bytes 5308416 | tf_op jit(solution)/shard_map/all_gather | solution.py:111
Sparse Core Ops, SparseCore 0:
  9.6 169.4 all-gather.2
  291.1 204.9 reduce-scatter.1
  502.2 121.8 all-reduce.4
  625.9 39.8 all-gather.4
where the time goes:
time: 678 us; the launch traced here: 677 us
  waiting for transfers between devices  408 us (60%)
  other arithmetic  152 us (22%)
  blocking collectives  39.1 us (6%)
  matrix products  36.1 us (5%)
  local copies, waits for them, and re-layouts  27.3 us (4%)
  between operations  15.2 us (2%)
    reduce_scatter x1, waiting for transfers between devices, local(): lax.psum_scatter(lax.dot_general(ordered, flat_grad, (((0,), (0,)), ((),...  156 us
    all_gather x1, waiting for transfers between devices, local(): weights = lax.all_gather(w_in, 'red', axis=0, tiled=True)  146 us
    reduce_sum x4, other arithmetic, block_pass(): kernel_terms.append(jnp.sum(grad_conv * window * same_seg, axis=(0, 1)))  93.8 us
    psum x1, waiting for transfers between devices, local(): kernel_total, gain_total = lax.psum((kernel_part, gain_part), ('dp', 'red'))  64.5 us
    all_gather x1, waiting for transfers between devices, local(): grad_weights = lax.all_gather(owned_rows, 'dp', axis=0, tiled=True)  40 us
    psum x1, blocking collectives, local(): kernel_total, gain_total = lax.psum((kernel_part, gain_part), ('dp', 'red'))  39.1 us
    another operation x2, other arithmetic  35.5 us
    dot_general x1, matrix products, block_pass(): lax.dot_general(flat_grad, weights, (((1,), (1,)), ((), ())), preferred_e...  14.5 us
  transfers between devices with their start and end apart: 4, of which 4 were waited for; matrix products, arithmetic and copies ran while one was open for 14% of the time, Pallas kernels for 0%

commit v1 on v0

v1 whole, which is shorter than its diff:
```python
import functools

import jax
import jax.numpy as jnp
import numpy as np
from jax import lax
from jax.experimental import pallas as pl
from jax.experimental.pallas import tpu as pltpu
from jax.sharding import PartitionSpec as P

EPSILON = 1e-05
GROUP = 4
VMEM_LIMIT = 44 * 1024 * 1024
CHUNKS = ((0, 512), (512, 512), (1024, 512))


def split_bf16(x):
    high = x.astype(jnp.bfloat16)
    low = (x - high.astype(jnp.float32)).astype(jnp.bfloat16)
    return high, low


def time_transforms(length, taps):
    reach = taps // 2
    size = 16
    while size < length + reach:
        size *= 2
    half = size // 2
    f = np.arange(half)[:, None]
    t = np.arange(length)[None, :]
    angle = 2 * np.pi * f * t / size
    sign = np.where(np.arange(length) % 2 == 0, 1.0, -1.0)
    fwd_re, fwd_im = np.cos(angle), -np.sin(angle)
    fwd_im[0] = sign
    weight = np.where(np.arange(half) == 0, 1.0, 2.0)[:, None] / size
    inv_re, inv_im = (weight * np.cos(angle)).T, (-weight * np.sin(angle)).T
    inv_im[:, 0] = sign / size
    eye = np.eye(GROUP)
    forward = np.concatenate([np.kron(eye, fwd_re), np.kron(eye, fwd_im)], axis=0)
    inverse = np.concatenate([np.kron(eye, inv_re), np.kron(eye, inv_im)], axis=1)
    m = np.arange(taps) - reach
    tap_angle = 2 * np.pi * f * m[None, :] / size
    tap_sign = np.where(m % 2 == 0, 1.0, -1.0)
    hat_re, hat_im = np.cos(tap_angle), np.sin(tap_angle)
    hat_nyq = hat_re.copy()
    hat_nyq[0] = tap_sign
    hats = np.concatenate([hat_re, hat_im, hat_nyq], axis=0)
    back_1 = (weight * np.cos(tap_angle)).T
    back_2 = back_1.copy()
    back_2[:, 0] = tap_sign / size
    back_3 = (-weight * np.sin(tap_angle)).T
    back = np.concatenate([back_1, back_2, back_3], axis=1)
    return half, forward, inverse, hats.astype(np.float32), back.astype(np.float32)


def three_pass(matrix):
    high = matrix.astype(np.float32).astype(jnp.bfloat16)
    low = (matrix - high.astype(np.float64)).astype(np.float32).astype(jnp.bfloat16)
    return np.concatenate([high, low, high], axis=1)


def apply_three(matrix, x):
    high, low = split_bf16(x)
    return jnp.dot(
        matrix, jnp.concatenate([high, high, low], axis=0), preferred_element_type=jnp.float32
    )


def sigmoid(x):
    return 1.0 / (1.0 + jnp.exp(-x))


def chunk_kernel(red_size, half, length, has_out, idx, scaled, scaled_t, own_v, own_g, *rest):
    rest = list(rest)
    z_mine, xv, yg, z_sib, xv_sib, yg_sib = rest[:6]
    frames, cot, live, hats, fwd, inv = rest[6:12]
    rest = rest[12 + has_out :]
    out, keep, send, gh, w, sums = rest
    core, quarter, red, parity = idx[0], idx[1], idx[2], idx[3]
    width = own_v.shape[1]
    block = own_v.shape[0]
    part = block // 4

    def place(s, par, cor, v, g):
        owner = lax.rem(red + red_size - s, red_size)
        row = pl.multiple_of(owner * block + (par * 2 + cor) * part, 16)
        w[pl.ds(row, part), :width] = v
        w[pl.ds(row, part), width:] = g

    own_row = pl.multiple_of(red * block, 16)
    w[pl.ds(own_row, block), :width] = own_v[...]
    w[pl.ds(own_row, block), width:] = own_g[...]
    for s in range(1, red_size):
        place(s, parity, core, z_mine[s - 1, :, :width], z_mine[s - 1, :, width:])
        place(s, 1 - parity, core, xv[s - 1], yg[s - 1])
        place(s, parity, 1 - core, z_sib[s - 1, :, :width], z_sib[s - 1, :, width:])
        place(s, 1 - parity, 1 - core, xv_sib[s - 1], yg_sib[s - 1])

    rows = GROUP * length
    hat_a, hat_b, hat_c = hats[0], hats[1], hats[2]
    total = [jnp.zeros((half, width), jnp.float32) for _ in range(3)]
    for group in range(scaled.shape[0] // rows):
        at = pl.ds(group * rows, rows)
        hidden = jnp.dot(scaled[at, :], w[...], preferred_element_type=jnp.float32)
        alive = jnp.concatenate([live[at, :]] * (width // 128), axis=1)
        value = hidden[:, :width]
        gate = sigmoid(hidden[:, width:])
        glu = value * gate * alive
        x_hat = apply_three(fwd[...], glu).reshape(2, GROUP, half, width)
        x_re, x_im = x_hat[0], x_hat[1]
        y_hat = jnp.concatenate(
            [
                (x_re * hat_a - x_im * hat_b).reshape(GROUP * half, width),
                (x_re * hat_b + x_im * hat_c).reshape(GROUP * half, width),
            ],
            axis=0,
        )
        conv = apply_three(inv[...], y_hat)
        s = sigmoid(conv)
        out[at, :] = ((frames[at, :].astype(jnp.float32) + conv * s) * alive).astype(out.dtype)
        grad_conv = cot[at, :].astype(jnp.float32) * alive * (s * (1.0 + conv * (1.0 - s)))
        g_hat = apply_three(fwd[...], grad_conv).reshape(2, GROUP, half, width)
        g_re, g_im = g_hat[0], g_hat[1]
        total[0] = total[0] + jnp.sum(g_re * x_re, axis=0)
        total[1] = total[1] + jnp.sum(g_im * x_im, axis=0)
        total[2] = total[2] + jnp.sum(g_re * x_im - g_im * x_re, axis=0)
        back_hat = jnp.concatenate(
            [
                (g_re * hat_a + g_im * hat_b).reshape(GROUP * half, width),
                (g_im * hat_c - g_re * hat_b).reshape(GROUP * half, width),
            ],
            axis=0,
        )
        grad_glu = apply_three(inv[...], back_hat) * alive
        grad_v = grad_glu * gate
        gh[0, at, :] = grad_v.astype(jnp.bfloat16)
        gh[1, at, :] = (grad_v * value * (1.0 - gate)).astype(jnp.bfloat16)
    sums[...] = jnp.concatenate(total, axis=0)

    for dest, which in ((send, 1 - core), (keep, core)):
        grad = gh[which]
        for b in range(red_size):
            slot = lax.rem(b + red_size - red, red_size)
            res = jnp.dot(
                scaled_t[b * block : (b + 1) * block, :], grad, preferred_element_type=jnp.float32
            ).astype(jnp.bfloat16)
            for q in range(4):
                dest[lax.bitwise_xor(q, quarter), slot] = res[q * part : (q + 1) * part]


def frame_kernel(n_chunks, scaled_inv, frames, cot, live, gain, *rest):
    ghs, ws = rest[:n_chunks], rest[n_chunks : 2 * n_chunks]
    out, gain_sum = rest[2 * n_chunks :]
    model_width = frames.shape[1]
    grad_scaled = None
    for gh, w in zip(ghs, ws):
        width = w.shape[1] // 2
        for part in range(2):
            term = lax.dot_general(
                gh[part],
                w[:, part * width : (part + 1) * width],
                (((1,), (1,)), ((), ())),
                preferred_element_type=jnp.float32,
            )
            grad_scaled = term if grad_scaled is None else grad_scaled + term
    wide = frames[...].astype(jnp.float32)
    center = wide - jnp.mean(wide, axis=-1, keepdims=True)
    inv_std = lax.rsqrt(jnp.mean(center * center, axis=-1, keepdims=True) + EPSILON)
    normed = center * inv_std
    prod = grad_scaled * normed
    part_sum = jnp.sum(prod.reshape(-1, 8, model_width), axis=0)

    @pl.when(pl.program_id(0) == 0)
    def _():
        gain_sum[...] = part_sum

    @pl.when(pl.program_id(0) != 0)
    def _():
        gain_sum[...] += part_sum

    grad_normed = grad_scaled * gain[...]
    alive = jnp.concatenate([live[...]] * (model_width // 128), axis=1)
    upstream = cot[...].astype(jnp.float32) * alive
    res = upstream + inv_std * (
        grad_normed
        - jnp.mean(grad_normed, axis=-1, keepdims=True)
        - normed * jnp.mean(grad_normed * normed, axis=-1, keepdims=True)
    )
    out[...] = (res * alive).astype(out.dtype)


def place_kernel(has_out, idx, mine, sib, *rest):
    out = rest[has_out]
    core, quarter = idx[0], idx[1]
    part = mine.shape[1]

    def write(src):
        for r in range(4):
            q = lax.bitwise_xor(r, quarter)
            out[pl.ds(pl.multiple_of(q * part, 16), part), :] = src[r].astype(jnp.float32)

    own = pl.program_id(0) == core
    pl.when(own)(lambda: write(mine))
    pl.when(jnp.logical_not(own))(lambda: write(sib))


def vmem(n):
    return [pl.BlockSpec(memory_space=pltpu.VMEM) for _ in range(n)]


def tree_sum(terms):
    if len(terms) == 1:
        return terms[0]
    return tree_sum(terms[::2]) + tree_sum(terms[1::2])


def local(frames, cotangent, w_in, kernel, gain, lengths):
    dp_size = lax.axis_size("dp")
    red_size = lax.axis_size("red")
    dp = lax.axis_index("dp")
    red = lax.axis_index("red")
    local_utts, length, model_width = frames.shape
    taps = kernel.shape[0]
    block = model_width // red_size
    part = block // 4
    n_rows = local_utts * length

    core = dp % 2
    quarter = (dp // 2) % 4
    parity = (quarter + quarter // 2) % 2
    idx = jnp.stack([core, quarter, red, parity]).astype(jnp.int32)

    def to_core(x):
        return lax.ppermute(x, "dp", [(i, i ^ 1) for i in range(dp_size)])

    def to_quarter(x, r):
        return lax.ppermute(x, "dp", [(i, i ^ (2 * r)) for i in range(dp_size)])

    def shift_red(x, s):
        return lax.ppermute(x, "red", [(i, (i + s) % red_size) for i in range(red_size)])

    def other_groups(x):
        bit = 8
        while bit < dp_size:
            x = x + lax.ppermute(x, "dp", [(i, i ^ bit) for i in range(dp_size)])
            bit *= 2
        return x

    half, forward, inverse, hat_matrix, back_matrix = time_transforms(length, taps)
    fwd3, inv3 = jnp.asarray(three_pass(forward)), jnp.asarray(three_pass(inverse))

    piece = lax.dynamic_slice(w_in, ((parity * 2 + core) * part, 0), (part, 2 * model_width))
    gathered = []
    for start, width in CHUNKS:
        gate_start = model_width + start
        mine = jnp.concatenate(
            [piece[:, start : start + width], piece[:, gate_start : gate_start + width]], axis=1
        )
        z_mine = jnp.stack([shift_red(mine, s) for s in range(1, red_size)])
        z_sib = to_core(z_mine)
        xv = to_quarter(z_mine[:, :, :width], 1)
        yg = to_quarter(z_mine[:, :, width:], 2)
        xv_sib, yg_sib = to_core(xv), to_core(yg)
        own_v = w_in[:, start : start + width]
        own_g = w_in[:, gate_start : gate_start + width]
        gathered.append((own_v, own_g, z_mine, xv, yg, z_sib, xv_sib, yg_sib))

    flat_frames = frames.reshape(n_rows, model_width)
    flat_cot = cotangent.reshape(n_rows, model_width)
    wide = flat_frames.astype(jnp.float32)
    center = wide - jnp.mean(wide, axis=-1, keepdims=True)
    inv_std = lax.rsqrt(jnp.mean(center * center, axis=-1, keepdims=True) + EPSILON)
    scaled = (center * inv_std * gain).astype(jnp.bfloat16)
    scaled_t = scaled.T
    own_lengths = lax.dynamic_slice(
        lengths.reshape(dp_size, red_size, local_utts), (dp, red, 0), (1, 1, local_utts)
    ).reshape(local_utts)
    alive = (jnp.arange(length, dtype=jnp.int32)[None, :] < own_lengths[:, None]).astype(jnp.float32)
    live = jnp.broadcast_to(alive.reshape(n_rows, 1), (n_rows, 128))
    root = lax.rsqrt(jnp.sum(lengths).astype(jnp.float32))
    hats = jnp.dot(hat_matrix, kernel, precision=lax.Precision.HIGHEST).reshape(3, half, model_width)

    out = None
    grad_out = None
    ghs, ws, sums = [], [], []
    for (start, width), weights in zip(CHUNKS, gathered):
        column = start // width
        strip = pl.BlockSpec((n_rows, width), lambda i, column=column: (0, column))
        has_out = 0 if out is None else 1
        operands = [idx, scaled, scaled_t, *weights, flat_frames, flat_cot, live, hats, fwd3, inv3]
        in_specs = [pl.BlockSpec(memory_space=pltpu.SMEM), *vmem(10), strip, strip, *vmem(1)]
        in_specs += [
            pl.BlockSpec((3, half, width), lambda i, column=column: (0, 0, column)),
            *vmem(2),
        ]
        aliases = {}
        if has_out:
            aliases = {len(operands): 0}
            operands.append(out)
            in_specs.append(pl.BlockSpec(memory_space=pl.ANY))
        flops = 2 * n_rows * model_width * width * 4 + 2 * 12 * 256 * n_rows * width
        out, keep, send, gh, w, tap_sums = pl.pallas_call(
            functools.partial(chunk_kernel, red_size, half, length, has_out),
            grid=(1,),
            in_specs=in_specs,
            out_specs=[strip, *vmem(5)],
            out_shape=[
                jax.ShapeDtypeStruct((n_rows, model_width), jnp.bfloat16),
                jax.ShapeDtypeStruct((4, red_size, part, width), jnp.bfloat16),
                jax.ShapeDtypeStruct((4, red_size, part, width), jnp.bfloat16),
                jax.ShapeDtypeStruct((2, n_rows, width), jnp.bfloat16),
                jax.ShapeDtypeStruct((model_width, 2 * width), jnp.bfloat16),
                jax.ShapeDtypeStruct((3 * half, width), jnp.float32),
            ],
            input_output_aliases=aliases,
            compiler_params=pltpu.CompilerParams(vmem_limit_bytes=VMEM_LIMIT),
            cost_estimate=pl.CostEstimate(
                flops=flops, bytes_accessed=24 * 1024 * width, transcendentals=4 * n_rows * width
            ),
        )(*operands)
        ghs.append(gh)
        ws.append(w)
        sums.append(tap_sums)

        pair = keep.astype(jnp.float32) + to_core(send).astype(jnp.float32)
        pair = pair.astype(jnp.bfloat16)
        parts = [pair[0], *(to_quarter(pair[r], r) for r in range(1, 4))]
        plane = tree_sum([p.astype(jnp.float32) for p in parts]).astype(jnp.bfloat16)
        parts = [plane[0], *(shift_red(plane[s], s) for s in range(1, red_size))]
        owned = other_groups(tree_sum([p.astype(jnp.float32) for p in parts]))
        owned = (owned * root).astype(jnp.bfloat16)
        mine = jnp.stack([owned, *(to_quarter(owned, r) for r in range(1, 4))])
        sib = to_core(mine)
        has_out = 0 if grad_out is None else 1
        operands = [idx, mine, sib] + ([grad_out] if has_out else [])
        half_step = model_width // width
        grad_out = pl.pallas_call(
            functools.partial(place_kernel, has_out),
            grid=(2,),
            in_specs=[
                pl.BlockSpec(memory_space=pltpu.SMEM),
                *vmem(2),
                *([pl.BlockSpec(memory_space=pl.ANY)] if has_out else []),
            ],
            out_specs=pl.BlockSpec(
                (block, width),
                lambda i, column=column, half_step=half_step: (0, column + i * half_step),
            ),
            out_shape=jax.ShapeDtypeStruct((block, 2 * model_width), jnp.float32),
            input_output_aliases={3: 0} if has_out else {},
            cost_estimate=pl.CostEstimate(
                flops=0, bytes_accessed=12 * block * width, transcendentals=0
            ),
        )(*operands)

    step = GROUP * length
    row_spec = pl.BlockSpec((step, model_width), lambda i: (i, 0))
    frame_gradient, gain_part = pl.pallas_call(
        functools.partial(frame_kernel, len(CHUNKS), None),
        grid=(n_rows // step,),
        in_specs=[
            row_spec,
            row_spec,
            pl.BlockSpec((step, 128), lambda i: (i, 0)),
            *vmem(1),
            *(pl.BlockSpec((2, step, width), lambda i: (0, i, 0)) for _, width in CHUNKS),
            *vmem(len(CHUNKS)),
        ],
        out_specs=[row_spec, pl.BlockSpec((8, model_width), lambda i: (0, 0))],
        out_shape=[
            jax.ShapeDtypeStruct((n_rows, model_width), jnp.bfloat16),
            jax.ShapeDtypeStruct((8, model_width), jnp.float32),
        ],
        compiler_params=pltpu.CompilerParams(vmem_limit_bytes=VMEM_LIMIT),
        cost_estimate=pl.CostEstimate(
            flops=4 * n_rows * model_width * model_width,
            bytes_accessed=24 * 1024 * 1024,
            transcendentals=0,
        ),
    )(flat_frames, flat_cot, live, gain.reshape(1, model_width), *ghs, *ws)

    order = sorted(range(len(CHUNKS)), key=lambda c: CHUNKS[c][0])
    tap_part = jnp.dot(
        back_matrix,
        jnp.concatenate([sums[c] for c in order], axis=1),
        precision=lax.Precision.HIGHEST,
    )
    small = jnp.concatenate([tap_part, jnp.sum(gain_part, axis=0, keepdims=True)], axis=0)
    side = model_width // 2
    small = small.reshape(taps + 1, 2, side)
    kept = lax.dynamic_index_in_dim(small, core, 1, keepdims=False)
    sent = lax.dynamic_index_in_dim(small, 1 - core, 1, keepdims=False)
    kept = kept + to_core(sent)
    kept = tree_sum([kept, *(to_quarter(kept, r) for r in range(1, 4))])
    kept = tree_sum([kept, *(shift_red(kept, s) for s in range(1, red_size))])
    kept = other_groups(kept) * root
    other = to_core(kept)
    first = core == 0
    small = jnp.concatenate([jnp.where(first, kept, other), jnp.where(first, other, kept)], axis=1)
    return (
        out.reshape(frames.shape),
        frame_gradient.reshape(frames.shape),
        grad_out,
        small[:taps],
        small[taps],
    )


def solution(mesh):
    placed = (
        P(("dp", "red"), None, None),
        P(("dp", "red"), None, None),
        P("red", None),
        P(),
        P(),
        P(),
    )
    return jax.shard_map(
        local,
        mesh=mesh,
        in_specs=placed,
        out_specs=(
            P(("dp", "red"), None, None),
            P(("dp", "red"), None, None),
            P("red", None),
            P(),
            P(),
        ),
        check_vma=False,
    )
```

time: 678 us -> 284 us (0.42)
  waiting for transfers between devices: 408 us -> 74.2 us
  other arithmetic: 152 us -> 18.4 us
  Pallas kernels: 0 us -> 78.6 us
  starting transfers between devices: 0.16 us -> 78.2 us
  blocking collectives: 39.1 us -> 0 us
  matrix products: 36.1 us -> 1.01 us
  between operations: 15.2 us -> 2.16 us
    all_gather x2 -> x0, waiting for transfers between devices: 186 us -> none  [the longest x1 146 us: local(): weights = lax.all_gather(w_in, 'red', axis=0, tiled=True)]
    reduce_scatter x1 -> x0, waiting for transfers between devices: 156 us -> none  [local(): lax.psum_scatter(lax.dot_general(ordered, flat_grad, (((0,), (0,)), ((),...]
    reduce_sum x7 -> x4, other arithmetic: 97.3 us -> 3.45 us  [the longest x1 2.05 us: local(): center = wide - jnp.mean(wide, axis=-1, keepdims=True)]
    pallas_call x0 -> x7, Pallas kernels: none -> 78.6 us  [the longest x3 51.1 us: local(): pl.pallas_call(functools.partial(chunk_kernel, red_size, half, length, ha...]
    ppermute x0 -> x65, starting transfers between devices: none -> 78.2 us  [the longest x21 44.8 us: shift_red(): lax.ppermute(x, 'red', [(i, (i + s) % red_size) for i in range(red_size)])]
    ppermute x0 -> x65, waiting for transfers between devices: none -> 74.2 us  [the longest x27 51.7 us: to_quarter(): return lax.ppermute(x, 'dp', [(i, i ^ 2 * r) for i in range(dp_size)])]
    psum x1 -> x0, waiting for transfers between devices: 64.5 us -> none  [local(): kernel_total, gain_total = lax.psum((kernel_part, gain_part), ('dp', 'red'))]
    psum x1 -> x0, blocking collectives: 39.1 us -> none  [local(): kernel_total, gain_total = lax.psum((kernel_part, gain_part), ('dp', 'red'))]
  transfers between devices with their start and end apart: 4 -> 65, of which waited for: 4 -> 23; matrix products, arithmetic and copies ran while one was open for 14% -> 11% of each run, Pallas kernels for 0% -> 27%
where the time goes in v1:
time: 284 us; the launch traced here: 279 us
  Pallas kernels  78.6 us (28%)
  starting transfers between devices  78.2 us (28%)
  waiting for transfers between devices  74.2 us (26%)
  local copies, waits for them, and re-layouts  26.7 us (9%)
  other arithmetic  18.4 us (6%)
    ppermute x27, waiting for transfers between devices, to_quarter(): return lax.ppermute(x, 'dp', [(i, i ^ 2 * r) for i in range(dp_size)])  51.7 us
    pallas_call x3, Pallas kernels, local(): pl.pallas_call(functools.partial(chunk_kernel, red_size, half, length, ha...  51.1 us
    ppermute x21, starting transfers between devices, shift_red(): lax.ppermute(x, 'red', [(i, (i + s) % red_size) for i in range(red_size)])  44.8 us
    ppermute x27, starting transfers between devices, to_quarter(): return lax.ppermute(x, 'dp', [(i, i ^ 2 * r) for i in range(dp_size)])  30.6 us
    ppermute x21, waiting for transfers between devices, shift_red(): lax.ppermute(x, 'red', [(i, (i + s) % red_size) for i in range(red_size)])  21.7 us
    pallas_call x1, Pallas kernels, local(): pl.pallas_call(functools.partial(frame_kernel, len(CHUNKS), None), grid=(...  20.5 us
    unnamed x72, local copies, waits for them, and re-layouts  13.1 us
    pallas_call x3, Pallas kernels, local(): pl.pallas_call(functools.partial(place_kernel, has_out), grid=(2,), in_sp...  7.02 us
  transfers between devices with their start and end apart: 65, of which 23 were waited for; matrix products, arithmetic and copies ran while one was open for 11% of the time, Pallas kernels for 27%

profile of v1, /device:TPU:0, one launch (start us, length us, event | category | flops | bytes accessed | tf_op | source)
XLA Modules:
  0.0 279.3 jit_solution(10286809987718647939)
XLA Ops:
  2.8 3.0 %collective-permute-start.16 = (bf16[96,1024]{1,0:T(8,128)(2,1)}, bf16[96,1024]{1,0:T(8,128)(2,1)}, u32[]{:S(2)}, u32[]{:S(2)}) collective-permute-start(bf16[96,1024]{1,0:T(8,128)(2,1)} %pad_maximum_fusion.8), channel_id=1, source_target_pairs={{0,1},{1,2},{2,3},{3,0},{4,5},{5,6},{6,7},{7,4},{8,9},{9,10},{10,1... | collective-permute-start | bytes 589832 | tf_op jit(solution)/shard_map/ppermute | solution.py:240
  5.8 2.6 collective-permute-start.17
  11.5 2.0 convert_reduce_fusion
  14.9 2.8 %fusion.27 = (bf16[384,512]{1,0:T(8,128)(2,1)S(1)}, bf16[384,512]{1,0:T(8,128)(2,1)}, bf16[384,512]{1,0:T(8,128)(2,1)}, bf16[384,512]{1,0:T(8,128)(2,1)S(1)}, bf...) fusion(bf16[384,3072]{1,0:T(8,128)(2,1)} %param.12), kind=kLoop, calls=%fused_computation.90 | loop fusion | bytes 4718592 | tf_op jit(solution)/shard_map/slice | solution.py:265
  20.7 2.9 %multiply_convert_fusion.scaled = bf16[768,1536]{1,0:T(8,128)(2,1)} fusion(f32[1536]{0:T(1024)} %param.14, f32[768]{0:T(1024)S(1)} %rsqrt.15, f32[768]{0:T(1024)} %div.30, bf16[16,48,1536]{2,1,0:T(8,128)(2,1)S(1)} %copy-done.2), kind=kLoop, calls=%fused_computation.4 | loop fusion | flops 5898240 | bytes 4730880 | tf_op jit(solution)/shard_map/convert_element_type | solution.py:273
  23.6 4.3 %copy.21.scaled_t = bf16[1536,768]{1,0:T(8,128)(2,1)} copy(bf16[1536,768]{0,1:T(8,128)(2,1)} %bitcast.119) | data formatting | bytes 4718592 | tf_op jit(solution)/shard_map/transpose | solution.py:274
  28.6 2.9 %collective-permute-start.10 = (bf16[96,1024]{1,0:T(8,128)(2,1)}, bf16[96,1024]{1,0:T(8,128)(2,1)S(1)}, u32[]{:S(2)}, u32[]{:S(2)}) collective-permute-start(bf16[96,1024]{1,0:T(8,128)(2,1)} %pad_maximum_fusion.7), channel_id=1, source_target_pairs={{0,3},{1,0},{2,1},{3,2},{4,7},{5,4},{6,5},{7,6},{8,11},{9,8},{10,9... | collective-permute-start | bytes 589832 | tf_op jit(solution)/shard_map/ppermute | solution.py:240
  32.1 1.7 collective-permute-start.1
  35.0 3.6 %collective-permute-start.2 = (bf16[96,1024]{1,0:T(8,128)(2,1)S(1)}, bf16[96,1024]{1,0:T(8,128)(2,1)S(1)}, u32[]{:S(2)}, u32[]{:S(2)}) collective-permute-start(bf16[96,1024]{1,0:T(8,128)(2,1)S(1)} %pad_maximum_fusion.6), channel_id=1, source_target_pairs={{0,3},{1,0},{2,1},{3,2},{4,7},{5,4},{6,5},{7,6},{8,11},{9,8},{10,9... | collective-permute-start | bytes 589832 | tf_op jit(solution)/shard_map/ppermute | solution.py:240
  38.6 8.0 %collective-permute-done.9 = bf16[96,1024]{1,0:T(8,128)(2,1)} collective-permute-done((bf16[96,1024]{1,0:T(8,128)(2,1)}, bf16[96,1024]{1,0:T(8,128)(2,1)}, u32[]{:S(2)}, u32[]{:S(2)}) %collective-permute-start.9) | collective-permute-done | bytes 196640 | tf_op jit(solution)/shard_map/ppermute | solution.py:240
  48.1 1.5 collective-permute-start.20
  50.9 4.3 %collective-permute-done.1 = bf16[96,1024]{1,0:T(8,128)(2,1)S(1)} collective-permute-done((bf16[96,1024]{1,0:T(8,128)(2,1)S(1)}, bf16[96,1024]{1,0:T(8,128)(2,1)S(1)}, u32[]{:S(2)}, u32[]{:S(2)}) %collective-permute-start.1) | collective-permute-done | bytes 196640 | tf_op jit(solution)/shard_map/ppermute | solution.py:240
  56.7 1.5 collective-permute-start.12
  58.9 5.2 %collective-permute-done.11.rest_1_ = bf16[3,96,512]{2,1,0:T(8,128)(2,1)S(1)} collective-permute-done((bf16[3,96,512]{2,1,0:T(8,128)(2,1)S(1)}, bf16[3,96,512]{2,1,0:T(8,128)(2,1)S(1)}, u32[]{:S(2)}, u32[]{:S(2)}) %collective-permute-start.11) | collective-permute-done | bytes 294944 | tf_op jit(solution)/shard_map/ppermute | solution.py:237
  65.8 1.5 collective-permute-start.4
  68.1 17.1 %shard_map.137 = (bf16[768,1536]{1,0:T(8,128)(2,1)}, bf16[4,4,96,512]{3,2,1,0:T(8,128)(2,1)S(1)}, bf16[4,4,96,512]{3,2,1,0:T(8,128)(2,1)}, bf16[2,768,512]{2,1,0...) custom-call(s32[4]{0:T(128)S(1)} %pad_add_fusion.idx, ...), custom_call_target="tpu_custom_call" | custom-call | flops 7247757312 | bytes 12582912 | tf_op jit(solution)/shard_map/pallas_call | solution.py:302
  87.4 16.8 %shard_map.138 = (bf16[768,1536]{1,0:T(8,128)(2,1)}, bf16[4,4,96,512]{3,2,1,0:T(8,128)(2,1)S(1)}, bf16[4,4,96,512]{3,2,1,0:T(8,128)(2,1)S(1)}, bf16[2,768,512]{2...) custom-call(s32[4]{0:T(128)S(1)} %pad_add_fusion.idx, ...), custom_call_target="tpu_custom_call", output_to_operand_aliasing={{0}: (17, {})} | custom-call | flops 7247757312 | bytes 12582912 | tf_op jit(solution)/shard_map/pallas_call | solution.py:302
  108.4 17.1 %shard_map.139 = (bf16[768,1536]{1,0:T(8,128)(2,1)}, bf16[4,4,96,512]{3,2,1,0:T(8,128)(2,1)S(1)}, bf16[4,4,96,512]{3,2,1,0:T(8,128)(2,1)S(1)}, bf16[2,768,512]{2...) custom-call(s32[4]{0:T(128)S(1)} %pad_add_fusion.idx, ...), custom_call_target="tpu_custom_call", output_to_operand_aliasing={{0}: (17, {})} | custom-call | flops 7247757312 | bytes 12582912 | tf_op jit(solution)/shard_map/pallas_call | solution.py:302
  129.4 20.5 %shard_map.140 = (bf16[768,1536]{1,0:T(8,128)(2,1)}, f32[8,1536]{1,0:T(8,128)S(1)}) custom-call(bf16[768,1536]{1,0:T(8,128)(2,1)S(1)} %bitcast.111, bf16[768,1536]{1,0:T(8,128)(2,1)S(1)} %bitcast.118, f32[768,128]{1,0:T(8,128)S(1)} %broadcast_in_dim.4.rest_8_.live, f32[1,1536]{1,0:T(1,128)S(1)} %broadcast_in_dim.5.gain, bf16[2,768,512]{2,1,0:T(8,128)(2,1)S(1)} %copy-done.21, ...), custom_call_target="tpu_custom_call" | custom-call | flops 7247757312 | bytes 25165824 | tf_op jit(solution)/shard_map/pallas_call | solution.py:358
  158.9 3.0 %collective-permute-done.60 = f32[32,768]{1,0:T(8,128)S(1)} collective-permute-done((f32[32,768]{1,0:T(8,128)S(1)}, f32[32,768]{1,0:T(8,128)S(1)}, u32[]{:S(2)}, u32[]{:S(2)}) %collective-permute-start.60) | collective-permute-done | bytes 98336 | tf_op jit(solution)/shard_map/ppermute | solution.py:237
  161.9 3.5 %collective-permute-start.61 = (f32[32,768]{1,0:T(8,128)S(1)}, f32[32,768]{1,0:T(8,128)S(1)}, u32[]{:S(2)}, u32[]{:S(2)}) collective-permute-start(f32[32,768]{1,0:T(8,128)S(1)} %add_add_fusion), channel_id=1, source_target_pairs={{0,2},{1,3},{2,0},{3,1},{4,6},{5,7},{6,4},{7,5},{8,10},{9,11},{10,... | collective-permute-start | bytes 294920 | tf_op jit(solution)/shard_map/ppermute | solution.py:240
  165.5 1.9 collective-permute-start.62
  168.1 6.2 %collective-permute-start.63 = (f32[32,768]{1,0:T(8,128)S(1)}, f32[32,768]{1,0:T(8,128)S(1)}, u32[]{:S(2)}, u32[]{:S(2)}) collective-permute-start(f32[32,768]{1,0:T(8,128)S(1)} %add_add_fusion), channel_id=1, source_target_pairs={{0,3},{1,0},{2,1},{3,2},{4,7},{5,4},{6,5},{7,6},{8,11},{9,8},{10,9... | collective-permute-start | bytes 294920 | tf_op jit(solution)/shard_map/ppermute | solution.py:240
  176.6 1.9 add_convert_fusion
  180.1 2.0 collective-permute-start.49
  182.1 1.9 add_convert_fusion.1
  185.4 1.9 add_convert_fusion.2
  187.5 3.0 %collective-permute-done.47 = bf16[4,96,512]{2,1,0:T(8,128)(2,1)S(1)} collective-permute-done((bf16[4,96,512]{2,1,0:T(8,128)(2,1)S(1)}, bf16[4,96,512]{2,1,0:T(8,128)(2,1)S(1)}, u32[]{:S(2)}, u32[]{:S(2)}) %collective-permute-start.47) | collective-permute-done | bytes 393248 | tf_op jit(solution)/shard_map/ppermute | solution.py:237
  191.3 1.5 collective-permute-start.38
  192.8 7.7 %collective-permute-done.49 = bf16[4,96,512]{2,1,0:T(8,128)(2,1)S(1)} collective-permute-done((bf16[4,96,512]{2,1,0:T(8,128)(2,1)S(1)}, bf16[4,96,512]{2,1,0:T(8,128)(2,1)S(1)}, u32[]{:S(2)}, u32[]{:S(2)}) %collective-permute-start.49) | collective-permute-done | bytes 393248 | tf_op jit(solution)/shard_map/ppermute | solution.py:237
  201.3 6.0 %collective-permute-done.36 = bf16[4,96,512]{2,1,0:T(8,128)(2,1)S(1)} collective-permute-done((bf16[4,96,512]{2,1,0:T(8,128)(2,1)S(1)}, bf16[4,96,512]{2,1,0:T(8,128)(2,1)S(1)}, u32[]{:S(2)}, u32[]{:S(2)}) %collective-permute-start.36) | collective-permute-done | bytes 393248 | tf_op jit(solution)/shard_map/ppermute | solution.py:237
  208.1 1.5 collective-permute-start.27
  209.7 7.7 %collective-permute-done.38 = bf16[4,96,512]{2,1,0:T(8,128)(2,1)S(1)} collective-permute-done((bf16[4,96,512]{2,1,0:T(8,128)(2,1)S(1)}, bf16[4,96,512]{2,1,0:T(8,128)(2,1)S(1)}, u32[]{:S(2)}, u32[]{:S(2)}) %collective-permute-start.38) | collective-permute-done | bytes 393248 | tf_op jit(solution)/shard_map/ppermute | solution.py:237
  218.6 5.2 %collective-permute-done.25 = bf16[4,96,512]{2,1,0:T(8,128)(2,1)S(1)} collective-permute-done((bf16[4,96,512]{2,1,0:T(8,128)(2,1)S(1)}, bf16[4,96,512]{2,1,0:T(8,128)(2,1)S(1)}, u32[]{:S(2)}, u32[]{:S(2)}) %collective-permute-start.25) | collective-permute-done | bytes 393248 | tf_op jit(solution)/shard_map/ppermute | solution.py:237
  225.3 3.9 %collective-permute-start.52 = (bf16[96,512]{1,0:T(8,128)(2,1)S(1)}, bf16[96,512]{1,0:T(8,128)(2,1)S(1)}, u32[]{:S(2)}, u32[]{:S(2)}) collective-permute-start(bf16[96,512]{1,0:T(8,128)(2,1)S(1)} %get-tuple-element.73), channel_id=1, source_target_pairs={{0,3},{1,0},{2,1},{3,2},{4,7},{5,4},{6,5},{7,6},{8,11},{9,8},{10,9... | collective-permute-start | bytes 294920 | tf_op jit(solution)/shard_map/ppermute | solution.py:240
  229.2 4.4 %collective-permute-done.27 = bf16[4,96,512]{2,1,0:T(8,128)(2,1)S(1)} collective-permute-done((bf16[4,96,512]{2,1,0:T(8,128)(2,1)S(1)}, bf16[4,96,512]{2,1,0:T(8,128)(2,1)S(1)}, u32[]{:S(2)}, u32[]{:S(2)}) %collective-permute-start.27) | collective-permute-done | bytes 393248 | tf_op jit(solution)/shard_map/ppermute | solution.py:237
  234.7 3.9 %collective-permute-start.40 = (bf16[96,512]{1,0:T(8,128)(2,1)S(1)}, bf16[96,512]{1,0:T(8,128)(2,1)S(1)}, u32[]{:S(2)}, u32[]{:S(2)}) collective-permute-start(bf16[96,512]{1,0:T(8,128)(2,1)S(1)} %get-tuple-element.77), channel_id=1, source_target_pairs={{0,1},{1,2},{2,3},{3,0},{4,5},{5,6},{6,7},{7,4},{8,9},{9,10},{10,1... | collective-permute-start | bytes 294920 | tf_op jit(solution)/shard_map/ppermute | solution.py:240
  238.6 1.5 collective-permute-start.28
  240.2 5.2 %collective-permute-done.39 = bf16[96,512]{1,0:T(8,128)(2,1)S(1)} collective-permute-done((bf16[96,512]{1,0:T(8,128)(2,1)S(1)}, bf16[96,512]{1,0:T(8,128)(2,1)S(1)}, u32[]{:S(2)}, u32[]{:S(2)}) %collective-permute-start.39) | collective-permute-done | bytes 98336 | tf_op jit(solution)/shard_map/ppermute | solution.py:240
  245.4 3.8 %collective-permute-start.30 = (bf16[96,512]{1,0:T(8,128)(2,1)S(1)}, bf16[96,512]{1,0:T(8,128)(2,1)S(1)}, u32[]{:S(2)}, u32[]{:S(2)}) collective-permute-start(bf16[96,512]{1,0:T(8,128)(2,1)S(1)} %get-tuple-element.79), channel_id=1, source_target_pairs={{0,3},{1,0},{2,1},{3,2},{4,7},{5,4},{6,5},{7,6},{8,11},{9,8},{10,9... | collective-permute-start | bytes 294920 | tf_op jit(solution)/shard_map/ppermute | solution.py:240
  250.0 2.6 collective-permute-done.28
  253.2 1.6 collective-permute-start.55
  256.9 2.2 collective-permute-done.54
  260.1 1.6 collective-permute-start.31
  266.4 1.8 collective-permute-done.33
  270.5 2.3 shard_map.141.rest_0_
  273.6 2.3 shard_map.142.rest_0_
  276.7 2.4 shard_map.143
  (219 shorter events, 63.1 us)
Async XLA Ops:
  2.8 25.8 %collective-permute-start.16 = (bf16[96,1024]{1,0:T(8,128)(2,1)}, bf16[96,1024]{1,0:T(8,128)(2,1)}, u32[]{:S(2)}, u32[]{:S(2)}) collective-permute-start(bf16[96,1024]{1,0:T(8,128)(2,1)} %pad_maximum_fusion.8), channel_id=1, source_target_pairs={{0,1},{1,2},{2,3},{3,0},{4,5},{5,6},{6,7},{7,4},{8,9},{9,10},{10,1... | collective-permute-start | bytes 589832 | tf_op jit(solution)/shard_map/ppermute | solution.py:240
  5.8 25.6 %collective-permute-start.17 = (bf16[96,1024]{1,0:T(8,128)(2,1)}, bf16[96,1024]{1,0:T(8,128)(2,1)}, u32[]{:S(2)}, u32[]{:S(2)}) collective-permute-start(bf16[96,1024]{1,0:T(8,128)(2,1)} %pad_maximum_fusion.8), channel_id=1, source_target_pairs={{0,2},{1,3},{2,0},{3,1},{4,6},{5,7},{6,4},{7,5},{8,10},{9,11},{10,... | collective-permute-start | bytes 589832 | tf_op jit(solution)/shard_map/ppermute | solution.py:240
  8.4 23.7 %collective-permute-start.18 = (bf16[96,1024]{1,0:T(8,128)(2,1)}, bf16[96,1024]{1,0:T(8,128)(2,1)}, u32[]{:S(2)}, u32[]{:S(2)}) collective-permute-start(bf16[96,1024]{1,0:T(8,128)(2,1)} %pad_maximum_fusion.8), channel_id=1, source_target_pairs={{0,3},{1,0},{2,1},{3,2},{4,7},{5,4},{6,5},{7,6},{8,11},{9,8},{10,9... | collective-permute-start | bytes 589832 | tf_op jit(solution)/shard_map/ppermute | solution.py:240
  10.4 24.6 %collective-permute-start.8 = (bf16[96,1024]{1,0:T(8,128)(2,1)}, bf16[96,1024]{1,0:T(8,128)(2,1)}, u32[]{:S(2)}, u32[]{:S(2)}) collective-permute-start(bf16[96,1024]{1,0:T(8,128)(2,1)} %pad_maximum_fusion.7), channel_id=1, source_target_pairs={{0,1},{1,2},{2,3},{3,0},{4,5},{5,6},{6,7},{7,4},{8,9},{9,10},{10,1... | collective-permute-start | bytes 589832 | tf_op jit(solution)/shard_map/ppermute | solution.py:240
  11.1 35.5 %collective-permute-start.9 = (bf16[96,1024]{1,0:T(8,128)(2,1)}, bf16[96,1024]{1,0:T(8,128)(2,1)}, u32[]{:S(2)}, u32[]{:S(2)}) collective-permute-start(bf16[96,1024]{1,0:T(8,128)(2,1)} %pad_maximum_fusion.7), channel_id=1, source_target_pairs={{0,2},{1,3},{2,0},{3,1},{4,6},{5,7},{6,4},{7,5},{8,10},{9,11},{10,... | collective-permute-start | bytes 589832 | tf_op jit(solution)/shard_map/ppermute | solution.py:240
  28.6 19.5 %collective-permute-start.10 = (bf16[96,1024]{1,0:T(8,128)(2,1)}, bf16[96,1024]{1,0:T(8,128)(2,1)S(1)}, u32[]{:S(2)}, u32[]{:S(2)}) collective-permute-start(bf16[96,1024]{1,0:T(8,128)(2,1)} %pad_maximum_fusion.7), channel_id=1, source_target_pairs={{0,3},{1,0},{2,1},{3,2},{4,7},{5,4},{6,5},{7,6},{8,11},{9,8},{10,9... | collective-permute-start | bytes 589832 | tf_op jit(solution)/shard_map/ppermute | solution.py:240
  31.4 19.3 %collective-permute-start = (bf16[96,1024]{1,0:T(8,128)(2,1)S(1)}, bf16[96,1024]{1,0:T(8,128)(2,1)S(1)}, u32[]{:S(2)}, u32[]{:S(2)}) collective-permute-start(bf16[96,1024]{1,0:T(8,128)(2,1)S(1)} %pad_maximum_fusion.6), channel_id=1, source_target_pairs={{0,1},{1,2},{2,3},{3,0},{4,5},{5,6},{6,7},{7,4},{8,9},{9,10},{10,1... | collective-permute-start | bytes 589832 | tf_op jit(solution)/shard_map/ppermute | solution.py:240
  32.1 23.2 %collective-permute-start.1 = (bf16[96,1024]{1,0:T(8,128)(2,1)S(1)}, bf16[96,1024]{1,0:T(8,128)(2,1)S(1)}, u32[]{:S(2)}, u32[]{:S(2)}) collective-permute-start(bf16[96,1024]{1,0:T(8,128)(2,1)S(1)} %pad_maximum_fusion.6), channel_id=1, source_target_pairs={{0,2},{1,3},{2,0},{3,1},{4,6},{5,7},{6,4},{7,5},{8,10},{9,11},{10,... | collective-permute-start | bytes 589832 | tf_op jit(solution)/shard_map/ppermute | solution.py:240
  35.0 21.7 %collective-permute-start.2 = (bf16[96,1024]{1,0:T(8,128)(2,1)S(1)}, bf16[96,1024]{1,0:T(8,128)(2,1)S(1)}, u32[]{:S(2)}, u32[]{:S(2)}) collective-permute-start(bf16[96,1024]{1,0:T(8,128)(2,1)S(1)} %pad_maximum_fusion.6), channel_id=1, source_target_pairs={{0,3},{1,0},{2,1},{3,2},{4,7},{5,4},{6,5},{7,6},{8,11},{9,8},{10,9... | collective-permute-start | bytes 589832 | tf_op jit(solution)/shard_map/ppermute | solution.py:240
  46.6 11.6 %collective-permute-start.19 = (bf16[3,96,512]{2,1,0:T(8,128)(2,1)S(1)}, bf16[3,96,512]{2,1,0:T(8,128)(2,1)S(1)}, u32[]{:S(2)}, u32[]{:S(2)}) collective-permute-start(bf16[3,96,512]{2,1,0:T(8,128)(2,1)S(1)} %get-tuple-element.67), channel_id=1, source_target_pairs={{0,8},{4,12},{8,0},{12,4},{16,24},{20,28},{24,16},{28,20},{1,9},{5... | collective-permute-start | bytes 884744 | tf_op jit(solution)/shard_map/ppermute | solution.py:237
  48.1 10.1 %collective-permute-start.20 = (bf16[3,96,512]{2,1,0:T(8,128)(2,1)S(1)}, bf16[3,96,512]{2,1,0:T(8,128)(2,1)S(1)}, u32[]{:S(2)}, u32[]{:S(2)}) collective-permute-start(bf16[3,96,512]{2,1,0:T(8,128)(2,1)S(1)} %get-tuple-element.66), channel_id=1, source_target_pairs={{0,16},{4,20},{8,24},{12,28},{16,0},{20,4},{24,8},{28,12},{1,17},{... | collective-permute-start | bytes 884744 | tf_op jit(solution)/shard_map/ppermute | solution.py:237
  50.8 15.0 %collective-permute-start.21 = (bf16[3,96,1024]{2,1,0:T(8,128)(2,1)S(1)}, bf16[3,96,1024]{2,1,0:T(8,128)(2,1)S(1)}, u32[]{:S(2)}, u32[]{:S(2)}) collective-permute-start(bf16[3,96,1024]{2,1,0:T(8,128)(2,1)S(1)} %pad_maximum_fusion.2.rest_0_), channel_id=1, source_target_pairs={{0,4},{4,0},{8,12},{12,8},{16,20},{20,16},{24,28},{28,24},{1,5},{5... | collective-permute-start | bytes 1769480 | tf_op jit(solution)/shard_map/ppermute | solution.py:234
  55.2 8.8 %collective-permute-start.11 = (bf16[3,96,512]{2,1,0:T(8,128)(2,1)S(1)}, bf16[3,96,512]{2,1,0:T(8,128)(2,1)S(1)}, u32[]{:S(2)}, u32[]{:S(2)}) collective-permute-start(bf16[3,96,512]{2,1,0:T(8,128)(2,1)S(1)} %get-tuple-element.69), channel_id=1, source_target_pairs={{0,8},{4,12},{8,0},{12,4},{16,24},{20,28},{24,16},{28,20},{1,9},{5... | collective-permute-start | bytes 884744 | tf_op jit(solution)/shard_map/ppermute | solution.py:237
  56.7 8.6 %collective-permute-start.12 = (bf16[3,96,512]{2,1,0:T(8,128)(2,1)S(1)}, bf16[3,96,512]{2,1,0:T(8,128)(2,1)S(1)}, u32[]{:S(2)}, u32[]{:S(2)}) collective-permute-start(bf16[3,96,512]{2,1,0:T(8,128)(2,1)S(1)} %get-tuple-element.68), channel_id=1, source_target_pairs={{0,16},{4,20},{8,24},{12,28},{16,0},{20,4},{24,8},{28,12},{1,17},{... | collective-permute-start | bytes 884744 | tf_op jit(solution)/shard_map/ppermute | solution.py:237
  58.2 9.1 %collective-permute-start.22 = (bf16[3,96,512]{2,1,0:T(8,128)(2,1)S(1)}, bf16[3,96,512]{2,1,0:T(8,128)(2,1)S(1)}, u32[]{:S(2)}, u32[]{:S(2)}) collective-permute-start(bf16[3,96,512]{2,1,0:T(8,128)(2,1)S(1)} %collective-permute-done.19.rest_1_), channel_id=1, source_target_pairs={{0,4},{4,0},{8,12},{12,8},{16,20},{20,16},{24,28},{28,24},{1,5},{5... | collective-permute-start | bytes 884744 | tf_op jit(solution)/shard_map/ppermute | solution.py:234
  58.2 9.1 %collective-permute-start.23 = (bf16[3,96,512]{2,1,0:T(8,128)(2,1)S(1)}, bf16[3,96,512]{2,1,0:T(8,128)(2,1)S(1)}, u32[]{:S(2)}, u32[]{:S(2)}) collective-permute-start(bf16[3,96,512]{2,1,0:T(8,128)(2,1)S(1)} %collective-permute-done.20.rest_2_), channel_id=1, source_target_pairs={{0,4},{4,0},{8,12},{12,8},{16,20},{20,16},{24,28},{28,24},{1,5},{5... | collective-permute-start | bytes 884744 | tf_op jit(solution)/shard_map/ppermute | solution.py:234
  64.1 22.8 %collective-permute-start.13 = (bf16[3,96,1024]{2,1,0:T(8,128)(2,1)S(1)}, bf16[3,96,1024]{2,1,0:T(8,128)(2,1)S(1)}, u32[]{:S(2)}, u32[]{:S(2)}) collective-permute-start(bf16[3,96,1024]{2,1,0:T(8,128)(2,1)S(1)} %pad_maximum_fusion.1.rest_0_), channel_id=1, source_target_pairs={{0,4},{4,0},{8,12},{12,8},{16,20},{20,16},{24,28},{28,24},{1,5},{5... | collective-permute-start | bytes 1769480 | tf_op jit(solution)/shard_map/ppermute | solution.py:234
  65.3 21.1 %collective-permute-start.3 = (bf16[3,96,512]{2,1,0:T(8,128)(2,1)S(1)}, bf16[3,96,512]{2,1,0:T(8,128)(2,1)S(1)}, u32[]{:S(2)}, u32[]{:S(2)}) collective-permute-start(bf16[3,96,512]{2,1,0:T(8,128)(2,1)S(1)} %get-tuple-element.71), channel_id=1, source_target_pairs={{0,8},{4,12},{8,0},{12,4},{16,24},{20,28},{24,16},{28,20},{1,9},{5... | collective-permute-start | bytes 884744 | tf_op jit(solution)/shard_map/ppermute | solution.py:237
  65.8 20.6 %collective-permute-start.4 = (bf16[3,96,512]{2,1,0:T(8,128)(2,1)S(1)}, bf16[3,96,512]{2,1,0:T(8,128)(2,1)S(1)}, u32[]{:S(2)}, u32[]{:S(2)}) collective-permute-start(bf16[3,96,512]{2,1,0:T(8,128)(2,1)S(1)} %get-tuple-element.70), channel_id=1, source_target_pairs={{0,16},{4,20},{8,24},{12,28},{16,0},{20,4},{24,8},{28,12},{1,17},{... | collective-permute-start | bytes 884744 | tf_op jit(solution)/shard_map/ppermute | solution.py:237
  67.3 19.6 %collective-permute-start.14 = (bf16[3,96,512]{2,1,0:T(8,128)(2,1)S(1)}, bf16[3,96,512]{2,1,0:T(8,128)(2,1)S(1)}, u32[]{:S(2)}, u32[]{:S(2)}) collective-permute-start(bf16[3,96,512]{2,1,0:T(8,128)(2,1)S(1)} %collective-permute-done.11.rest_1_), channel_id=1, source_target_pairs={{0,4},{4,0},{8,12},{12,8},{16,20},{20,16},{24,28},{28,24},{1,5},{5... | collective-permute-start | bytes 884744 | tf_op jit(solution)/shard_map/ppermute | solution.py:234
  67.3 20.0 %collective-permute-start.15 = (bf16[3,96,512]{2,1,0:T(8,128)(2,1)S(1)}, bf16[3,96,512]{2,1,0:T(8,128)(2,1)S(1)}, u32[]{:S(2)}, u32[]{:S(2)}) collective-permute-start(bf16[3,96,512]{2,1,0:T(8,128)(2,1)S(1)} %collective-permute-done.12.rest_2_), channel_id=1, source_target_pairs={{0,4},{4,0},{8,12},{12,8},{16,20},{20,16},{24,28},{28,24},{1,5},{5... | collective-permute-start | bytes 884744 | tf_op jit(solution)/shard_map/ppermute | solution.py:234
  86.3 19.0 %collective-permute-start.5 = (bf16[3,96,1024]{2,1,0:T(8,128)(2,1)S(1)}, bf16[3,96,1024]{2,1,0:T(8,128)(2,1)S(1)}, u32[]{:S(2)}, u32[]{:S(2)}) collective-permute-start(bf16[3,96,1024]{2,1,0:T(8,128)(2,1)S(1)} %pad_maximum_fusion.rest_0_), channel_id=1, source_target_pairs={{0,4},{4,0},{8,12},{12,8},{16,20},{20,16},{24,28},{28,24},{1,5},{5... | collective-permute-start | bytes 1769480 | tf_op jit(solution)/shard_map/ppermute | solution.py:234
  86.4 19.0 %collective-permute-start.6 = (bf16[3,96,512]{2,1,0:T(8,128)(2,1)S(1)}, bf16[3,96,512]{2,1,0:T(8,128)(2,1)S(1)}, u32[]{:S(2)}, u32[]{:S(2)}) collective-permute-start(bf16[3,96,512]{2,1,0:T(8,128)(2,1)S(1)} %collective-permute-done.3.rest_1_), channel_id=1, source_target_pairs={{0,4},{4,0},{8,12},{12,8},{16,20},{20,16},{24,28},{28,24},{1,5},{5... | collective-permute-start | bytes 884744 | tf_op jit(solution)/shard_map/ppermute | solution.py:234
  86.9 18.5 %collective-permute-start.7 = (bf16[3,96,512]{2,1,0:T(8,128)(2,1)S(1)}, bf16[3,96,512]{2,1,0:T(8,128)(2,1)S(1)}, u32[]{:S(2)}, u32[]{:S(2)}) collective-permute-start(bf16[3,96,512]{2,1,0:T(8,128)(2,1)S(1)} %collective-permute-done.4.rest_2_), channel_id=1, source_target_pairs={{0,4},{4,0},{8,12},{12,8},{16,20},{20,16},{24,28},{28,24},{1,5},{5... | collective-permute-start | bytes 884744 | tf_op jit(solution)/shard_map/ppermute | solution.py:234
  86.9 89.6 %collective-permute-start.46 = (bf16[4,4,96,512]{3,2,1,0:T(8,128)(2,1)}, bf16[4,4,96,512]{3,2,1,0:T(8,128)(2,1)}, u32[]{:S(2)}, u32[]{:S(2)}) collective-permute-start(bf16[4,4,96,512]{3,2,1,0:T(8,128)(2,1)} %get-tuple-element.40), channel_id=1, source_target_pairs={{0,4},{4,0},{8,12},{12,8},{16,20},{20,16},{24,28},{28,24},{1,5},{5... | collective-permute-start | bytes 4718600 | tf_op jit(solution)/shard_map/ppermute | solution.py:234
  152.4 27.7 %collective-permute-start.35 = (bf16[4,4,96,512]{3,2,1,0:T(8,128)(2,1)}, bf16[4,4,96,512]{3,2,1,0:T(8,128)(2,1)}, u32[]{:S(2)}, u32[]{:S(2)}) collective-permute-start(bf16[4,4,96,512]{3,2,1,0:T(8,128)(2,1)} %copy-done.12), channel_id=1, source_target_pairs={{0,4},{4,0},{8,12},{12,8},{16,20},{20,16},{24,28},{28,24},{1,5},{5... | collective-permute-start | bytes 4718600 | tf_op jit(solution)/shard_map/ppermute | solution.py:234
  165.5 18.7 %collective-permute-start.24 = (bf16[4,4,96,512]{3,2,1,0:T(8,128)(2,1)}, bf16[4,4,96,512]{3,2,1,0:T(8,128)(2,1)}, u32[]{:S(2)}, u32[]{:S(2)}) collective-permute-start(bf16[4,4,96,512]{3,2,1,0:T(8,128)(2,1)} %copy-done.13), channel_id=1, source_target_pairs={{0,4},{4,0},{8,12},{12,8},{16,20},{20,16},{24,28},{28,24},{1,5},{5... | collective-permute-start | bytes 4718600 | tf_op jit(solution)/shard_map/ppermute | solution.py:234
  165.5 10.1 %collective-permute-start.62 = (f32[32,768]{1,0:T(8,128)S(1)}, f32[32,768]{1,0:T(8,128)S(1)}, u32[]{:S(2)}, u32[]{:S(2)}) collective-permute-start(f32[32,768]{1,0:T(8,128)S(1)} %add_add_fusion), channel_id=1, source_target_pairs={{0,1},{1,2},{2,3},{3,0},{4,5},{5,6},{6,7},{7,4},{8,9},{9,10},{10,1... | collective-permute-start | bytes 294920 | tf_op jit(solution)/shard_map/ppermute | solution.py:240
  168.1 8.4 %collective-permute-start.63 = (f32[32,768]{1,0:T(8,128)S(1)}, f32[32,768]{1,0:T(8,128)S(1)}, u32[]{:S(2)}, u32[]{:S(2)}) collective-permute-start(f32[32,768]{1,0:T(8,128)S(1)} %add_add_fusion), channel_id=1, source_target_pairs={{0,3},{1,0},{2,1},{3,2},{4,7},{5,4},{6,5},{7,6},{8,11},{9,8},{10,9... | collective-permute-start | bytes 294920 | tf_op jit(solution)/shard_map/ppermute | solution.py:240
  176.5 91.9 %collective-permute-start.64 = (f32[32,768]{1,0:T(8,128)S(1)}, f32[32,768]{1,0:T(8,128)S(1)}, u32[]{:S(2)}, u32[]{:S(2)}) collective-permute-start(f32[32,768]{1,0:T(8,128)S(1)} %add_multiply_fusion), channel_id=1, source_target_pairs={{0,4},{4,0},{8,12},{12,8},{16,20},{20,16},{24,28},{28,24},{1,5},{5... | collective-permute-start | bytes 294920 | tf_op jit(solution)/shard_map/ppermute | solution.py:234
  178.5 12.0 %collective-permute-start.47 = (bf16[4,96,512]{2,1,0:T(8,128)(2,1)S(1)}, bf16[4,96,512]{2,1,0:T(8,128)(2,1)S(1)}, u32[]{:S(2)}, u32[]{:S(2)}) collective-permute-start(bf16[4,96,512]{2,1,0:T(8,128)(2,1)S(1)} %get-tuple-element.57), channel_id=1, source_target_pairs={{0,16},{4,20},{8,24},{12,28},{16,0},{20,4},{24,8},{28,12},{1,17},{... | collective-permute-start | bytes 1179656 | tf_op jit(solution)/shard_map/ppermute | solution.py:237
  179.2 12.0 %collective-permute-start.48 = (bf16[4,96,512]{2,1,0:T(8,128)(2,1)S(1)}, bf16[4,96,512]{2,1,0:T(8,128)(2,1)S(1)}, u32[]{:S(2)}, u32[]{:S(2)}) collective-permute-start(bf16[4,96,512]{2,1,0:T(8,128)(2,1)S(1)} %get-tuple-element.59), channel_id=1, source_target_pairs={{0,8},{4,12},{8,0},{12,4},{16,24},{20,28},{24,16},{28,20},{1,9},{5... | collective-permute-start | bytes 1179656 | tf_op jit(solution)/shard_map/ppermute | solution.py:237
  180.1 20.4 %collective-permute-start.49 = (bf16[4,96,512]{2,1,0:T(8,128)(2,1)S(1)}, bf16[4,96,512]{2,1,0:T(8,128)(2,1)S(1)}, u32[]{:S(2)}, u32[]{:S(2)}) collective-permute-start(bf16[4,96,512]{2,1,0:T(8,128)(2,1)S(1)} %get-tuple-element.58), channel_id=1, source_target_pairs={{0,24},{4,28},{8,16},{12,20},{16,8},{20,12},{24,0},{28,4},{1,25},{... | collective-permute-start | bytes 1179656 | tf_op jit(solution)/shard_map/ppermute | solution.py:237
  184.1 23.3 %collective-permute-start.36 = (bf16[4,96,512]{2,1,0:T(8,128)(2,1)S(1)}, bf16[4,96,512]{2,1,0:T(8,128)(2,1)S(1)}, u32[]{:S(2)}, u32[]{:S(2)}) collective-permute-start(bf16[4,96,512]{2,1,0:T(8,128)(2,1)S(1)} %get-tuple-element.60), channel_id=1, source_target_pairs={{0,16},{4,20},{8,24},{12,28},{16,0},{20,4},{24,8},{28,12},{1,17},{... | collective-permute-start | bytes 1179656 | tf_op jit(solution)/shard_map/ppermute | solution.py:237
  190.5 17.6 %collective-permute-start.37 = (bf16[4,96,512]{2,1,0:T(8,128)(2,1)S(1)}, bf16[4,96,512]{2,1,0:T(8,128)(2,1)S(1)}, u32[]{:S(2)}, u32[]{:S(2)}) collective-permute-start(bf16[4,96,512]{2,1,0:T(8,128)(2,1)S(1)} %get-tuple-element.62), channel_id=1, source_target_pairs={{0,8},{4,12},{8,0},{12,4},{16,24},{20,28},{24,16},{28,20},{1,9},{5... | collective-permute-start | bytes 1179656 | tf_op jit(solution)/shard_map/ppermute | solution.py:237
  191.3 26.1 %collective-permute-start.38 = (bf16[4,96,512]{2,1,0:T(8,128)(2,1)S(1)}, bf16[4,96,512]{2,1,0:T(8,128)(2,1)S(1)}, u32[]{:S(2)}, u32[]{:S(2)}) collective-permute-start(bf16[4,96,512]{2,1,0:T(8,128)(2,1)S(1)} %get-tuple-element.61), channel_id=1, source_target_pairs={{0,24},{4,28},{8,16},{12,20},{16,8},{20,12},{24,0},{28,4},{1,25},{... | collective-permute-start | bytes 1179656 | tf_op jit(solution)/shard_map/ppermute | solution.py:237
  200.5 23.3 %collective-permute-start.25 = (bf16[4,96,512]{2,1,0:T(8,128)(2,1)S(1)}, bf16[4,96,512]{2,1,0:T(8,128)(2,1)S(1)}, u32[]{:S(2)}, u32[]{:S(2)}) collective-permute-start(bf16[4,96,512]{2,1,0:T(8,128)(2,1)S(1)} %get-tuple-element.63), channel_id=1, source_target_pairs={{0,16},{4,20},{8,24},{12,28},{16,0},{20,4},{24,8},{28,12},{1,17},{... | collective-permute-start | bytes 1179656 | tf_op jit(solution)/shard_map/ppermute | solution.py:237
  207.4 17.9 %collective-permute-start.26 = (bf16[4,96,512]{2,1,0:T(8,128)(2,1)S(1)}, bf16[4,96,512]{2,1,0:T(8,128)(2,1)S(1)}, u32[]{:S(2)}, u32[]{:S(2)}) collective-permute-start(bf16[4,96,512]{2,1,0:T(8,128)(2,1)S(1)} %get-tuple-element.65), channel_id=1, source_target_pairs={{0,8},{4,12},{8,0},{12,4},{16,24},{20,28},{24,16},{28,20},{1,9},{5... | collective-permute-start | bytes 1179656 | tf_op jit(solution)/shard_map/ppermute | solution.py:237
  208.1 25.4 %collective-permute-start.27 = (bf16[4,96,512]{2,1,0:T(8,128)(2,1)S(1)}, bf16[4,96,512]{2,1,0:T(8,128)(2,1)S(1)}, u32[]{:S(2)}, u32[]{:S(2)}) collective-permute-start(bf16[4,96,512]{2,1,0:T(8,128)(2,1)S(1)} %get-tuple-element.64), channel_id=1, source_target_pairs={{0,24},{4,28},{8,16},{12,20},{16,8},{20,12},{24,0},{28,4},{1,25},{... | collective-permute-start | bytes 1179656 | tf_op jit(solution)/shard_map/ppermute | solution.py:237
  217.4 17.3 %collective-permute-start.50 = (bf16[96,512]{1,0:T(8,128)(2,1)S(1)}, bf16[96,512]{1,0:T(8,128)(2,1)S(1)}, u32[]{:S(2)}, u32[]{:S(2)}) collective-permute-start(bf16[96,512]{1,0:T(8,128)(2,1)S(1)} %get-tuple-element.72), channel_id=1, source_target_pairs={{0,2},{1,3},{2,0},{3,1},{4,6},{5,7},{6,4},{7,5},{8,10},{9,11},{10,... | collective-permute-start | bytes 294920 | tf_op jit(solution)/shard_map/ppermute | solution.py:240
  223.8 14.8 %collective-permute-start.51 = (bf16[96,512]{1,0:T(8,128)(2,1)S(1)}, bf16[96,512]{1,0:T(8,128)(2,1)S(1)}, u32[]{:S(2)}, u32[]{:S(2)}) collective-permute-start(bf16[96,512]{1,0:T(8,128)(2,1)S(1)} %get-tuple-element.74), channel_id=1, source_target_pairs={{0,1},{1,2},{2,3},{3,0},{4,5},{5,6},{6,7},{7,4},{8,9},{9,10},{10,1... | collective-permute-start | bytes 294920 | tf_op jit(solution)/shard_map/ppermute | solution.py:240
  225.3 13.3 %collective-permute-start.52 = (bf16[96,512]{1,0:T(8,128)(2,1)S(1)}, bf16[96,512]{1,0:T(8,128)(2,1)S(1)}, u32[]{:S(2)}, u32[]{:S(2)}) collective-permute-start(bf16[96,512]{1,0:T(8,128)(2,1)S(1)} %get-tuple-element.73), channel_id=1, source_target_pairs={{0,3},{1,0},{2,1},{3,2},{4,7},{5,4},{6,5},{7,6},{8,11},{9,8},{10,9... | collective-permute-start | bytes 294920 | tf_op jit(solution)/shard_map/ppermute | solution.py:240
  233.5 11.9 %collective-permute-start.39 = (bf16[96,512]{1,0:T(8,128)(2,1)S(1)}, bf16[96,512]{1,0:T(8,128)(2,1)S(1)}, u32[]{:S(2)}, u32[]{:S(2)}) collective-permute-start(bf16[96,512]{1,0:T(8,128)(2,1)S(1)} %get-tuple-element.75), channel_id=1, source_target_pairs={{0,2},{1,3},{2,0},{3,1},{4,6},{5,7},{6,4},{7,5},{8,10},{9,11},{10,... | collective-permute-start | bytes 294920 | tf_op jit(solution)/shard_map/ppermute | solution.py:240
  234.7 10.7 %collective-permute-start.40 = (bf16[96,512]{1,0:T(8,128)(2,1)S(1)}, bf16[96,512]{1,0:T(8,128)(2,1)S(1)}, u32[]{:S(2)}, u32[]{:S(2)}) collective-permute-start(bf16[96,512]{1,0:T(8,128)(2,1)S(1)} %get-tuple-element.77), channel_id=1, source_target_pairs={{0,1},{1,2},{2,3},{3,0},{4,5},{5,6},{6,7},{7,4},{8,9},{9,10},{10,1... | collective-permute-start | bytes 294920 | tf_op jit(solution)/shard_map/ppermute | solution.py:240
  238.6 10.6 %collective-permute-start.41 = (bf16[96,512]{1,0:T(8,128)(2,1)S(1)}, bf16[96,512]{1,0:T(8,128)(2,1)S(1)}, u32[]{:S(2)}, u32[]{:S(2)}) collective-permute-start(bf16[96,512]{1,0:T(8,128)(2,1)S(1)} %get-tuple-element.76), channel_id=1, source_target_pairs={{0,3},{1,0},{2,1},{3,2},{4,7},{5,4},{6,5},{7,6},{8,11},{9,8},{10,9... | collective-permute-start | bytes 294920 | tf_op jit(solution)/shard_map/ppermute | solution.py:240
  238.6 14.0 %collective-permute-start.28 = (bf16[96,512]{1,0:T(8,128)(2,1)S(1)}, bf16[96,512]{1,0:T(8,128)(2,1)S(1)}, u32[]{:S(2)}, u32[]{:S(2)}) collective-permute-start(bf16[96,512]{1,0:T(8,128)(2,1)S(1)} %get-tuple-element.78), channel_id=1, source_target_pairs={{0,2},{1,3},{2,0},{3,1},{4,6},{5,7},{6,4},{7,5},{8,10},{9,11},{10,... | collective-permute-start | bytes 294920 | tf_op jit(solution)/shard_map/ppermute | solution.py:240
  245.4 7.9 %collective-permute-start.29 = (bf16[96,512]{1,0:T(8,128)(2,1)S(1)}, bf16[96,512]{1,0:T(8,128)(2,1)S(1)}, u32[]{:S(2)}, u32[]{:S(2)}) collective-permute-start(bf16[96,512]{1,0:T(8,128)(2,1)S(1)} %get-tuple-element.80), channel_id=1, source_target_pairs={{0,1},{1,2},{2,3},{3,0},{4,5},{5,6},{6,7},{7,4},{8,9},{9,10},{10,1... | collective-permute-start | bytes 294920 | tf_op jit(solution)/shard_map/ppermute | solution.py:240
  245.4 9.4 %collective-permute-start.30 = (bf16[96,512]{1,0:T(8,128)(2,1)S(1)}, bf16[96,512]{1,0:T(8,128)(2,1)S(1)}, u32[]{:S(2)}, u32[]{:S(2)}) collective-permute-start(bf16[96,512]{1,0:T(8,128)(2,1)S(1)} %get-tuple-element.79), channel_id=1, source_target_pairs={{0,3},{1,0},{2,1},{3,2},{4,7},{5,4},{6,5},{7,6},{8,11},{9,8},{10,9... | collective-permute-start | bytes 294920 | tf_op jit(solution)/shard_map/ppermute | solution.py:240
  (52 other events, 530.6 us)

commit v2 on v1

v2 whole, which is shorter than its diff:
```python
import functools

import jax
import jax.numpy as jnp
import numpy as np
from jax import lax
from jax.experimental import pallas as pl
from jax.experimental.pallas import tpu as pltpu
from jax.sharding import PartitionSpec as P

EPSILON = 1e-05
GROUP = 4
VMEM_LIMIT = 48 * 1024 * 1024
CHUNKS = ((0, 256), (256, 256), (512, 256))


def split_bf16(x):
    high = x.astype(jnp.bfloat16)
    low = (x - high.astype(jnp.float32)).astype(jnp.bfloat16)
    return high, low


def time_transforms(length, taps):
    reach = taps // 2
    size = 16
    while size < length + reach:
        size *= 2
    half = size // 2
    f = np.arange(half)[:, None]
    t = np.arange(length)[None, :]
    angle = 2 * np.pi * f * t / size
    sign = np.where(np.arange(length) % 2 == 0, 1.0, -1.0)
    fwd_re, fwd_im = np.cos(angle), -np.sin(angle)
    fwd_im[0] = sign
    weight = np.where(np.arange(half) == 0, 1.0, 2.0)[:, None] / size
    inv_re, inv_im = (weight * np.cos(angle)).T, (-weight * np.sin(angle)).T
    inv_im[:, 0] = sign / size
    eye = np.eye(GROUP)
    forward = np.concatenate([np.kron(eye, fwd_re), np.kron(eye, fwd_im)], axis=0)
    inverse = np.concatenate([np.kron(eye, inv_re), np.kron(eye, inv_im)], axis=1)
    m = np.arange(taps) - reach
    tap_angle = 2 * np.pi * f * m[None, :] / size
    tap_sign = np.where(m % 2 == 0, 1.0, -1.0)
    hat_re, hat_im = np.cos(tap_angle), np.sin(tap_angle)
    hat_nyq = hat_re.copy()
    hat_nyq[0] = tap_sign
    hats = np.concatenate([hat_re, hat_im, hat_nyq], axis=0)
    back_1 = (weight * np.cos(tap_angle)).T
    back_2 = back_1.copy()
    back_2[:, 0] = tap_sign / size
    back_3 = (-weight * np.sin(tap_angle)).T
    back = np.concatenate([back_1, back_2, back_3], axis=1)
    return half, forward, inverse, hats.astype(np.float32), back.astype(np.float32)


def three_pass(matrix):
    high = matrix.astype(np.float32).astype(jnp.bfloat16)
    low = (matrix - high.astype(np.float64)).astype(np.float32).astype(jnp.bfloat16)
    return np.concatenate([high, low, high], axis=1)


def three_terms(x):
    high, low = split_bf16(x)
    return jnp.concatenate([high, high, low], axis=0)


def sigmoid(x):
    return 1.0 / (1.0 + jnp.exp(-x))


def scale_kernel(own, sib, gain, scaled, scaled_t):
    def run(frames):
        wide = frames[...].astype(jnp.float32)
        center = wide - jnp.mean(wide, axis=-1, keepdims=True)
        inv_std = lax.rsqrt(jnp.mean(center * center, axis=-1, keepdims=True) + EPSILON)
        res = (center * inv_std * gain[...]).astype(jnp.bfloat16)
        scaled[...] = res
        scaled_t[...] = res.T

    first = pl.program_id(0) < pl.num_programs(0) // 2
    pl.when(first)(lambda: run(own))
    pl.when(jnp.logical_not(first))(lambda: run(sib))


def chunk_kernel(red_size, length, start, has_out, idx, *rest):
    rest = list(rest)
    scaled_hbm, scaled_t_hbm, w_in = rest[:3]
    z_parts, rest = rest[3 : 2 + red_size], rest[2 + red_size :]
    xv, yg, frames_own, frames_sib, cot_own, cot_sib, live, hats, fwd, inv = rest[:10]
    rest = rest[10 + 2 * has_out :]
    out_own, out_sib, grads, gh, w_out, sums = rest[0], rest[1], rest[2:6], *rest[6:9]
    scaled, scaled_t, w, grad, sem_w, sem_s, sem_t, sem_o, sem_g = rest[9:]
    core, quarter, red, parity = idx[0], idx[1], idx[2], idx[3]
    n_rows, model_width = scaled.shape
    width = w.shape[1] // 2
    block = model_width // red_size
    half_block, part = block // 2, block // 4
    half = hats.shape[1]

    copies = []

    def fetch(src, row, rows, column):
        row = pl.multiple_of(row, 16)
        dst = w.at[pl.ds(row, rows), column : column + src.shape[-1]]
        copies.append(pltpu.make_async_copy(src, dst, sem_w.at[len(copies)]))

    for side in range(2):
        column = pl.multiple_of(core * (model_width // 2) + side * model_width + start, 128)
        fetch(w_in.at[:, pl.ds(column, width)], red * block, block, side * width)
    for s in range(1, red_size):
        row = lax.rem(red + red_size - s, red_size) * block
        fetch(z_parts[s - 1], row + parity * half_block, half_block, 0)
        fetch(xv.at[s - 1], row + (1 - parity) * half_block, half_block, 0)
        fetch(yg.at[s - 1], row + (1 - parity) * half_block, half_block, width)
    get_scaled = pltpu.make_async_copy(scaled_hbm, scaled, sem_s)
    get_scaled_t = pltpu.make_async_copy(scaled_t_hbm, scaled_t, sem_t)
    for copy in copies:
        copy.start()
    get_scaled.start()
    get_scaled_t.start()
    for copy in copies:
        copy.wait()
    put_w = pltpu.make_async_copy(w, w_out, sem_o)
    put_w.start()
    get_scaled.wait()

    rows = GROUP * length
    per_core = n_rows // rows // 2
    hat_a, hat_b, hat_c = hats[0], hats[1], hats[2]
    sums[...] = jnp.zeros_like(sums)

    def stages(group):
        at = pl.ds(group * rows, rows)
        local_at = pl.ds(group % per_core * rows, rows)
        if group < per_core:
            frames, cot, out = frames_own, cot_own, out_own
        else:
            frames, cot, out = frames_sib, cot_sib, out_sib

        def alive():
            return jnp.concatenate([live[at, :]] * (width // 128), axis=1)

        hidden = jnp.dot(scaled[at, :], w[...], preferred_element_type=jnp.float32)
        yield
        value = hidden[:, :width]
        gate = sigmoid(hidden[:, width:])
        terms = three_terms(value * gate * alive())
        yield
        x_hat = jnp.dot(fwd[...], terms, preferred_element_type=jnp.float32)
        yield
        x_hat = x_hat.reshape(2, GROUP, half, width)
        x_re, x_im = x_hat[0], x_hat[1]
        terms = three_terms(
            jnp.concatenate(
                [
                    (x_re * hat_a - x_im * hat_b).reshape(GROUP * half, width),
                    (x_re * hat_b + x_im * hat_c).reshape(GROUP * half, width),
                ],
                axis=0,
            )
        )
        yield
        conv = jnp.dot(inv[...], terms, preferred_element_type=jnp.float32)
        yield
        s = sigmoid(conv)
        wide = frames[local_at, :].astype(jnp.float32)
        out[local_at, :] = ((wide + conv * s) * alive()).astype(out.dtype)
        upstream = cot[local_at, :].astype(jnp.float32) * alive()
        terms = three_terms(upstream * (s * (1.0 + conv * (1.0 - s))))
        yield
        g_hat = jnp.dot(fwd[...], terms, preferred_element_type=jnp.float32)
        yield
        g_hat = g_hat.reshape(2, GROUP, half, width)
        g_re, g_im = g_hat[0], g_hat[1]
        sums[:half] += jnp.sum(g_re * x_re, axis=0)
        sums[half : 2 * half] += jnp.sum(g_im * x_im, axis=0)
        sums[2 * half :] += jnp.sum(g_re * x_im - g_im * x_re, axis=0)
        terms = three_terms(
            jnp.concatenate(
                [
                    (g_re * hat_a + g_im * hat_b).reshape(GROUP * half, width),
                    (g_im * hat_c - g_re * hat_b).reshape(GROUP * half, width),
                ],
                axis=0,
            )
        )
        yield
        grad_glu = jnp.dot(inv[...], terms, preferred_element_type=jnp.float32)
        yield
        grad_v = grad_glu * alive() * gate
        gh[at, :width] = grad_v.astype(jnp.bfloat16)
        gh[at, width:] = (grad_v * value * (1.0 - gate)).astype(jnp.bfloat16)

    running = [stages(group) for group in range(2 * per_core)]
    turn = 0
    while any(g is not None for g in running):
        for group in range(min(turn + 1, len(running))):
            if running[group] is not None:
                try:
                    next(running[group])
                except StopIteration:
                    running[group] = None
        turn += 1

    get_scaled_t.wait()
    sends = []
    for b in range(red_size):
        grad[pl.ds(b * block, block), :] = jnp.dot(
            scaled_t[pl.ds(b * block, block), :], gh[...], preferred_element_type=jnp.float32
        ).astype(jnp.bfloat16)
        slot = lax.rem(b + red_size - red, red_size)
        for r in range(4):
            row = pl.multiple_of(b * block + lax.bitwise_xor(quarter, r) * part, 16)
            copy = pltpu.make_async_copy(
                grad.at[pl.ds(row, part), :], grads[r].at[slot], sem_g.at[len(sends)]
            )
            copy.start()
            sends.append(copy)
    for copy in sends:
        copy.wait()
    put_w.wait()


def plane_kernel(*refs):
    parts, outs = refs[:4], refs[4:]
    for s, out in enumerate(outs):
        terms = [p[s].astype(jnp.float32) for p in parts]
        out[...] = tree_sum(terms).astype(out.dtype)


def grad_scaled_kernel(n_chunks, *refs):
    ghs, ws, out = refs[:n_chunks], refs[n_chunks : 2 * n_chunks], refs[2 * n_chunks]
    out[...] = scaled_gradient(ghs, ws).astype(out.dtype)


def scaled_gradient(ghs, ws):
    total = None
    for gh, w in zip(ghs, ws):
        term = lax.dot_general(
            gh[...], w[...], (((1,), (1,)), ((), ())), preferred_element_type=jnp.float32
        )
        total = term if total is None else total + term
    return total


def frame_kernel(n_chunks, idx, frames, cot, live, gain, other, out_mine, out_other, *rest):
    ghs, ws = rest[:n_chunks], rest[n_chunks : 2 * n_chunks]
    out, frame_out, gain_sum = rest[2 * n_chunks :]
    model_width = frames.shape[1]
    side = model_width // 2
    mine = pl.multiple_of(idx[0] * side, 128)
    out[:, pl.ds(mine, side)] = out_mine[...]
    out[:, pl.ds(pl.multiple_of(side - mine, 128), side)] = out_other[...]
    grad_scaled = scaled_gradient(ghs, ws) + other[...].astype(jnp.float32)
    wide = frames[...].astype(jnp.float32)
    center = wide - jnp.mean(wide, axis=-1, keepdims=True)
    inv_std = lax.rsqrt(jnp.mean(center * center, axis=-1, keepdims=True) + EPSILON)
    normed = center * inv_std
    part_sum = jnp.sum((grad_scaled * normed).reshape(-1, 8, model_width), axis=0)

    @pl.when(pl.program_id(0) == 0)
    def _():
        gain_sum[...] = part_sum

    @pl.when(pl.program_id(0) != 0)
    def _():
        gain_sum[...] += part_sum

    grad_normed = grad_scaled * gain[...]
    alive = jnp.concatenate([live[...]] * (model_width // 128), axis=1)
    upstream = cot[...].astype(jnp.float32) * alive
    res = upstream + inv_std * (
        grad_normed
        - jnp.mean(grad_normed, axis=-1, keepdims=True)
        - normed * jnp.mean(grad_normed * normed, axis=-1, keepdims=True)
    )
    frame_out[...] = (res * alive).astype(frame_out.dtype)


def place_kernel(has_out, idx, mine, sib, *rest):
    out = rest[has_out]
    quarter = idx[1]
    part = mine.shape[1]
    side = pl.program_id(1)
    width = out.shape[1]

    def write(src):
        for r in range(4):
            q = lax.bitwise_xor(r, quarter)
            row = pl.ds(pl.multiple_of(q * part, 16), part)
            out[row, :] = src[r, :, pl.ds(pl.multiple_of(side * width, 128), width)].astype(jnp.float32)

    own = pl.program_id(0) == idx[0]
    pl.when(own)(lambda: write(mine))
    pl.when(jnp.logical_not(own))(lambda: write(sib))


def pack_first_kernel(idx, values, gates, out):
    width = values.shape[1]
    out[:, :width] = values[...]
    out[:, width:] = gates[...]


def pack_second_kernel(n, *refs):
    parts, (out_v, out_g) = refs[:n], refs[n:]
    width = out_v.shape[2]
    for s in range(n):
        out_v[s] = parts[s][:, :width]
        out_g[s] = parts[s][:, width:]


def line_kernel(n, root, *refs):
    terms = [part[...].astype(jnp.float32) for part in refs[:n]]
    refs[n][...] = (tree_sum(terms) * root[0]).astype(refs[n].dtype)


def ordered(body, n_in, n_after):
    def kernel(*refs):
        return body(*refs[:n_in], *refs[n_in + n_after :])

    return kernel


def tree_sum(terms):
    if len(terms) == 1:
        return terms[0]
    return tree_sum(terms[::2]) + tree_sum(terms[1::2])


def whole(shape):
    return pl.BlockSpec(shape, lambda *_: (0,) * len(shape))


def params():
    return pltpu.CompilerParams(vmem_limit_bytes=VMEM_LIMIT)


def cost(flops, moved, transcendentals=0):
    return pl.CostEstimate(flops=flops, bytes_accessed=moved, transcendentals=transcendentals)


ANY = pl.BlockSpec(memory_space=pltpu.HBM)


def local(frames, cotangent, w_in, kernel, gain, lengths):
    dp_size = lax.axis_size("dp")
    red_size = lax.axis_size("red")
    dp = lax.axis_index("dp")
    red = lax.axis_index("red")
    local_utts, length, model_width = frames.shape
    taps = kernel.shape[0]
    block = model_width // red_size
    part = block // 4
    side = model_width // 2
    own_rows = local_utts * length
    n_rows = 2 * own_rows
    n_chunks = len(CHUNKS)

    core = dp % 2
    quarter = (dp // 2) % 4
    parity = (quarter + quarter // 2) % 2
    idx = jnp.stack([core, quarter, red, parity]).astype(jnp.int32)

    def to_core(x):
        return lax.ppermute(x, "dp", [(i, i ^ 1) for i in range(dp_size)])

    def to_quarter(x, r):
        return lax.ppermute(x, "dp", [(i, i ^ (2 * r)) for i in range(dp_size)])

    def shift_red(x, s):
        return lax.ppermute(x, "red", [(i, (i + s) % red_size) for i in range(red_size)])

    def other_groups(x):
        bit = 8
        while bit < dp_size:
            x = x + lax.ppermute(x, "dp", [(i, i ^ bit) for i in range(dp_size)])
            bit *= 2
        return x

    half, forward, inverse, hat_matrix, back_matrix = time_transforms(length, taps)
    fwd3, inv3 = jnp.asarray(three_pass(forward)), jnp.asarray(three_pass(inverse))

    flat_frames = frames.reshape(own_rows, model_width)
    flat_cot = cotangent.reshape(own_rows, model_width)

    def first_sends(chunk, *deps):
        start, width = CHUNKS[chunk]
        column, columns = start // width, side // width

        def strip(which):
            return pl.BlockSpec(
                (block // 2, width),
                lambda i, idx: (idx[3], idx[0] * columns + column + which * 2 * columns),
            )

        mine = pl.pallas_call(
            ordered(pack_first_kernel, 3, len(deps)),
            grid_spec=pltpu.PrefetchScalarGridSpec(
                num_scalar_prefetch=1,
                grid=(1,),
                in_specs=[strip(0), strip(1)] + [ANY] * len(deps),
                out_specs=whole((block // 2, 2 * width)),
            ),
            out_shape=jax.ShapeDtypeStruct((block // 2, 2 * width), jnp.bfloat16),
            compiler_params=params(),
            cost_estimate=cost(0, 4 * block * width),
        )(idx, w_in, w_in, *deps)
        return mine, [shift_red(mine, s) for s in range(1, red_size)]

    def second_pack(z_parts, *deps):
        n = len(z_parts)
        width = z_parts[0].shape[1] // 2
        shape = (n, block // 2, width)
        return pl.pallas_call(
            ordered(functools.partial(pack_second_kernel, n), n, len(deps)),
            grid=(1,),
            in_specs=[whole(z_parts[0].shape)] * n + [ANY] * len(deps),
            out_specs=[whole(shape)] * 2,
            out_shape=[jax.ShapeDtypeStruct(shape, jnp.bfloat16)] * 2,
            compiler_params=params(),
            cost_estimate=cost(0, 4 * n * block * width),
        )(*z_parts, *deps)

    def second_sends(packed):
        return to_quarter(packed[0], 1), to_quarter(packed[1], 2)

    mine, z_first = first_sends(0)
    z = [z_first]
    sib_frames, sib_cot = to_core(flat_frames), to_core(flat_cot)

    tile = 256
    tiles = own_rows // tile
    scaled, scaled_t = pl.pallas_call(
        ordered(scale_kernel, 3, 1),
        grid=(2 * tiles,),
        in_specs=[
            pl.BlockSpec((tile, model_width), lambda i: (jnp.minimum(i, tiles - 1), 0)),
            pl.BlockSpec((tile, model_width), lambda i: (jnp.maximum(i - tiles, 0), 0)),
            whole((1, model_width)),
            ANY,
        ],
        out_specs=[
            pl.BlockSpec((tile, model_width), lambda i: (i, 0)),
            pl.BlockSpec((model_width, tile), lambda i: (0, i)),
        ],
        out_shape=[
            pltpu.HBM((n_rows, model_width), jnp.bfloat16),
            pltpu.HBM((model_width, n_rows), jnp.bfloat16),
        ],
        compiler_params=params(),
        cost_estimate=cost(10 * n_rows * model_width, 6 * n_rows * model_width),
    )(flat_frames, sib_frames, gain.reshape(1, model_width), mine)

    packed = [second_pack(z[0], scaled)]
    near = [second_sends(packed[0])]
    firsts = []
    for chunk in range(1, n_chunks):
        mine, z_next = first_sends(chunk, *z[-1], *([scaled] if chunk == 1 else []))
        z.append(z_next)
        firsts.append(mine)
    if n_chunks > 1:
        packed.append(second_pack(z[1], *near[0]))
        near.append(second_sends(packed[1]))

    by_owner = lengths.reshape(dp_size, red_size, local_utts)

    def alive_rows(device):
        own = lax.dynamic_slice(by_owner, (device, red, 0), (1, 1, local_utts)).reshape(local_utts)
        return jnp.arange(length, dtype=jnp.int32)[None, :] < own[:, None]

    alive = jnp.stack([alive_rows(dp), alive_rows(dp + 1 - 2 * core)]).astype(jnp.float32)
    live = jnp.broadcast_to(alive.reshape(n_rows, 1), (n_rows, 128))
    root = lax.rsqrt(jnp.sum(lengths).astype(jnp.float32))
    hats = jnp.dot(hat_matrix, kernel, precision=lax.Precision.HIGHEST).reshape(3, half, model_width)

    def middle(chunk, outs, deps):
        start, width = CHUNKS[chunk]
        near_column = start // width
        columns = side // width

        def strip(*leading):
            return pl.BlockSpec(
                (*leading, width),
                lambda i, idx: (*(0 for _ in leading), idx[0] * columns + near_column),
            )

        operands = [scaled, scaled_t, w_in, *z[chunk], *near[chunk]]
        in_specs = [ANY] * len(operands)
        operands += [flat_frames, sib_frames, flat_cot, sib_cot, live, hats, fwd3, inv3]
        in_specs += [strip(own_rows)] * 4
        in_specs += [whole((n_rows, 128)), strip(3, half), whole(fwd3.shape), whole(inv3.shape)]
        aliases = {}
        if outs is not None:
            aliases = {len(operands) + 1: 0, len(operands) + 2: 1}
            operands += outs
            in_specs += [ANY] * 2
        n_in = len(operands) + 1
        operands += deps
        in_specs += [ANY] * len(deps)
        near_strip = pl.BlockSpec((own_rows, width), lambda i, idx: (0, near_column))
        return pl.pallas_call(
            ordered(
                functools.partial(chunk_kernel, red_size, length, start, 1 if aliases else 0),
                n_in,
                len(deps),
            ),
            grid_spec=pltpu.PrefetchScalarGridSpec(
                num_scalar_prefetch=1,
                grid=(1,),
                in_specs=in_specs,
                out_specs=[near_strip, near_strip]
                + [ANY] * 4
                + [whole((n_rows, 2 * width)), ANY, whole((3 * half, width))],
                scratch_shapes=[
                    pltpu.VMEM((n_rows, model_width), jnp.bfloat16),
                    pltpu.VMEM((model_width, n_rows), jnp.bfloat16),
                    pltpu.VMEM((model_width, 2 * width), jnp.bfloat16),
                    pltpu.VMEM((model_width, 2 * width), jnp.bfloat16),
                    pltpu.SemaphoreType.DMA((3 * red_size - 1,)),
                    pltpu.SemaphoreType.DMA,
                    pltpu.SemaphoreType.DMA,
                    pltpu.SemaphoreType.DMA,
                    pltpu.SemaphoreType.DMA((4 * red_size,)),
                ],
            ),
            out_shape=[
                pltpu.HBM((own_rows, side), jnp.bfloat16),
                pltpu.HBM((own_rows, side), jnp.bfloat16),
                *[jax.ShapeDtypeStruct((red_size, part, 2 * width), jnp.bfloat16)] * 4,
                pltpu.HBM((n_rows, 2 * width), jnp.bfloat16),
                jax.ShapeDtypeStruct((model_width, 2 * width), jnp.bfloat16),
                jax.ShapeDtypeStruct((3 * half, width), jnp.float32),
            ],
            input_output_aliases=aliases,
            compiler_params=params(),
            cost_estimate=cost(
                8 * n_rows * model_width * width + 24 * 256 * n_rows * width, 1 << 24, 4 * n_rows * width
            ),
        )(idx, *operands)

    def add_plane(parts, *deps):
        shape = parts[0].shape
        return pl.pallas_call(
            ordered(plane_kernel, 4, len(deps)),
            grid=(1,),
            in_specs=[whole(shape)] * 4 + [ANY] * len(deps),
            out_specs=[whole(shape[1:])] * red_size,
            out_shape=[jax.ShapeDtypeStruct(shape[1:], jnp.bfloat16)] * red_size,
            compiler_params=params(),
            cost_estimate=cost(4 * parts[0].size, 10 * parts[0].size),
        )(*parts, *deps)

    def send_plane(grads):
        return [grads[0], *(to_quarter(grads[r], r) for r in range(1, 4))]

    def send_line(parts):
        return [parts[0], *(shift_red(parts[s], s) for s in range(1, red_size))]

    def add_line(parts, *deps):
        shape = parts[0].shape
        kind = jnp.bfloat16 if dp_size <= 8 else jnp.float32
        owned = pl.pallas_call(
            ordered(functools.partial(line_kernel, red_size), 1 + red_size, len(deps)),
            grid=(1,),
            in_specs=[pl.BlockSpec(memory_space=pltpu.SMEM)]
            + [whole(shape)] * red_size
            + [ANY] * len(deps),
            out_specs=whole(shape),
            out_shape=jax.ShapeDtypeStruct(shape, kind),
            compiler_params=params(),
            cost_estimate=cost(8 * parts[0].size, 10 * parts[0].size),
        )(root.reshape(1), *parts, *deps)
        return other_groups(owned).astype(jnp.bfloat16)

    def spread(owned):
        return [owned, *(to_quarter(owned, r) for r in range(1, 4))]

    def place(chunk, mine, sib, grad_out):
        start, width = CHUNKS[chunk]
        near_column, columns = start // width, side // width
        has_out = 0 if grad_out is None else 1
        operands = [mine, sib] + ([grad_out] if has_out else [])
        return pl.pallas_call(
            functools.partial(place_kernel, has_out),
            grid_spec=pltpu.PrefetchScalarGridSpec(
                num_scalar_prefetch=1,
                grid=(2, 2),
                in_specs=[whole(mine.shape)] * 2 + [ANY] * has_out,
                out_specs=pl.BlockSpec(
                    (block, width),
                    lambda c, h, idx: (0, near_column + c * columns + h * 2 * columns),
                ),
            ),
            out_shape=jax.ShapeDtypeStruct((block, 2 * model_width), jnp.float32),
            input_output_aliases={3: 0} if has_out else {},
            compiler_params=params(),
            cost_estimate=cost(0, 20 * block * width),
        )(idx, *operands)

    outs, ghs, ws, sums = None, [], [], []
    on_way, planes, lines = [], [], []
    for chunk in range(n_chunks):
        deps = []
        if chunk == 0 and n_chunks > 1:
            deps += [packed[1][0], *firsts]
        if chunk + 1 < n_chunks and chunk > 0:
            packed.append(second_pack(z[chunk + 1], sums[-1]))
            near.append(second_sends(packed[-1]))
            deps += [packed[-1][0]]
        if chunk >= 2:
            planes.append(send_line(add_plane(on_way[chunk - 2], sums[-1])))
            deps += [planes[-1][0]]
        *outs, g0, g1, g2, g3, gh, w, tap_sums = middle(chunk, outs, deps)
        on_way.append(send_plane([g0, g1, g2, g3]))
        ghs.append(gh)
        ws.append(w)
        sums.append(tap_sums)

    out_other = to_core(outs[1])
    step = GROUP * length
    steps = own_rows // step
    row_spec = pl.BlockSpec((step, model_width), lambda i, *_: (i, 0))
    gh_specs = [pl.BlockSpec((step, gh.shape[1]), lambda i, *_: (i, 0)) for gh in ghs]
    sib_specs = [pl.BlockSpec((step, gh.shape[1]), lambda i, *_: (i + steps, 0)) for gh in ghs]
    w_specs = [whole(w.shape) for w in ws]
    flops = 2 * own_rows * model_width * model_width
    deps = [sums[-1]]
    while len(planes) < n_chunks - 1:
        planes.append(send_line(add_plane(on_way[len(planes)], sums[-1])))
        deps.append(planes[-1][0])
    while len(lines) < n_chunks - 2:
        lines.append(add_line(planes[len(lines)], sums[-1]))
        deps.append(lines[-1])
    grad_scaled_sib = pl.pallas_call(
        ordered(functools.partial(grad_scaled_kernel, n_chunks), 2 * n_chunks, len(deps)),
        grid=(steps,),
        in_specs=sib_specs + w_specs + [ANY] * len(deps),
        out_specs=row_spec,
        out_shape=jax.ShapeDtypeStruct((own_rows, model_width), jnp.bfloat16),
        compiler_params=params(),
        cost_estimate=cost(flops, 10 << 20),
    )(*ghs, *ws, *deps)
    other = to_core(grad_scaled_sib)
    deps = []
    while len(lines) < n_chunks - 1:
        lines.append(add_line(planes[len(lines)], grad_scaled_sib))
        deps.append(lines[-1])
    planes.append(send_line(add_plane(on_way[-1], grad_scaled_sib)))
    deps.append(planes[-1][0])
    side_spec = pl.BlockSpec((step, side), lambda i, *_: (i, 0))
    module_output, frame_gradient, gain_part = pl.pallas_call(
        ordered(functools.partial(frame_kernel, n_chunks), 8 + 2 * n_chunks, len(deps)),
        grid_spec=pltpu.PrefetchScalarGridSpec(
            num_scalar_prefetch=1,
            grid=(steps,),
            in_specs=[
                row_spec,
                row_spec,
                pl.BlockSpec((step, 128), lambda i, *_: (i, 0)),
                whole((1, model_width)),
                row_spec,
                side_spec,
                side_spec,
                *gh_specs,
                *w_specs,
                *[ANY] * len(deps),
            ],
            out_specs=[row_spec, row_spec, whole((8, model_width))],
        ),
        out_shape=[
            jax.ShapeDtypeStruct((own_rows, model_width), jnp.bfloat16),
            jax.ShapeDtypeStruct((own_rows, model_width), jnp.bfloat16),
            jax.ShapeDtypeStruct((8, model_width), jnp.float32),
        ],
        compiler_params=params(),
        cost_estimate=cost(2 * flops, 30 << 20),
    )(
        idx,
        flat_frames,
        flat_cot,
        live,
        gain.reshape(1, model_width),
        other,
        outs[0],
        out_other,
        *ghs,
        *ws,
        *deps,
    )

    while len(lines) < n_chunks:
        lines.append(add_line(planes[len(lines)], gain_part))
    grad_out = None
    for chunk in range(n_chunks):
        mine = jnp.stack(spread(lines[chunk]))
        grad_out = place(chunk, mine, to_core(mine), grad_out)

    order = sorted(range(n_chunks), key=lambda c: CHUNKS[c][0])
    tap_part = jnp.dot(
        back_matrix,
        jnp.concatenate([sums[c] for c in order], axis=1),
        precision=lax.Precision.HIGHEST,
    )
    gain_part = jnp.sum(gain_part, axis=0).reshape(2, side)
    kept = lax.dynamic_index_in_dim(gain_part, core, 0)
    sent = lax.dynamic_index_in_dim(gain_part, 1 - core, 0)
    small = jnp.concatenate([tap_part, kept + to_core(sent)], axis=0)
    small = tree_sum([small, *(to_quarter(small, r) for r in range(1, 4))])
    small = tree_sum([small, *(shift_red(small, s) for s in range(1, red_size))])
    small = other_groups(small) * root
    both = to_core(small)
    first = core == 0
    small = jnp.concatenate([jnp.where(first, small, both), jnp.where(first, both, small)], axis=1)
    return (
        module_output.reshape(frames.shape),
        frame_gradient.reshape(frames.shape),
        grad_out,
        small[:taps],
        small[taps],
    )


def solution(mesh):
    placed = (
        P(("dp", "red"), None, None),
        P(("dp", "red"), None, None),
        P("red", None),
        P(),
        P(),
        P(),
    )
    return jax.shard_map(
        local,
        mesh=mesh,
        in_specs=placed,
        out_specs=(
            P(("dp", "red"), None, None),
            P(("dp", "red"), None, None),
            P("red", None),
            P(),
            P(),
        ),
        check_vma=False,
    )
```

time: 284 us -> 229 us (0.81); the launches traced: 279 us -> 228 us
  waiting for transfers between devices: 74.2 us -> 35.2 us
  Pallas kernels: 78.6 us -> 103 us
  local copies, waits for them, and re-layouts: 26.7 us -> 9.24 us
  other arithmetic: 18.4 us -> 3.3 us
  starting transfers between devices: 78.2 us -> 73.3 us
    ppermute x27, waiting for transfers between devices: 51.7 us -> 20.1 us  [to_quarter(): return lax.ppermute(x, 'dp', [(i, i ^ 2 * r) for i in range(dp_size)])]
    pallas_call x7 -> x21, Pallas kernels: 78.6 us -> 103 us  [the longest x3 56.9 us: middle(): pl.pallas_call(ordered(functools.partial(chunk_kernel, red_size, length,...]
    convert_element_type x11 -> x1, other arithmetic: 9.45 us -> 0.01 us  [local(): jnp.stack([alive_rows(dp), alive_rows(dp + 1 - 2 * core)])]
    ppermute x21, waiting for transfers between devices: 21.7 us -> 14.2 us  [shift_red(): lax.ppermute(x, 'red', [(i, (i + s) % red_size) for i in range(red_size)])]
    ppermute x21, starting transfers between devices: 44.8 us -> 37.4 us  [shift_red(): lax.ppermute(x, 'red', [(i, (i + s) % red_size) for i in range(red_size)])]
    unnamed x72 -> x66, local copies, waits for them, and re-layouts: 13.1 us -> 8.19 us
    slice x5 -> x0, local copies, waits for them, and re-layouts: 4.29 us -> none  [the longest x1 2.82 us: local(): own_g = w_in[:, gate_start:gate_start + width]]
    transpose x1 -> x0, local copies, waits for them, and re-layouts: 4.28 us -> none  [local(): scaled_t = scaled.T]
  transfers between devices with their start and end apart: 65 -> 57, of which waited for: 23 -> 16; matrix products, arithmetic and copies ran while one was open for 11% -> 3% of each run, Pallas kernels for 27% -> 40%
where the time goes in v2:
time: 229 us; the launch traced here: 228 us
  Pallas kernels  103 us (45%)
  starting transfers between devices  73.3 us (32%)
  waiting for transfers between devices  35.2 us (15%)
  local copies, waits for them, and re-layouts  9.24 us (4%)
  other arithmetic  3.3 us (1%)
  matrix products  2.33 us (1%)
    pallas_call x3, Pallas kernels, middle(): pl.pallas_call(ordered(functools.partial(chunk_kernel, red_size, length,...  56.9 us
    ppermute x21, starting transfers between devices, shift_red(): lax.ppermute(x, 'red', [(i, (i + s) % red_size) for i in range(red_size)])  37.4 us
    ppermute x27, starting transfers between devices, to_quarter(): return lax.ppermute(x, 'dp', [(i, i ^ 2 * r) for i in range(dp_size)])  34 us
    ppermute x27, waiting for transfers between devices, to_quarter(): return lax.ppermute(x, 'dp', [(i, i ^ 2 * r) for i in range(dp_size)])  20.1 us
    pallas_call x1, Pallas kernels, local(): pl.pallas_call(ordered(functools.partial(frame_kernel, n_chunks), 8 + 2 *...  14.7 us
    ppermute x21, waiting for transfers between devices, shift_red(): lax.ppermute(x, 'red', [(i, (i + s) % red_size) for i in range(red_size)])  14.2 us
    pallas_call x1, Pallas kernels, local(): pl.pallas_call(ordered(functools.partial(grad_scaled_kernel, n_chunks), 2...  9.96 us
    unnamed x66, local copies, waits for them, and re-layouts  8.19 us
  transfers between devices with their start and end apart: 57, of which 16 were waited for; matrix products, arithmetic and copies ran while one was open for 3% of the time, Pallas kernels for 40%

profile of v2, /device:TPU:0, one launch (start us, length us, event | category | flops | bytes accessed | tf_op | source)
XLA Modules:
  0.0 228.4 jit_solution(6159027516758718493)
XLA Ops:
  1.3 1.7 copy-done.2
  3.6 3.1 %collective-permute-start.1 = (bf16[192,512]{1,0:T(8,128)(2,1)S(1)}, bf16[192,512]{1,0:T(8,128)(2,1)S(1)}, u32[]{:S(2)}, u32[]{:S(2)}) collective-permute-start(bf16[192,512]{1,0:T(8,128)(2,1)S(1)} %shard_map.137.refs_3_), channel_id=1, source_target_pairs={{0,1},{1,2},{2,3},{3,0},{4,5},{5,6},{6,7},{7,4},{8,9},{9,10},{10,1... | collective-permute-start | bytes 589832 | tf_op jit(solution)/shard_map/ppermute | solution.py:371
  6.6 2.6 %collective-permute-start.2 = (bf16[192,512]{1,0:T(8,128)(2,1)S(1)}, bf16[192,512]{1,0:T(8,128)(2,1)S(1)}, u32[]{:S(2)}, u32[]{:S(2)}) collective-permute-start(bf16[192,512]{1,0:T(8,128)(2,1)S(1)} %shard_map.137.refs_3_), channel_id=1, source_target_pairs={{0,2},{1,3},{2,0},{3,1},{4,6},{5,7},{6,4},{7,5},{8,10},{9,11},{10,... | collective-permute-start | bytes 589832 | tf_op jit(solution)/shard_map/ppermute | solution.py:371
  10.7 1.8 copy-done.4
  12.5 8.1 %shard_map.138 = (bf16[1536,1536]{1,0:T(8,128)(2,1)}, bf16[1536,1536]{1,0:T(8,128)(2,1)}) custom-call(bf16[768,1536]{1,0:T(8,128)(2,1)S(1)} %bitcast.36, bf16[768,1536]{1,0:T(8,128)(2,1)} %collective-permute-done.refs_1_.refs_10_, f32[1,1536]{1,0:T(1,128)S(1)} %reshape.129.refs_2_.refs_4_, bf16[192,512]{1,0:T(8,128)(2,1)S(1)} %shard_map.137.refs_3_), custom_call_target="tpu_custom_call" | custom-call | flops 23592960 | bytes 14155776 | tf_op jit(solution)/shard_map/pallas_call | solution.py:433
  20.6 1.7 collective-permute-done.2.refs_1_.refs_4_.refs_5_
  23.6 4.7 %collective-permute-start.7 = (bf16[192,512]{1,0:T(8,128)(2,1)}, bf16[192,512]{1,0:T(8,128)(2,1)S(1)}, u32[]{:S(2)}, u32[]{:S(2)}) collective-permute-start(bf16[192,512]{1,0:T(8,128)(2,1)} %shard_map.140.refs_18_), channel_id=1, source_target_pairs={{0,1},{1,2},{2,3},{3,0},{4,5},{5,6},{6,7},{7,4},{8,9},{9,10},{10,1... | collective-permute-start | bytes 589832 | tf_op jit(solution)/shard_map/ppermute | solution.py:371
  30.7 1.5 collective-permute-start.5
  32.9 1.6 collective-permute-start.8
  34.6 1.8 collective-permute-start.9
  37.8 7.4 %collective-permute-done.8.refs_1_.refs_4_.refs_5_ = bf16[192,512]{1,0:T(8,128)(2,1)S(1)} collective-permute-done((bf16[192,512]{1,0:T(8,128)(2,1)}, bf16[192,512]{1,0:T(8,128)(2,1)S(1)}, u32[]{:S(2)}, u32[]{:S(2)}) %collective-permute-start.8) | collective-permute-done | bytes 196640 | tf_op jit(solution)/shard_map/ppermute | solution.py:371
  45.8 3.9 %collective-permute-start.12 = (bf16[192,512]{1,0:T(8,128)(2,1)S(1)}, bf16[192,512]{1,0:T(8,128)(2,1)S(1)}, u32[]{:S(2)}, u32[]{:S(2)}) collective-permute-start(bf16[192,512]{1,0:T(8,128)(2,1)S(1)} %shard_map.142.refs_19_), channel_id=1, source_target_pairs={{0,1},{1,2},{2,3},{3,0},{4,5},{5,6},{6,7},{7,4},{8,9},{9,10},{10,1... | collective-permute-start | bytes 589832 | tf_op jit(solution)/shard_map/ppermute | solution.py:371
  49.6 1.7 collective-permute-start.13
  53.6 19.2 %shard_map.143 = (bf16[768,768]{1,0:T(8,128)(2,1)}, bf16[768,768]{1,0:T(8,128)(2,1)}, bf16[4,96,512]{2,1,0:T(8,128)(2,1)S(1)}, bf16[4,96,512]{2,1,0:T(8,128)(2,1...) custom-call(s32[4]{0:T(128)S(1)} %pad_add_fusion.refs_0_.idx, ...), custom_call_target="tpu_custom_call" | custom-call | flops 7247757312 | bytes 16777216 | tf_op jit(solution)/shard_map/pallas_call | solution.py:501
  72.8 1.6 collective-permute-start.17
  74.3 1.5 collective-permute-start.18
  77.2 1.5 collective-permute-start.15
  78.7 1.5 collective-permute-start.16
  80.2 19.4 %shard_map.145 = (bf16[768,768]{1,0:T(8,128)(2,1)}, bf16[768,768]{1,0:T(8,128)(2,1)}, bf16[4,96,512]{2,1,0:T(8,128)(2,1)S(1)}, bf16[4,96,512]{2,1,0:T(8,128)(2,1...) custom-call(s32[4]{0:T(128)S(1)} %pad_add_fusion.refs_0_.idx, ...), custom_call_target="tpu_custom_call", output_to_operand_aliasing={{0}: (17, {}), {1}: (18, {})} | custom-call | flops 7247757312 | bytes 16777216 | tf_op jit(solution)/shard_map/pallas_call | solution.py:501
  106.2 2.0 collective-permute-start.22
  110.8 18.4 %shard_map.147 = (bf16[768,768]{1,0:T(8,128)(2,1)}, bf16[768,768]{1,0:T(8,128)(2,1)}, bf16[4,96,512]{2,1,0:T(8,128)(2,1)S(1)}, bf16[4,96,512]{2,1,0:T(8,128)(2,1...) custom-call(s32[4]{0:T(128)S(1)} %pad_add_fusion.refs_0_.idx, ...), custom_call_target="tpu_custom_call", output_to_operand_aliasing={{0}: (17, {}), {1}: (18, {})} | custom-call | flops 7247757312 | bytes 16777216 | tf_op jit(solution)/shard_map/pallas_call | solution.py:501
  131.0 10.0 %shard_map.150.refs_5_.refs_4_ = bf16[768,1536]{1,0:T(8,128)(2,1)} custom-call(bf16[1536,512]{1,0:T(8,128)(2,1)S(1)} %copy-done.22, bf16[1536,512]{1,0:T(8,128)(2,1)S(1)} %copy-done.17, bf16[1536,512]{1,0:T(8,128)(2,1)S(1)} %copy-done.18, bf16[1536,512]{1,0:T(8,128)(2,1)} %get-tuple-element.77.refs_3_.refs_11_, ...), custom_call_target="tpu_custom_call" | custom-call | flops 3623878656 | bytes 10485760 | tf_op jit(solution)/shard_map/pallas_call | solution.py:634
  142.8 2.2 collective-permute-start.47
  145.0 2.0 collective-permute-done.45
  148.7 1.9 collective-permute-start.29
  151.8 2.2 collective-permute-done.28.refs_2_
  154.3 2.3 %collective-permute-done.29.refs_3_ = bf16[96,512]{1,0:T(8,128)(2,1)S(1)} collective-permute-done((bf16[96,512]{1,0:T(8,128)(2,1)S(1)}, bf16[96,512]{1,0:T(8,128)(2,1)S(1)}, u32[]{:S(2)}, u32[]{:S(2)}) %collective-permute-start.29) | collective-permute-done | bytes 98336 | tf_op jit(solution)/shard_map/ppermute | solution.py:371
  156.8 2.4 %collective-permute-start.33 = (bf16[4,96,512]{2,1,0:T(8,128)(2,1)}, bf16[4,96,512]{2,1,0:T(8,128)(2,1)}, u32[]{:S(2)}, u32[]{:S(2)}) collective-permute-start(bf16[4,96,512]{2,1,0:T(8,128)(2,1)} %get-tuple-element.97), channel_id=1, source_target_pairs={{0,24},{4,28},{8,16},{12,20},{16,8},{20,12},{24,0},{28,4},{1,25},{... | collective-permute-start | bytes 1179656 | tf_op jit(solution)/shard_map/ppermute | solution.py:368
  161.1 1.7 copy-done.5
  162.9 3.4 %collective-permute-done.31.refs_1_ = bf16[4,96,512]{2,1,0:T(8,128)(2,1)S(1)} collective-permute-done((bf16[4,96,512]{2,1,0:T(8,128)(2,1)}, bf16[4,96,512]{2,1,0:T(8,128)(2,1)S(1)}, u32[]{:S(2)}, u32[]{:S(2)}) %collective-permute-start.31) | collective-permute-done | bytes 393248 | tf_op jit(solution)/shard_map/ppermute | solution.py:368
  166.2 6.1 %collective-permute-done.32.refs_2_ = bf16[4,96,512]{2,1,0:T(8,128)(2,1)S(1)} collective-permute-done((bf16[4,96,512]{2,1,0:T(8,128)(2,1)}, bf16[4,96,512]{2,1,0:T(8,128)(2,1)S(1)}, u32[]{:S(2)}, u32[]{:S(2)}) %collective-permute-start.32) | collective-permute-done | bytes 393248 | tf_op jit(solution)/shard_map/ppermute | solution.py:368
  172.3 2.5 %collective-permute-start.41 = (bf16[96,512]{1,0:T(8,128)(2,1)S(1)}, bf16[96,512]{1,0:T(8,128)(2,1)S(1)}, u32[]{:S(2)}, u32[]{:S(2)}) collective-permute-start(bf16[96,512]{1,0:T(8,128)(2,1)S(1)} %shard_map.151.refs_14_), channel_id=1, source_target_pairs={{0,8},{4,12},{8,0},{12,4},{16,24},{20,28},{24,16},{28,20},{1,9},{5... | collective-permute-start | bytes 294920 | tf_op jit(solution)/shard_map/ppermute | solution.py:368
  174.9 1.7 collective-permute-start.42
  177.9 14.7 %shard_map.153 = (bf16[768,1536]{1,0:T(8,128)(2,1)}, bf16[768,1536]{1,0:T(8,128)(2,1)}, f32[8,1536]{1,0:T(8,128)S(1)}) custom-call(s32[4]{0:T(128)S(1)} %pad_add_fusion.refs_0_.idx, bf16[768,1536]{1,0:T(8,128)(2,1)} %bitcast.35, bf16[768,1536]{1,0:T(8,128)(2,1)} %bitcast.47, f32[1536,128]{1,0:T(8,128)S(1)} %broadcast_in_dim.2.refs_13_.refs_3_, ...), custom_call_target="tpu_custom_call" | custom-call | flops 7247757312 | bytes 31457280 | tf_op jit(solution)/shard_map/pallas_call | solution.py:651
  194.0 1.5 collective-permute-start.50
  195.5 2.0 collective-permute-start.51
  199.1 2.0 collective-permute-done.51
  201.1 1.6 collective-permute-start.35
  203.0 2.9 %collective-permute-start.36 = (bf16[96,512]{1,0:T(8,128)(2,1)S(1)}, bf16[96,512]{1,0:T(8,128)(2,1)S(1)}, u32[]{:S(2)}, u32[]{:S(2)}) collective-permute-start(bf16[96,512]{1,0:T(8,128)(2,1)S(1)} %get-tuple-element.103), channel_id=1, source_target_pairs={{0,3},{1,0},{2,1},{3,2},{4,7},{5,4},{6,5},{7,6},{8,11},{9,8},{10,9... | collective-permute-start | bytes 294920 | tf_op jit(solution)/shard_map/ppermute | solution.py:371
  207.0 3.4 %collective-permute-start.55 = (f32[32,768]{1,0:T(8,128)S(1)}, f32[32,768]{1,0:T(8,128)S(1)}, u32[]{:S(2)}, u32[]{:S(2)}) collective-permute-start(f32[32,768]{1,0:T(8,128)S(1)} %add_add_fusion), channel_id=1, source_target_pairs={{0,3},{1,0},{2,1},{3,2},{4,7},{5,4},{6,5},{7,6},{8,11},{9,8},{10,9... | collective-permute-start | bytes 294920 | tf_op jit(solution)/shard_map/ppermute | solution.py:371
  210.4 2.3 shard_map.155.rest_0_
  212.7 2.3 shard_map.156.rest_0_
  215.0 1.8 collective-permute-start.37
  216.8 2.0 collective-permute-start.38
  218.8 1.7 collective-permute-start.39
  220.6 1.6 collective-permute-done.38
  222.2 2.1 collective-permute-done.39
  226.1 2.3 shard_map.157
  (178 shorter events, 37.6 us)
Async XLA Ops:
  0.6 10.0 %collective-permute-start = (bf16[768,1536]{1,0:T(8,128)(2,1)}, bf16[768,1536]{1,0:T(8,128)(2,1)}, u32[]{:S(2)}, u32[]{:S(2)}) collective-permute-start(bf16[768,1536]{1,0:T(8,128)(2,1)} %bitcast.31), channel_id=1, source_target_pairs={{0,4},{4,0},{8,12},{12,8},{16,20},{20,16},{24,28},{28,24},{1,5},{5... | collective-permute-start | bytes 7077896 | tf_op jit(solution)/shard_map/ppermute | solution.py:365
  1.2 51.6 %collective-permute-start.6 = (bf16[768,1536]{1,0:T(8,128)(2,1)}, bf16[768,1536]{1,0:T(8,128)(2,1)}, u32[]{:S(2)}, u32[]{:S(2)}) collective-permute-start(bf16[768,1536]{1,0:T(8,128)(2,1)} %bitcast.43), channel_id=1, source_target_pairs={{0,4},{4,0},{8,12},{12,8},{16,20},{20,16},{24,28},{28,24},{1,5},{5... | collective-permute-start | bytes 7077896 | tf_op jit(solution)/shard_map/ppermute | solution.py:365
  3.6 17.0 %collective-permute-start.1 = (bf16[192,512]{1,0:T(8,128)(2,1)S(1)}, bf16[192,512]{1,0:T(8,128)(2,1)S(1)}, u32[]{:S(2)}, u32[]{:S(2)}) collective-permute-start(bf16[192,512]{1,0:T(8,128)(2,1)S(1)} %shard_map.137.refs_3_), channel_id=1, source_target_pairs={{0,1},{1,2},{2,3},{3,0},{4,5},{5,6},{6,7},{7,4},{8,9},{9,10},{10,1... | collective-permute-start | bytes 589832 | tf_op jit(solution)/shard_map/ppermute | solution.py:371
  6.6 15.7 %collective-permute-start.2 = (bf16[192,512]{1,0:T(8,128)(2,1)S(1)}, bf16[192,512]{1,0:T(8,128)(2,1)S(1)}, u32[]{:S(2)}, u32[]{:S(2)}) collective-permute-start(bf16[192,512]{1,0:T(8,128)(2,1)S(1)} %shard_map.137.refs_3_), channel_id=1, source_target_pairs={{0,2},{1,3},{2,0},{3,1},{4,6},{5,7},{6,4},{7,5},{8,10},{9,11},{10,... | collective-permute-start | bytes 589832 | tf_op jit(solution)/shard_map/ppermute | solution.py:371
  9.2 13.2 %collective-permute-start.3 = (bf16[192,512]{1,0:T(8,128)(2,1)S(1)}, bf16[192,512]{1,0:T(8,128)(2,1)S(1)}, u32[]{:S(2)}, u32[]{:S(2)}) collective-permute-start(bf16[192,512]{1,0:T(8,128)(2,1)S(1)} %shard_map.137.refs_3_), channel_id=1, source_target_pairs={{0,3},{1,0},{2,1},{3,2},{4,7},{5,4},{6,5},{7,6},{8,11},{9,8},{10,9... | collective-permute-start | bytes 589832 | tf_op jit(solution)/shard_map/ppermute | solution.py:371
  23.6 10.9 %collective-permute-start.7 = (bf16[192,512]{1,0:T(8,128)(2,1)}, bf16[192,512]{1,0:T(8,128)(2,1)S(1)}, u32[]{:S(2)}, u32[]{:S(2)}) collective-permute-start(bf16[192,512]{1,0:T(8,128)(2,1)} %shard_map.140.refs_18_), channel_id=1, source_target_pairs={{0,1},{1,2},{2,3},{3,0},{4,5},{5,6},{6,7},{7,4},{8,9},{9,10},{10,1... | collective-permute-start | bytes 589832 | tf_op jit(solution)/shard_map/ppermute | solution.py:371
  29.3 22.1 %collective-permute-start.4 = (bf16[3,192,256]{2,1,0:T(8,128)(2,1)}, bf16[3,192,256]{2,1,0:T(8,128)(2,1)}, u32[]{:S(2)}, u32[]{:S(2)}) collective-permute-start(bf16[3,192,256]{2,1,0:T(8,128)(2,1)} %get-tuple-element.57), channel_id=1, source_target_pairs={{0,8},{4,12},{8,0},{12,4},{16,24},{20,28},{24,16},{28,20},{1,9},{5... | collective-permute-start | bytes 884744 | tf_op jit(solution)/shard_map/ppermute | solution.py:368
  30.7 21.4 %collective-permute-start.5 = (bf16[3,192,256]{2,1,0:T(8,128)(2,1)}, bf16[3,192,256]{2,1,0:T(8,128)(2,1)}, u32[]{:S(2)}, u32[]{:S(2)}) collective-permute-start(bf16[3,192,256]{2,1,0:T(8,128)(2,1)} %get-tuple-element.58), channel_id=1, source_target_pairs={{0,16},{4,20},{8,24},{12,28},{16,0},{20,4},{24,8},{28,12},{1,17},{... | collective-permute-start | bytes 884744 | tf_op jit(solution)/shard_map/ppermute | solution.py:368
  32.9 12.3 %collective-permute-start.8 = (bf16[192,512]{1,0:T(8,128)(2,1)}, bf16[192,512]{1,0:T(8,128)(2,1)S(1)}, u32[]{:S(2)}, u32[]{:S(2)}) collective-permute-start(bf16[192,512]{1,0:T(8,128)(2,1)} %shard_map.140.refs_18_), channel_id=1, source_target_pairs={{0,2},{1,3},{2,0},{3,1},{4,6},{5,7},{6,4},{7,5},{8,10},{9,11},{10,... | collective-permute-start | bytes 589832 | tf_op jit(solution)/shard_map/ppermute | solution.py:371
  34.6 10.6 %collective-permute-start.9 = (bf16[192,512]{1,0:T(8,128)(2,1)}, bf16[192,512]{1,0:T(8,128)(2,1)S(1)}, u32[]{:S(2)}, u32[]{:S(2)}) collective-permute-start(bf16[192,512]{1,0:T(8,128)(2,1)} %shard_map.140.refs_18_), channel_id=1, source_target_pairs={{0,3},{1,0},{2,1},{3,2},{4,7},{5,4},{6,5},{7,6},{8,11},{9,8},{10,9... | collective-permute-start | bytes 589832 | tf_op jit(solution)/shard_map/ppermute | solution.py:371
  45.8 27.0 %collective-permute-start.12 = (bf16[192,512]{1,0:T(8,128)(2,1)S(1)}, bf16[192,512]{1,0:T(8,128)(2,1)S(1)}, u32[]{:S(2)}, u32[]{:S(2)}) collective-permute-start(bf16[192,512]{1,0:T(8,128)(2,1)S(1)} %shard_map.142.refs_19_), channel_id=1, source_target_pairs={{0,1},{1,2},{2,3},{3,0},{4,5},{5,6},{6,7},{7,4},{8,9},{9,10},{10,1... | collective-permute-start | bytes 589832 | tf_op jit(solution)/shard_map/ppermute | solution.py:371
  49.6 24.7 %collective-permute-start.13 = (bf16[192,512]{1,0:T(8,128)(2,1)S(1)}, bf16[192,512]{1,0:T(8,128)(2,1)S(1)}, u32[]{:S(2)}, u32[]{:S(2)}) collective-permute-start(bf16[192,512]{1,0:T(8,128)(2,1)S(1)} %shard_map.142.refs_19_), channel_id=1, source_target_pairs={{0,2},{1,3},{2,0},{3,1},{4,6},{5,7},{6,4},{7,5},{8,10},{9,11},{10,... | collective-permute-start | bytes 589832 | tf_op jit(solution)/shard_map/ppermute | solution.py:371
  51.3 24.5 %collective-permute-start.14 = (bf16[192,512]{1,0:T(8,128)(2,1)S(1)}, bf16[192,512]{1,0:T(8,128)(2,1)S(1)}, u32[]{:S(2)}, u32[]{:S(2)}) collective-permute-start(bf16[192,512]{1,0:T(8,128)(2,1)S(1)} %shard_map.142.refs_19_), channel_id=1, source_target_pairs={{0,3},{1,0},{2,1},{3,2},{4,7},{5,4},{6,5},{7,6},{8,11},{9,8},{10,9... | collective-permute-start | bytes 589832 | tf_op jit(solution)/shard_map/ppermute | solution.py:371
  52.1 25.1 %collective-permute-start.10 = (bf16[3,192,256]{2,1,0:T(8,128)(2,1)S(1)}, bf16[3,192,256]{2,1,0:T(8,128)(2,1)S(1)}, u32[]{:S(2)}, u32[]{:S(2)}) collective-permute-start(bf16[3,192,256]{2,1,0:T(8,128)(2,1)S(1)} %get-tuple-element.59.refs_17_), channel_id=1, source_target_pairs={{0,8},{4,12},{8,0},{12,4},{16,24},{20,28},{24,16},{28,20},{1,9},{5... | collective-permute-start | bytes 884744 | tf_op jit(solution)/shard_map/ppermute | solution.py:368
  52.7 26.0 %collective-permute-start.11 = (bf16[3,192,256]{2,1,0:T(8,128)(2,1)S(1)}, bf16[3,192,256]{2,1,0:T(8,128)(2,1)S(1)}, u32[]{:S(2)}, u32[]{:S(2)}) collective-permute-start(bf16[3,192,256]{2,1,0:T(8,128)(2,1)S(1)} %get-tuple-element.61), channel_id=1, source_target_pairs={{0,16},{4,20},{8,24},{12,28},{16,0},{20,4},{24,8},{28,12},{1,17},{... | collective-permute-start | bytes 884744 | tf_op jit(solution)/shard_map/ppermute | solution.py:368
  72.8 28.3 %collective-permute-start.17 = (bf16[4,96,512]{2,1,0:T(8,128)(2,1)S(1)}, bf16[4,96,512]{2,1,0:T(8,128)(2,1)S(1)}, u32[]{:S(2)}, u32[]{:S(2)}) collective-permute-start(bf16[4,96,512]{2,1,0:T(8,128)(2,1)S(1)} %get-tuple-element.71), channel_id=1, source_target_pairs={{0,8},{4,12},{8,0},{12,4},{16,24},{20,28},{24,16},{28,20},{1,9},{5... | collective-permute-start | bytes 1179656 | tf_op jit(solution)/shard_map/ppermute | solution.py:368
  74.3 26.8 %collective-permute-start.18 = (bf16[4,96,512]{2,1,0:T(8,128)(2,1)S(1)}, bf16[4,96,512]{2,1,0:T(8,128)(2,1)S(1)}, u32[]{:S(2)}, u32[]{:S(2)}) collective-permute-start(bf16[4,96,512]{2,1,0:T(8,128)(2,1)S(1)} %get-tuple-element.72), channel_id=1, source_target_pairs={{0,16},{4,20},{8,24},{12,28},{16,0},{20,4},{24,8},{28,12},{1,17},{... | collective-permute-start | bytes 1179656 | tf_op jit(solution)/shard_map/ppermute | solution.py:368
  75.9 25.3 %collective-permute-start.19 = (bf16[4,96,512]{2,1,0:T(8,128)(2,1)S(1)}, bf16[4,96,512]{2,1,0:T(8,128)(2,1)S(1)}, u32[]{:S(2)}, u32[]{:S(2)}) collective-permute-start(bf16[4,96,512]{2,1,0:T(8,128)(2,1)S(1)} %get-tuple-element.73), channel_id=1, source_target_pairs={{0,24},{4,28},{8,16},{12,20},{16,8},{20,12},{24,0},{28,4},{1,25},{... | collective-permute-start | bytes 1179656 | tf_op jit(solution)/shard_map/ppermute | solution.py:368
  77.2 29.0 %collective-permute-start.15 = (bf16[3,192,256]{2,1,0:T(8,128)(2,1)}, bf16[3,192,256]{2,1,0:T(8,128)(2,1)}, u32[]{:S(2)}, u32[]{:S(2)}) collective-permute-start(bf16[3,192,256]{2,1,0:T(8,128)(2,1)} %get-tuple-element.65.refs_19_), channel_id=1, source_target_pairs={{0,8},{4,12},{8,0},{12,4},{16,24},{20,28},{24,16},{28,20},{1,9},{5... | collective-permute-start | bytes 884744 | tf_op jit(solution)/shard_map/ppermute | solution.py:368
  78.7 29.5 %collective-permute-start.16 = (bf16[3,192,256]{2,1,0:T(8,128)(2,1)}, bf16[3,192,256]{2,1,0:T(8,128)(2,1)}, u32[]{:S(2)}, u32[]{:S(2)}) collective-permute-start(bf16[3,192,256]{2,1,0:T(8,128)(2,1)} %get-tuple-element.67), channel_id=1, source_target_pairs={{0,16},{4,20},{8,24},{12,28},{16,0},{20,4},{24,8},{28,12},{1,17},{... | collective-permute-start | bytes 884744 | tf_op jit(solution)/shard_map/ppermute | solution.py:368
  102.1 7.4 %collective-permute-start.23 = (bf16[96,512]{1,0:T(8,128)(2,1)S(1)}, bf16[96,512]{1,0:T(8,128)(2,1)S(1)}, u32[]{:S(2)}, u32[]{:S(2)}) collective-permute-start(bf16[96,512]{1,0:T(8,128)(2,1)S(1)} %get-tuple-element.86), channel_id=1, source_target_pairs={{0,1},{1,2},{2,3},{3,0},{4,5},{5,6},{6,7},{7,4},{8,9},{9,10},{10,1... | collective-permute-start | bytes 294920 | tf_op jit(solution)/shard_map/ppermute | solution.py:371
  104.7 24.7 %collective-permute-start.20 = (bf16[4,96,512]{2,1,0:T(8,128)(2,1)}, bf16[4,96,512]{2,1,0:T(8,128)(2,1)S(1)}, u32[]{:S(2)}, u32[]{:S(2)}) collective-permute-start(bf16[4,96,512]{2,1,0:T(8,128)(2,1)} %copy-done.21), channel_id=1, source_target_pairs={{0,8},{4,12},{8,0},{12,4},{16,24},{20,28},{24,16},{28,20},{1,9},{5... | collective-permute-start | bytes 1179656 | tf_op jit(solution)/shard_map/ppermute | solution.py:368
  105.3 24.1 %collective-permute-start.21 = (bf16[4,96,512]{2,1,0:T(8,128)(2,1)}, bf16[4,96,512]{2,1,0:T(8,128)(2,1)S(1)}, u32[]{:S(2)}, u32[]{:S(2)}) collective-permute-start(bf16[4,96,512]{2,1,0:T(8,128)(2,1)} %copy-done.20), channel_id=1, source_target_pairs={{0,16},{4,20},{8,24},{12,28},{16,0},{20,4},{24,8},{28,12},{1,17},{... | collective-permute-start | bytes 1179656 | tf_op jit(solution)/shard_map/ppermute | solution.py:368
  106.2 23.2 %collective-permute-start.22 = (bf16[4,96,512]{2,1,0:T(8,128)(2,1)}, bf16[4,96,512]{2,1,0:T(8,128)(2,1)S(1)}, u32[]{:S(2)}, u32[]{:S(2)}) collective-permute-start(bf16[4,96,512]{2,1,0:T(8,128)(2,1)} %copy-done.19), channel_id=1, source_target_pairs={{0,24},{4,28},{8,16},{12,20},{16,8},{20,12},{24,0},{28,4},{1,25},{... | collective-permute-start | bytes 1179656 | tf_op jit(solution)/shard_map/ppermute | solution.py:368
  108.2 21.0 %collective-permute-start.24 = (bf16[96,512]{1,0:T(8,128)(2,1)}, bf16[96,512]{1,0:T(8,128)(2,1)S(1)}, u32[]{:S(2)}, u32[]{:S(2)}) collective-permute-start(bf16[96,512]{1,0:T(8,128)(2,1)} %get-tuple-element.87), channel_id=1, source_target_pairs={{0,2},{1,3},{2,0},{3,1},{4,6},{5,7},{6,4},{7,5},{8,10},{9,11},{10,... | collective-permute-start | bytes 294920 | tf_op jit(solution)/shard_map/ppermute | solution.py:371
  109.5 19.8 %collective-permute-start.25 = (bf16[96,512]{1,0:T(8,128)(2,1)}, bf16[96,512]{1,0:T(8,128)(2,1)S(1)}, u32[]{:S(2)}, u32[]{:S(2)}) collective-permute-start(bf16[96,512]{1,0:T(8,128)(2,1)} %get-tuple-element.88), channel_id=1, source_target_pairs={{0,3},{1,0},{2,1},{3,2},{4,7},{5,4},{6,5},{7,6},{8,11},{9,8},{10,9... | collective-permute-start | bytes 294920 | tf_op jit(solution)/shard_map/ppermute | solution.py:371
  141.0 36.9 %collective-permute-start.26 = (bf16[768,1536]{1,0:T(8,128)(2,1)}, bf16[768,1536]{1,0:T(8,128)(2,1)}, u32[]{:S(2)}, u32[]{:S(2)}) collective-permute-start(bf16[768,1536]{1,0:T(8,128)(2,1)} %shard_map.150.refs_5_.refs_4_), channel_id=1, source_target_pairs={{0,4},{4,0},{8,12},{12,8},{16,20},{20,16},{24,28},{28,24},{1,5},{5... | collective-permute-start | bytes 7077896 | tf_op jit(solution)/shard_map/ppermute | solution.py:365
  141.0 36.8 %collective-permute-start.27 = (bf16[768,768]{1,0:T(8,128)(2,1)}, bf16[768,768]{1,0:T(8,128)(2,1)}, u32[]{:S(2)}, u32[]{:S(2)}) collective-permute-start(bf16[768,768]{1,0:T(8,128)(2,1)} %get-tuple-element.90), channel_id=1, source_target_pairs={{0,4},{4,0},{8,12},{12,8},{16,20},{20,16},{24,28},{28,24},{1,5},{5... | collective-permute-start | bytes 3538952 | tf_op jit(solution)/shard_map/ppermute | solution.py:365
  142.0 6.7 %collective-permute-start.46 = (bf16[96,512]{1,0:T(8,128)(2,1)S(1)}, bf16[96,512]{1,0:T(8,128)(2,1)S(1)}, u32[]{:S(2)}, u32[]{:S(2)}) collective-permute-start(bf16[96,512]{1,0:T(8,128)(2,1)S(1)} %shard_map.149.refs_8_), channel_id=1, source_target_pairs={{0,16},{4,20},{8,24},{12,28},{16,0},{20,4},{24,8},{28,12},{1,17},{... | collective-permute-start | bytes 294920 | tf_op jit(solution)/shard_map/ppermute | solution.py:368
  142.8 7.9 %collective-permute-start.47 = (bf16[96,512]{1,0:T(8,128)(2,1)S(1)}, bf16[96,512]{1,0:T(8,128)(2,1)S(1)}, u32[]{:S(2)}, u32[]{:S(2)}) collective-permute-start(bf16[96,512]{1,0:T(8,128)(2,1)S(1)} %shard_map.149.refs_8_), channel_id=1, source_target_pairs={{0,24},{4,28},{8,16},{12,20},{16,8},{20,12},{24,0},{28,4},{1,25},{... | collective-permute-start | bytes 294920 | tf_op jit(solution)/shard_map/ppermute | solution.py:368
  146.9 7.1 %collective-permute-start.28 = (bf16[96,512]{1,0:T(8,128)(2,1)S(1)}, bf16[96,512]{1,0:T(8,128)(2,1)S(1)}, u32[]{:S(2)}, u32[]{:S(2)}) collective-permute-start(bf16[96,512]{1,0:T(8,128)(2,1)S(1)} %get-tuple-element.91), channel_id=1, source_target_pairs={{0,1},{1,2},{2,3},{3,0},{4,5},{5,6},{6,7},{7,4},{8,9},{9,10},{10,1... | collective-permute-start | bytes 294920 | tf_op jit(solution)/shard_map/ppermute | solution.py:371
  148.7 7.8 %collective-permute-start.29 = (bf16[96,512]{1,0:T(8,128)(2,1)S(1)}, bf16[96,512]{1,0:T(8,128)(2,1)S(1)}, u32[]{:S(2)}, u32[]{:S(2)}) collective-permute-start(bf16[96,512]{1,0:T(8,128)(2,1)S(1)} %get-tuple-element.92), channel_id=1, source_target_pairs={{0,2},{1,3},{2,0},{3,1},{4,6},{5,7},{6,4},{7,5},{8,10},{9,11},{10,... | collective-permute-start | bytes 294920 | tf_op jit(solution)/shard_map/ppermute | solution.py:371
  150.6 6.2 %collective-permute-start.30 = (bf16[96,512]{1,0:T(8,128)(2,1)S(1)}, bf16[96,512]{1,0:T(8,128)(2,1)S(1)}, u32[]{:S(2)}, u32[]{:S(2)}) collective-permute-start(bf16[96,512]{1,0:T(8,128)(2,1)S(1)} %get-tuple-element.93), channel_id=1, source_target_pairs={{0,3},{1,0},{2,1},{3,2},{4,7},{5,4},{6,5},{7,6},{8,11},{9,8},{10,9... | collective-permute-start | bytes 294920 | tf_op jit(solution)/shard_map/ppermute | solution.py:371
  154.0 12.3 %collective-permute-start.31 = (bf16[4,96,512]{2,1,0:T(8,128)(2,1)}, bf16[4,96,512]{2,1,0:T(8,128)(2,1)S(1)}, u32[]{:S(2)}, u32[]{:S(2)}) collective-permute-start(bf16[4,96,512]{2,1,0:T(8,128)(2,1)} %get-tuple-element.95), channel_id=1, source_target_pairs={{0,8},{4,12},{8,0},{12,4},{16,24},{20,28},{24,16},{28,20},{1,9},{5... | collective-permute-start | bytes 1179656 | tf_op jit(solution)/shard_map/ppermute | solution.py:368
  156.6 15.8 %collective-permute-start.32 = (bf16[4,96,512]{2,1,0:T(8,128)(2,1)}, bf16[4,96,512]{2,1,0:T(8,128)(2,1)S(1)}, u32[]{:S(2)}, u32[]{:S(2)}) collective-permute-start(bf16[4,96,512]{2,1,0:T(8,128)(2,1)} %get-tuple-element.96), channel_id=1, source_target_pairs={{0,16},{4,20},{8,24},{12,28},{16,0},{20,4},{24,8},{28,12},{1,17},{... | collective-permute-start | bytes 1179656 | tf_op jit(solution)/shard_map/ppermute | solution.py:368
  156.8 18.0 %collective-permute-start.33 = (bf16[4,96,512]{2,1,0:T(8,128)(2,1)}, bf16[4,96,512]{2,1,0:T(8,128)(2,1)}, u32[]{:S(2)}, u32[]{:S(2)}) collective-permute-start(bf16[4,96,512]{2,1,0:T(8,128)(2,1)} %get-tuple-element.97), channel_id=1, source_target_pairs={{0,24},{4,28},{8,16},{12,20},{16,8},{20,12},{24,0},{28,4},{1,25},{... | collective-permute-start | bytes 1179656 | tf_op jit(solution)/shard_map/ppermute | solution.py:368
  166.2 40.3 %collective-permute-start.48 = (bf16[4,96,512]{2,1,0:T(8,128)(2,1)S(1)}, bf16[4,96,512]{2,1,0:T(8,128)(2,1)S(1)}, u32[]{:S(2)}, u32[]{:S(2)}) collective-permute-start(bf16[4,96,512]{2,1,0:T(8,128)(2,1)S(1)} %pad_maximum_fusion.2.mine), channel_id=1, source_target_pairs={{0,4},{4,0},{8,12},{12,8},{16,20},{20,16},{24,28},{28,24},{1,5},{5... | collective-permute-start | bytes 1179656 | tf_op jit(solution)/shard_map/ppermute | solution.py:365
  172.3 20.5 %collective-permute-start.41 = (bf16[96,512]{1,0:T(8,128)(2,1)S(1)}, bf16[96,512]{1,0:T(8,128)(2,1)S(1)}, u32[]{:S(2)}, u32[]{:S(2)}) collective-permute-start(bf16[96,512]{1,0:T(8,128)(2,1)S(1)} %shard_map.151.refs_14_), channel_id=1, source_target_pairs={{0,8},{4,12},{8,0},{12,4},{16,24},{20,28},{24,16},{28,20},{1,9},{5... | collective-permute-start | bytes 294920 | tf_op jit(solution)/shard_map/ppermute | solution.py:368
  174.9 18.0 %collective-permute-start.42 = (bf16[96,512]{1,0:T(8,128)(2,1)S(1)}, bf16[96,512]{1,0:T(8,128)(2,1)S(1)}, u32[]{:S(2)}, u32[]{:S(2)}) collective-permute-start(bf16[96,512]{1,0:T(8,128)(2,1)S(1)} %shard_map.151.refs_14_), channel_id=1, source_target_pairs={{0,16},{4,20},{8,24},{12,28},{16,0},{20,4},{24,8},{28,12},{1,17},{... | collective-permute-start | bytes 294920 | tf_op jit(solution)/shard_map/ppermute | solution.py:368
  177.8 15.0 %collective-permute-start.43 = (bf16[96,512]{1,0:T(8,128)(2,1)S(1)}, bf16[96,512]{1,0:T(8,128)(2,1)S(1)}, u32[]{:S(2)}, u32[]{:S(2)}) collective-permute-start(bf16[96,512]{1,0:T(8,128)(2,1)S(1)} %shard_map.151.refs_14_), channel_id=1, source_target_pairs={{0,24},{4,28},{8,16},{12,20},{16,8},{20,12},{24,0},{28,4},{1,25},{... | collective-permute-start | bytes 294920 | tf_op jit(solution)/shard_map/ppermute | solution.py:368
  192.9 14.1 %collective-permute-start.44 = (bf16[4,96,512]{2,1,0:T(8,128)(2,1)S(1)}, bf16[4,96,512]{2,1,0:T(8,128)(2,1)S(1)}, u32[]{:S(2)}, u32[]{:S(2)}) collective-permute-start(bf16[4,96,512]{2,1,0:T(8,128)(2,1)S(1)} %pad_maximum_fusion.1.mine), channel_id=1, source_target_pairs={{0,4},{4,0},{8,12},{12,8},{16,20},{20,16},{24,28},{28,24},{1,5},{5... | collective-permute-start | bytes 1179656 | tf_op jit(solution)/shard_map/ppermute | solution.py:365
  195.5 5.6 %collective-permute-start.51 = (f32[32,768]{1,0:T(8,128)S(1)}, f32[32,768]{1,0:T(8,128)S(1)}, u32[]{:S(2)}, u32[]{:S(2)}) collective-permute-start(f32[32,768]{1,0:T(8,128)S(1)} %pad_maximum_fusion.3), channel_id=1, source_target_pairs={{0,8},{4,12},{8,0},{12,4},{16,24},{20,28},{24,16},{28,20},{1,9},{5... | collective-permute-start | bytes 294920 | tf_op jit(solution)/shard_map/ppermute | solution.py:368
  198.9 7.6 %collective-permute-start.34 = (bf16[96,512]{1,0:T(8,128)(2,1)S(1)}, bf16[96,512]{1,0:T(8,128)(2,1)S(1)}, u32[]{:S(2)}, u32[]{:S(2)}) collective-permute-start(bf16[96,512]{1,0:T(8,128)(2,1)S(1)} %get-tuple-element.101), channel_id=1, source_target_pairs={{0,1},{1,2},{2,3},{3,0},{4,5},{5,6},{6,7},{7,4},{8,9},{9,10},{10,1... | collective-permute-start | bytes 294920 | tf_op jit(solution)/shard_map/ppermute | solution.py:371
  201.1 13.8 %collective-permute-start.35 = (bf16[96,512]{1,0:T(8,128)(2,1)S(1)}, bf16[96,512]{1,0:T(8,128)(2,1)S(1)}, u32[]{:S(2)}, u32[]{:S(2)}) collective-permute-start(bf16[96,512]{1,0:T(8,128)(2,1)S(1)} %get-tuple-element.102), channel_id=1, source_target_pairs={{0,2},{1,3},{2,0},{3,1},{4,6},{5,7},{6,4},{7,5},{8,10},{9,11},{10,... | collective-permute-start | bytes 294920 | tf_op jit(solution)/shard_map/ppermute | solution.py:371
  203.0 11.9 %collective-permute-start.36 = (bf16[96,512]{1,0:T(8,128)(2,1)S(1)}, bf16[96,512]{1,0:T(8,128)(2,1)S(1)}, u32[]{:S(2)}, u32[]{:S(2)}) collective-permute-start(bf16[96,512]{1,0:T(8,128)(2,1)S(1)} %get-tuple-element.103), channel_id=1, source_target_pairs={{0,3},{1,0},{2,1},{3,2},{4,7},{5,4},{6,5},{7,6},{8,11},{9,8},{10,9... | collective-permute-start | bytes 294920 | tf_op jit(solution)/shard_map/ppermute | solution.py:371
  206.6 12.2 %collective-permute-start.53 = (f32[32,768]{1,0:T(8,128)S(1)}, f32[32,768]{1,0:T(8,128)S(1)}, u32[]{:S(2)}, u32[]{:S(2)}) collective-permute-start(f32[32,768]{1,0:T(8,128)S(1)} %add_add_fusion), channel_id=1, source_target_pairs={{0,2},{1,3},{2,0},{3,1},{4,6},{5,7},{6,4},{7,5},{8,10},{9,11},{10,... | collective-permute-start | bytes 294920 | tf_op jit(solution)/shard_map/ppermute | solution.py:371
  206.6 13.9 %collective-permute-start.54 = (f32[32,768]{1,0:T(8,128)S(1)}, f32[32,768]{1,0:T(8,128)S(1)}, u32[]{:S(2)}, u32[]{:S(2)}) collective-permute-start(f32[32,768]{1,0:T(8,128)S(1)} %add_add_fusion), channel_id=1, source_target_pairs={{0,1},{1,2},{2,3},{3,0},{4,5},{5,6},{6,7},{7,4},{8,9},{9,10},{10,1... | collective-permute-start | bytes 294920 | tf_op jit(solution)/shard_map/ppermute | solution.py:371
  207.0 13.5 %collective-permute-start.55 = (f32[32,768]{1,0:T(8,128)S(1)}, f32[32,768]{1,0:T(8,128)S(1)}, u32[]{:S(2)}, u32[]{:S(2)}) collective-permute-start(f32[32,768]{1,0:T(8,128)S(1)} %add_add_fusion), channel_id=1, source_target_pairs={{0,3},{1,0},{2,1},{3,2},{4,7},{5,4},{6,5},{7,6},{8,11},{9,8},{10,9... | collective-permute-start | bytes 294920 | tf_op jit(solution)/shard_map/ppermute | solution.py:371
  (42 other events, 429.1 us)

commit v3 on v2

--- a/solution.py
+++ b/solution.py
@@ -88,8 +88,8 @@
     z_parts, rest = rest[3 : 2 + red_size], rest[2 + red_size :]
     xv, yg, frames_own, frames_sib, cot_own, cot_sib, live, hats, fwd, inv = rest[:10]
     rest = rest[10 + 2 * has_out :]
-    out_own, out_sib, grads, gh, w_out, sums = rest[0], rest[1], rest[2:6], *rest[6:9]
-    scaled, scaled_t, w, grad, sem_w, sem_s, sem_t, sem_o, sem_g = rest[9:]
+    outs_hbm, grads, gh_hbm, w_out, sums = rest[:2], rest[2:6], *rest[6:9]
+    scaled, scaled_t, w, grad, out_own, out_sib, gh, sem_w, sem_s, sem_t, sem_o, sem_g = rest[9:]
     core, quarter, red, parity = idx[0], idx[1], idx[2], idx[3]
     n_rows, model_width = scaled.shape
     width = w.shape[1] // 2
@@ -120,8 +120,19 @@
     get_scaled_t.start()
     for copy in copies:
         copy.wait()
-    put_w = pltpu.make_async_copy(w, w_out, sem_o)
-    put_w.start()
+    near_columns = pl.ds(start, width)
+    puts = [
+        pltpu.make_async_copy(src, dst, sem_o.at[n])
+        for n, (src, dst) in enumerate(
+            (
+                (w, w_out),
+                (out_own, outs_hbm[0].at[:, near_columns]),
+                (out_sib, outs_hbm[1].at[:, near_columns]),
+                (gh, gh_hbm),
+            )
+        )
+    ]
+    puts[0].start()
     get_scaled.wait()
 
     rows = GROUP * length
@@ -202,30 +213,30 @@
                     running[group] = None
         turn += 1
 
+    for put in puts[1:]:
+        put.start()
     get_scaled_t.wait()
     sends = []
     for b in range(red_size):
         grad[pl.ds(b * block, block), :] = jnp.dot(
             scaled_t[pl.ds(b * block, block), :], gh[...], preferred_element_type=jnp.float32
         ).astype(jnp.bfloat16)
-        slot = lax.rem(b + red_size - red, red_size)
         for r in range(4):
             row = pl.multiple_of(b * block + lax.bitwise_xor(quarter, r) * part, 16)
             copy = pltpu.make_async_copy(
-                grad.at[pl.ds(row, part), :], grads[r].at[slot], sem_g.at[len(sends)]
+                grad.at[pl.ds(row, part), :], grads[r].at[b], sem_g.at[len(sends)]
             )
             copy.start()
             sends.append(copy)
     for copy in sends:
         copy.wait()
-    put_w.wait()
+    for put in puts:
+        put.wait()
 
 
 def plane_kernel(*refs):
-    parts, outs = refs[:4], refs[4:]
-    for s, out in enumerate(outs):
-        terms = [p[s].astype(jnp.float32) for p in parts]
-        out[...] = tree_sum(terms).astype(out.dtype)
+    out = refs[4]
+    out[...] = tree_sum([p[...].astype(jnp.float32) for p in refs[:4]]).astype(out.dtype)
 
 
 def grad_scaled_kernel(n_chunks, *refs):
@@ -277,20 +288,26 @@
     frame_out[...] = (res * alive).astype(frame_out.dtype)
 
 
+def stack_kernel(*refs):
+    for r in range(4):
+        refs[4][r] = refs[r][...]
+
+
 def place_kernel(has_out, idx, mine, sib, *rest):
     out = rest[has_out]
     quarter = idx[1]
-    part = mine.shape[1]
-    side = pl.program_id(1)
+    part = mine.shape[2]
+    chunk, which, side = pl.program_id(0), pl.program_id(1), pl.program_id(2)
     width = out.shape[1]
 
     def write(src):
         for r in range(4):
             q = lax.bitwise_xor(r, quarter)
             row = pl.ds(pl.multiple_of(q * part, 16), part)
-            out[row, :] = src[r, :, pl.ds(pl.multiple_of(side * width, 128), width)].astype(jnp.float32)
-
-    own = pl.program_id(0) == idx[0]
+            column = pl.ds(pl.multiple_of(side * width, 128), width)
+            out[row, :] = src[r, chunk, :, column].astype(jnp.float32)
+
+    own = which == idx[0]
     pl.when(own)(lambda: write(mine))
     pl.when(jnp.logical_not(own))(lambda: write(sib))
 
@@ -310,8 +327,10 @@
 
 
 def line_kernel(n, root, *refs):
-    terms = [part[...].astype(jnp.float32) for part in refs[:n]]
-    refs[n][...] = (tree_sum(terms) * root[0]).astype(refs[n].dtype)
+    parts, out = refs[:n], refs[n]
+    for k, part in enumerate(parts):
+        terms = [part[b].astype(jnp.float32) for b in range(part.shape[0])]
+        out[k] = (tree_sum(terms) * root[0]).astype(out.dtype)
 
 
 def ordered(body, n_in, n_after):
@@ -335,8 +354,8 @@
     return pltpu.CompilerParams(vmem_limit_bytes=VMEM_LIMIT)
 
 
-def cost(flops, moved, transcendentals=0):
-    return pl.CostEstimate(flops=flops, bytes_accessed=moved, transcendentals=transcendentals)
+LONG = pl.CostEstimate(flops=10**11, bytes_accessed=2 * 10**8, transcendentals=0)
+SHORT = pl.CostEstimate(flops=10**6, bytes_accessed=10**6, transcendentals=0)
 
 
 ANY = pl.BlockSpec(memory_space=pltpu.HBM)
@@ -403,7 +422,7 @@
             ),
             out_shape=jax.ShapeDtypeStruct((block // 2, 2 * width), jnp.bfloat16),
             compiler_params=params(),
-            cost_estimate=cost(0, 4 * block * width),
+            cost_estimate=LONG,
         )(idx, w_in, w_in, *deps)
         return mine, [shift_red(mine, s) for s in range(1, red_size)]
 
@@ -418,7 +437,7 @@
             out_specs=[whole(shape)] * 2,
             out_shape=[jax.ShapeDtypeStruct(shape, jnp.bfloat16)] * 2,
             compiler_params=params(),
-            cost_estimate=cost(0, 4 * n * block * width),
+            cost_estimate=LONG,
         )(*z_parts, *deps)
 
     def second_sends(packed):
@@ -431,12 +450,13 @@
     tile = 256
     tiles = own_rows // tile
     scaled, scaled_t = pl.pallas_call(
-        ordered(scale_kernel, 3, 1),
+        ordered(scale_kernel, 3, 2),
         grid=(2 * tiles,),
         in_specs=[
             pl.BlockSpec((tile, model_width), lambda i: (jnp.minimum(i, tiles - 1), 0)),
             pl.BlockSpec((tile, model_width), lambda i: (jnp.maximum(i - tiles, 0), 0)),
             whole((1, model_width)),
+            ANY,
             ANY,
         ],
         out_specs=[
@@ -448,8 +468,8 @@
             pltpu.HBM((model_width, n_rows), jnp.bfloat16),
         ],
         compiler_params=params(),
-        cost_estimate=cost(10 * n_rows * model_width, 6 * n_rows * model_width),
-    )(flat_frames, sib_frames, gain.reshape(1, model_width), mine)
+        cost_estimate=LONG,
+    )(flat_frames, sib_frames, gain.reshape(1, model_width), mine, sib_cot)
 
     packed = [second_pack(z[0], scaled)]
     near = [second_sends(packed[0])]
@@ -497,7 +517,6 @@
         n_in = len(operands) + 1
         operands += deps
         in_specs += [ANY] * len(deps)
-        near_strip = pl.BlockSpec((own_rows, width), lambda i, idx: (0, near_column))
         return pl.pallas_call(
             ordered(
                 functools.partial(chunk_kernel, red_size, length, start, 1 if aliases else 0),
@@ -508,18 +527,19 @@
                 num_scalar_prefetch=1,
                 grid=(1,),
                 in_specs=in_specs,
-                out_specs=[near_strip, near_strip]
-                + [ANY] * 4
-                + [whole((n_rows, 2 * width)), ANY, whole((3 * half, width))],
+                out_specs=[ANY] * 8 + [whole((3 * half, width))],
                 scratch_shapes=[
                     pltpu.VMEM((n_rows, model_width), jnp.bfloat16),
                     pltpu.VMEM((model_width, n_rows), jnp.bfloat16),
                     pltpu.VMEM((model_width, 2 * width), jnp.bfloat16),
                     pltpu.VMEM((model_width, 2 * width), jnp.bfloat16),
+                    pltpu.VMEM((own_rows, width), jnp.bfloat16),
+                    pltpu.VMEM((own_rows, width), jnp.bfloat16),
+                    pltpu.VMEM((n_rows, 2 * width), jnp.bfloat16),
                     pltpu.SemaphoreType.DMA((3 * red_size - 1,)),
                     pltpu.SemaphoreType.DMA,
                     pltpu.SemaphoreType.DMA,
-                    pltpu.SemaphoreType.DMA,
+                    pltpu.SemaphoreType.DMA((4,)),
                     pltpu.SemaphoreType.DMA((4 * red_size,)),
                 ],
             ),
@@ -533,9 +553,7 @@
             ],
             input_output_aliases=aliases,
             compiler_params=params(),
-            cost_estimate=cost(
-                8 * n_rows * model_width * width + 24 * 256 * n_rows * width, 1 << 24, 4 * n_rows * width
-            ),
+            cost_estimate=LONG,
         )(idx, *operands)
 
     def add_plane(parts, *deps):
@@ -544,39 +562,49 @@
             ordered(plane_kernel, 4, len(deps)),
             grid=(1,),
             in_specs=[whole(shape)] * 4 + [ANY] * len(deps),
-            out_specs=[whole(shape[1:])] * red_size,
-            out_shape=[jax.ShapeDtypeStruct(shape[1:], jnp.bfloat16)] * red_size,
+            out_specs=whole(shape),
+            out_shape=jax.ShapeDtypeStruct(shape, jnp.bfloat16),
             compiler_params=params(),
-            cost_estimate=cost(4 * parts[0].size, 10 * parts[0].size),
+            cost_estimate=LONG,
         )(*parts, *deps)
 
     def send_plane(grads):
         return [grads[0], *(to_quarter(grads[r], r) for r in range(1, 4))]
 
     def send_line(parts):
-        return [parts[0], *(shift_red(parts[s], s) for s in range(1, red_size))]
+        return lax.all_to_all(parts, "red", 0, 0, tiled=True)
 
     def add_line(parts, *deps):
         shape = parts[0].shape
+        out_shape = (len(parts), *shape[1:])
         kind = jnp.bfloat16 if dp_size <= 8 else jnp.float32
         owned = pl.pallas_call(
-            ordered(functools.partial(line_kernel, red_size), 1 + red_size, len(deps)),
+            ordered(functools.partial(line_kernel, len(parts)), 1 + len(parts), len(deps)),
             grid=(1,),
             in_specs=[pl.BlockSpec(memory_space=pltpu.SMEM)]
-            + [whole(shape)] * red_size
+            + [whole(shape)] * len(parts)
             + [ANY] * len(deps),
-            out_specs=whole(shape),
-            out_shape=jax.ShapeDtypeStruct(shape, kind),
+            out_specs=whole(out_shape),
+            out_shape=jax.ShapeDtypeStruct(out_shape, kind),
             compiler_params=params(),
-            cost_estimate=cost(8 * parts[0].size, 10 * parts[0].size),
+            cost_estimate=LONG,
         )(root.reshape(1), *parts, *deps)
         return other_groups(owned).astype(jnp.bfloat16)
 
-    def spread(owned):
-        return [owned, *(to_quarter(owned, r) for r in range(1, 4))]
-
-    def place(chunk, mine, sib, grad_out):
-        start, width = CHUNKS[chunk]
+    def spread(owned, *deps):
+        parts = [owned, *(to_quarter(owned, r) for r in range(1, 4))]
+        return pl.pallas_call(
+            ordered(stack_kernel, 4, len(deps)),
+            grid=(1,),
+            in_specs=[whole(owned.shape)] * 4 + [ANY] * len(deps),
+            out_specs=whole((4, *owned.shape)),
+            out_shape=jax.ShapeDtypeStruct((4, *owned.shape), owned.dtype),
+            compiler_params=params(),
+            cost_estimate=SHORT,
+        )(*parts, *deps)
+
+    def place(first, mine, sib, grad_out, estimate):
+        start, width = CHUNKS[first]
         near_column, columns = start // width, side // width
         has_out = 0 if grad_out is None else 1
         operands = [mine, sib] + ([grad_out] if has_out else [])
@@ -584,21 +612,26 @@
             functools.partial(place_kernel, has_out),
             grid_spec=pltpu.PrefetchScalarGridSpec(
                 num_scalar_prefetch=1,
-                grid=(2, 2),
+                grid=(mine.shape[1], 2, 2),
                 in_specs=[whole(mine.shape)] * 2 + [ANY] * has_out,
                 out_specs=pl.BlockSpec(
                     (block, width),
-                    lambda c, h, idx: (0, near_column + c * columns + h * 2 * columns),
+                    lambda k, c, h, idx: (0, near_column + k + c * columns + h * 2 * columns),
                 ),
             ),
             out_shape=jax.ShapeDtypeStruct((block, 2 * model_width), jnp.float32),
             input_output_aliases={3: 0} if has_out else {},
             compiler_params=params(),
-            cost_estimate=cost(0, 20 * block * width),
+            cost_estimate=estimate,
         )(idx, *operands)
 
     outs, ghs, ws, sums = None, [], [], []
-    on_way, planes, lines = [], [], []
+    on_way, planes, after_plane = [], [], []
+
+    def step_plane(chunk, *deps):
+        after_plane.append(add_plane(on_way[chunk], *deps))
+        planes.append(send_line(after_plane[-1]))
+
     for chunk in range(n_chunks):
         deps = []
         if chunk == 0 and n_chunks > 1:
@@ -608,8 +641,8 @@
             near.append(second_sends(packed[-1]))
             deps += [packed[-1][0]]
         if chunk >= 2:
-            planes.append(send_line(add_plane(on_way[chunk - 2], sums[-1])))
-            deps += [planes[-1][0]]
+            step_plane(chunk - 2, sums[-1])
+            deps += [after_plane[-1]]
         *outs, g0, g1, g2, g3, gh, w, tap_sums = middle(chunk, outs, deps)
         on_way.append(send_plane([g0, g1, g2, g3]))
         ghs.append(gh)
@@ -617,7 +650,7 @@
         sums.append(tap_sums)
 
     out_other = to_core(outs[1])
-    step = GROUP * length
+    step = own_rows // 2
     steps = own_rows // step
     row_spec = pl.BlockSpec((step, model_width), lambda i, *_: (i, 0))
     gh_specs = [pl.BlockSpec((step, gh.shape[1]), lambda i, *_: (i, 0)) for gh in ghs]
@@ -626,27 +659,23 @@
     flops = 2 * own_rows * model_width * model_width
     deps = [sums[-1]]
     while len(planes) < n_chunks - 1:
-        planes.append(send_line(add_plane(on_way[len(planes)], sums[-1])))
-        deps.append(planes[-1][0])
-    while len(lines) < n_chunks - 2:
-        lines.append(add_line(planes[len(lines)], sums[-1]))
-        deps.append(lines[-1])
+        step_plane(len(planes), sums[-1])
+        deps.append(after_plane[-1])
     grad_scaled_sib = pl.pallas_call(
         ordered(functools.partial(grad_scaled_kernel, n_chunks), 2 * n_chunks, len(deps)),
-        grid=(steps,),
-        in_specs=sib_specs + w_specs + [ANY] * len(deps),
-        out_specs=row_spec,
+        grid=(1,),
+        in_specs=[pl.BlockSpec((own_rows, gh.shape[1]), lambda i: (1, 0)) for gh in ghs]
+        + w_specs
+        + [ANY] * len(deps),
+        out_specs=whole((own_rows, model_width)),
         out_shape=jax.ShapeDtypeStruct((own_rows, model_width), jnp.bfloat16),
         compiler_params=params(),
-        cost_estimate=cost(flops, 10 << 20),
+        cost_estimate=LONG,
     )(*ghs, *ws, *deps)
     other = to_core(grad_scaled_sib)
-    deps = []
-    while len(lines) < n_chunks - 1:
-        lines.append(add_line(planes[len(lines)], grad_scaled_sib))
-        deps.append(lines[-1])
-    planes.append(send_line(add_plane(on_way[-1], grad_scaled_sib)))
-    deps.append(planes[-1][0])
+    early = add_line(planes, grad_scaled_sib)
+    step_plane(n_chunks - 1, early)
+    deps = [after_plane[-1]]
     side_spec = pl.BlockSpec((step, side), lambda i, *_: (i, 0))
     module_output, frame_gradient, gain_part = pl.pallas_call(
         ordered(functools.partial(frame_kernel, n_chunks), 8 + 2 * n_chunks, len(deps)),
@@ -673,7 +702,7 @@
             jax.ShapeDtypeStruct((8, model_width), jnp.float32),
         ],
         compiler_params=params(),
-        cost_estimate=cost(2 * flops, 30 << 20),
+        cost_estimate=LONG,
     )(
         idx,
         flat_frames,
@@ -688,12 +717,10 @@
         *deps,
     )
 
-    while len(lines) < n_chunks:
-        lines.append(add_line(planes[len(lines)], gain_part))
-    grad_out = None
-    for chunk in range(n_chunks):
-        mine = jnp.stack(spread(lines[chunk]))
-        grad_out = place(chunk, mine, to_core(mine), grad_out)
+    mine = spread(early)
+    grad_out = place(0, mine, to_core(mine), None, LONG)
+    mine = spread(add_line(planes[-1:]), grad_out)
+    grad_out = place(n_chunks - 1, mine, to_core(mine), grad_out, SHORT)
 
     order = sorted(range(n_chunks), key=lambda c: CHUNKS[c][0])
     tap_part = jnp.dot(
@@ -702,21 +729,25 @@
         precision=lax.Precision.HIGHEST,
     )
     gain_part = jnp.sum(gain_part, axis=0).reshape(2, side)
-    kept = lax.dynamic_index_in_dim(gain_part, core, 0)
-    sent = lax.dynamic_index_in_dim(gain_part, 1 - core, 0)
-    small = jnp.concatenate([tap_part, kept + to_core(sent)], axis=0)
-    small = tree_sum([small, *(to_quarter(small, r) for r in range(1, 4))])
-    small = tree_sum([small, *(shift_red(small, s) for s in range(1, red_size))])
+    small = jnp.concatenate([tap_part, gain_part], axis=0)
+    for r in (1, 2):
+        small = small + to_quarter(small, r)
+    bit = 1
+    while bit < red_size:
+        small = small + lax.ppermute(small, "red", [(i, i ^ bit) for i in range(red_size)])
+        bit *= 2
     small = other_groups(small) * root
     both = to_core(small)
     first = core == 0
-    small = jnp.concatenate([jnp.where(first, small, both), jnp.where(first, both, small)], axis=1)
+    left, right = jnp.where(first, small, both), jnp.where(first, both, small)
+    tap_total = jnp.concatenate([left[:taps], right[:taps]], axis=1)
+    gain_total = (small[taps:] + both[taps:]).reshape(model_width)
     return (
         module_output.reshape(frames.shape),
         frame_gradient.reshape(frames.shape),
         grad_out,
-        small[:taps],
-        small[taps],
+        tap_total,
+        gain_total,
     )
 
 

time: 229 us -> 212 us (0.926); the launches traced: 228 us -> 208 us
  waiting for transfers between devices: 35.2 us -> 19.7 us
  starting transfers between devices: 73.3 us -> 67.7 us
  local copies, waits for them, and re-layouts: 9.24 us -> 14.1 us
    ppermute x21 -> x9, starting transfers between devices: 37.4 us -> 20.6 us  [shift_red(): lax.ppermute(x, 'red', [(i, (i + s) % red_size) for i in range(red_size)])]
    all_to_all x0 -> x3, starting transfers between devices: none -> 13.1 us  [send_line(): return lax.all_to_all(parts, 'red', 0, 0, tiled=True)]
    ppermute x27 -> x23, waiting for transfers between devices: 20.1 us -> 8.5 us  [to_quarter(): return lax.ppermute(x, 'dp', [(i, i ^ 2 * r) for i in range(dp_size)])]
    ppermute x27 -> x23, starting transfers between devices: 34 us -> 27.9 us  [to_quarter(): return lax.ppermute(x, 'dp', [(i, i ^ 2 * r) for i in range(dp_size)])]
    ppermute x21 -> x9, waiting for transfers between devices: 14.2 us -> 8.32 us  [shift_red(): lax.ppermute(x, 'red', [(i, (i + s) % red_size) for i in range(red_size)])]
    ppermute x0 -> x2, starting transfers between devices: none -> 4.51 us  [local(): lax.ppermute(small, 'red', [(i, i ^ bit) for i in range(red_size)])]
    pallas_call x3, Pallas kernels: 2.3 us -> 6.81 us  [add_plane(): pl.pallas_call(ordered(plane_kernel, 4, len(deps)), grid=(1,), in_specs=[...]
    pallas_call x3, Pallas kernels: 56.9 us -> 52.5 us  [middle(): pl.pallas_call(ordered(functools.partial(chunk_kernel, red_size, length,...]
  transfers between devices with their start and end apart: 57 -> 44, of which waited for: 16 -> 9; matrix products, arithmetic and copies ran while one was open for 3% -> 2% of each run, Pallas kernels for 40% -> 48%
where the time goes in v3:
time: 212 us; the launch traced here: 208 us
  Pallas kernels  101 us (48%)
  starting transfers between devices  67.7 us (32%)
  waiting for transfers between devices  19.7 us (9%)
  local copies, waits for them, and re-layouts  14.1 us (7%)
  between operations  2.17 us (1%)
    pallas_call x3, Pallas kernels, middle(): pl.pallas_call(ordered(functools.partial(chunk_kernel, red_size, length,...  52.5 us
    ppermute x23, starting transfers between devices, to_quarter(): return lax.ppermute(x, 'dp', [(i, i ^ 2 * r) for i in range(dp_size)])  27.9 us
    ppermute x9, starting transfers between devices, shift_red(): lax.ppermute(x, 'red', [(i, (i + s) % red_size) for i in range(red_size)])  20.6 us
    pallas_call x1, Pallas kernels, local(): pl.pallas_call(ordered(functools.partial(frame_kernel, n_chunks), 8 + 2 *...  13.3 us
    all_to_all x3, starting transfers between devices, send_line(): return lax.all_to_all(parts, 'red', 0, 0, tiled=True)  13.1 us
    unnamed x70, local copies, waits for them, and re-layouts  12.5 us
    ppermute x23, waiting for transfers between devices, to_quarter(): return lax.ppermute(x, 'dp', [(i, i ^ 2 * r) for i in range(dp_size)])  8.5 us
    ppermute x9, waiting for transfers between devices, shift_red(): lax.ppermute(x, 'red', [(i, (i + s) % red_size) for i in range(red_size)])  8.32 us
  transfers between devices with their start and end apart: 44, of which 9 were waited for; matrix products, arithmetic and copies ran while one was open for 2% of the time, Pallas kernels for 48%

profile of v3, /device:TPU:0, one launch (start us, length us, event | category | flops | bytes accessed | tf_op | source)
XLA Modules:
  0.0 207.8 jit_solution(4628208092160435119)
XLA Ops:
  1.3 1.7 copy-done.7
  3.6 3.1 %collective-permute-start.2 = (bf16[192,512]{1,0:T(8,128)(2,1)S(1)}, bf16[192,512]{1,0:T(8,128)(2,1)S(1)}, u32[]{:S(2)}, u32[]{:S(2)}) collective-permute-start(bf16[192,512]{1,0:T(8,128)(2,1)S(1)} %shard_map.137.refs_3_), channel_id=1, source_target_pairs={{0,1},{1,2},{2,3},{3,0},{4,5},{5,6},{6,7},{7,4},{8,9},{9,10},{10,1... | collective-permute-start | bytes 589832 | tf_op jit(solution)/shard_map/ppermute | solution.py:390
  6.6 2.6 %collective-permute-start.3 = (bf16[192,512]{1,0:T(8,128)(2,1)S(1)}, bf16[192,512]{1,0:T(8,128)(2,1)S(1)}, u32[]{:S(2)}, u32[]{:S(2)}) collective-permute-start(bf16[192,512]{1,0:T(8,128)(2,1)S(1)} %shard_map.137.refs_3_), channel_id=1, source_target_pairs={{0,2},{1,3},{2,0},{3,1},{4,6},{5,7},{6,4},{7,5},{8,10},{9,11},{10,... | collective-permute-start | bytes 589832 | tf_op jit(solution)/shard_map/ppermute | solution.py:390
  13.5 1.8 copy-done.9
  15.3 8.2 %shard_map.138 = (bf16[1536,1536]{1,0:T(8,128)(2,1)}, bf16[1536,1536]{1,0:T(8,128)(2,1)}) custom-call(bf16[768,1536]{1,0:T(8,128)(2,1)S(1)} %bitcast.25, bf16[768,1536]{1,0:T(8,128)(2,1)} %collective-permute-done.refs_1_.refs_10_, f32[1,1536]{1,0:T(1,128)S(1)} %reshape.131.refs_2_.refs_4_, bf16[192,512]{1,0:T(8,128)(2,1)S(1)} %shard_map.137.refs_3_, ...), custom_call_target="tpu_custom_call" | custom-call | flops 99999997952 | bytes 200000000 | tf_op jit(solution)/shard_map/pallas_call | solution.py:452
  24.1 3.5 %collective-permute-start.7 = (bf16[192,512]{1,0:T(8,128)(2,1)S(1)}, bf16[192,512]{1,0:T(8,128)(2,1)S(1)}, u32[]{:S(2)}, u32[]{:S(2)}) collective-permute-start(bf16[192,512]{1,0:T(8,128)(2,1)S(1)} %shard_map.140.refs_18_), channel_id=1, source_target_pairs={{0,1},{1,2},{2,3},{3,0},{4,5},{5,6},{6,7},{7,4},{8,9},{9,10},{10,1... | collective-permute-start | bytes 589832 | tf_op jit(solution)/shard_map/ppermute | solution.py:390
  27.7 1.6 collective-permute-start.8
  30.2 1.5 collective-permute-start.5
  31.7 1.5 collective-permute-start.6
  34.6 6.9 %collective-permute-done.8.refs_1_.refs_4_.refs_5_ = bf16[192,512]{1,0:T(8,128)(2,1)S(1)} collective-permute-done((bf16[192,512]{1,0:T(8,128)(2,1)S(1)}, bf16[192,512]{1,0:T(8,128)(2,1)S(1)}, u32[]{:S(2)}, u32[]{:S(2)}) %collective-permute-start.8) | collective-permute-done | bytes 196640 | tf_op jit(solution)/shard_map/ppermute | solution.py:390
  42.8 4.7 %collective-permute-start.12 = (bf16[192,512]{1,0:T(8,128)(2,1)}, bf16[192,512]{1,0:T(8,128)(2,1)}, u32[]{:S(2)}, u32[]{:S(2)}) collective-permute-start(bf16[192,512]{1,0:T(8,128)(2,1)} %shard_map.142.refs_19_), channel_id=1, source_target_pairs={{0,1},{1,2},{2,3},{3,0},{4,5},{5,6},{6,7},{7,4},{8,9},{9,10},{10,1... | collective-permute-start | bytes 589832 | tf_op jit(solution)/shard_map/ppermute | solution.py:390
  47.5 2.1 %collective-permute-start.13 = (bf16[192,512]{1,0:T(8,128)(2,1)}, bf16[192,512]{1,0:T(8,128)(2,1)}, u32[]{:S(2)}, u32[]{:S(2)}) collective-permute-start(bf16[192,512]{1,0:T(8,128)(2,1)} %shard_map.142.refs_19_), channel_id=1, source_target_pairs={{0,2},{1,3},{2,0},{3,1},{4,6},{5,7},{6,4},{7,5},{8,10},{9,11},{10,... | collective-permute-start | bytes 589832 | tf_op jit(solution)/shard_map/ppermute | solution.py:390
  51.4 1.5 collective-permute-start.10
  52.9 1.5 collective-permute-start.11
  54.7 17.3 %shard_map.143 = (bf16[768,768]{1,0:T(8,128)(2,1)}, bf16[768,768]{1,0:T(8,128)(2,1)}, bf16[4,96,512]{2,1,0:T(8,128)(2,1)S(1)}, bf16[4,96,512]{2,1,0:T(8,128)(2,1...) custom-call(s32[4]{0:T(128)S(1)} %pad_add_fusion.refs_0_.idx, ...), custom_call_target="tpu_custom_call" | custom-call | flops 99999997952 | bytes 200000000 | tf_op jit(solution)/shard_map/pallas_call | solution.py:520
  73.1 2.4 %collective-permute-start.19 = (bf16[4,96,512]{2,1,0:T(8,128)(2,1)}, bf16[4,96,512]{2,1,0:T(8,128)(2,1)}, u32[]{:S(2)}, u32[]{:S(2)}) collective-permute-start(bf16[4,96,512]{2,1,0:T(8,128)(2,1)} %get-tuple-element.61), channel_id=1, source_target_pairs={{0,24},{4,28},{8,16},{12,20},{16,8},{20,12},{24,0},{28,4},{1,25},{... | collective-permute-start | bytes 1179656 | tf_op jit(solution)/shard_map/ppermute | solution.py:387
  75.6 2.0 shard_map.144
  78.7 17.5 %shard_map.145 = (bf16[768,768]{1,0:T(8,128)(2,1)}, bf16[768,768]{1,0:T(8,128)(2,1)}, bf16[4,96,512]{2,1,0:T(8,128)(2,1)S(1)}, bf16[4,96,512]{2,1,0:T(8,128)(2,1...) custom-call(s32[4]{0:T(128)S(1)} %pad_add_fusion.refs_0_.idx, ...), custom_call_target="tpu_custom_call", output_to_operand_aliasing={{0}: (17, {}), {1}: (18, {})} | custom-call | flops 99999997952 | bytes 200000000 | tf_op jit(solution)/shard_map/pallas_call | solution.py:520
  97.0 1.5 collective-permute-start.20
  98.5 1.5 collective-permute-start.21
  100.5 2.2 %shard_map.146.refs_19_ = bf16[4,96,512]{2,1,0:T(8,128)(2,1)} custom-call(bf16[4,96,512]{2,1,0:T(8,128)(2,1)S(1)} %get-tuple-element.58.refs_0_, bf16[4,96,512]{2,1,0:T(8,128)(2,1)} %collective-permute-done.17.refs_1_, bf16[4,96,512]{2,1,0:T(8,128)(2,1)} %collective-permute-done.18.refs_2_, bf16[4,96,512]{2,1,0:T(8,128)(2,1)} %collective-permute-done.19.refs_3_, ...), custom_call_target="tpu_custom_call" | custom-call | flops 99999997952 | bytes 200000000 | tf_op jit(solution)/shard_map/pallas_call | solution.py:561
  102.7 4.3 %all-to-all-start = ((bf16[4,96,512]{2,1,0:T(8,128)(2,1)}), bf16[4,96,512]{2,1,0:T(8,128)(2,1)}, u32[]{:S(2)}, u32[]{:S(2)}) async-start(bf16[4,96,512]{2,1,0:T(8,128)(2,1)} %shard_map.146.refs_19_), calls=%async_computation | async-start | bytes 786432 | tf_op jit(solution)/shard_map/all_to_all | solution.py:575
  107.0 17.7 %shard_map.147 = (bf16[768,768]{1,0:T(8,128)(2,1)}, bf16[768,768]{1,0:T(8,128)(2,1)}, bf16[4,96,512]{2,1,0:T(8,128)(2,1)S(1)}, bf16[4,96,512]{2,1,0:T(8,128)(2,1...) custom-call(s32[4]{0:T(128)S(1)} %pad_add_fusion.refs_0_.idx, ...), custom_call_target="tpu_custom_call", output_to_operand_aliasing={{0}: (17, {}), {1}: (18, {})} | custom-call | flops 99999997952 | bytes 200000000 | tf_op jit(solution)/shard_map/pallas_call | solution.py:520
  124.8 1.6 collective-permute-start.25
  126.3 1.5 collective-permute-start.26
  129.3 2.3 %shard_map.148.refs_7_ = bf16[4,96,512]{2,1,0:T(8,128)(2,1)} custom-call(bf16[4,96,512]{2,1,0:T(8,128)(2,1)S(1)} %copy-done.28, bf16[4,96,512]{2,1,0:T(8,128)(2,1)} %collective-permute-done.20.refs_1_, bf16[4,96,512]{2,1,0:T(8,128)(2,1)} %collective-permute-done.21.refs_2_, bf16[4,96,512]{2,1,0:T(8,128)(2,1)} %collective-permute-done.22.refs_3_, ...), custom_call_target="tpu_custom_call" | custom-call | flops 99999997952 | bytes 200000000 | tf_op jit(solution)/shard_map/pallas_call | solution.py:561
  131.6 5.1 %all-to-all-start.1 = ((bf16[4,96,512]{2,1,0:T(8,128)(2,1)}), bf16[4,96,512]{2,1,0:T(8,128)(2,1)S(1)}, u32[]{:S(2)}, u32[]{:S(2)}) async-start(bf16[4,96,512]{2,1,0:T(8,128)(2,1)} %shard_map.148.refs_7_), calls=%async_computation.1 | async-start | bytes 786432 | tf_op jit(solution)/shard_map/all_to_all | solution.py:575
  136.7 1.4 copy-done.23
  138.1 1.4 copy-done.24
  139.5 7.7 %shard_map.149.refs_3_ = bf16[768,1536]{1,0:T(8,128)(2,1)} custom-call(bf16[1536,512]{1,0:T(8,128)(2,1)S(1)} %copy-done.24, bf16[1536,512]{1,0:T(8,128)(2,1)S(1)} %copy-done.23, bf16[1536,512]{1,0:T(8,128)(2,1)S(1)} %copy-done.22, bf16[1536,512]{1,0:T(8,128)(2,1)} %get-tuple-element.64.refs_3_.refs_11_, ...), custom_call_target="tpu_custom_call" | custom-call | flops 99999997952 | bytes 200000000 | tf_op jit(solution)/shard_map/pallas_call | solution.py:664
  147.4 1.6 all-to-all-done.1.refs_2_
  149.0 1.7 copy-done.10
  151.8 2.3 %shard_map.151.refs_14_ = bf16[4,96,512]{2,1,0:T(8,128)(2,1)} custom-call(bf16[4,96,512]{2,1,0:T(8,128)(2,1)S(1)} %get-tuple-element.74.refs_0_, bf16[4,96,512]{2,1,0:T(8,128)(2,1)} %collective-permute-done.25.refs_1_, bf16[4,96,512]{2,1,0:T(8,128)(2,1)} %collective-permute-done.26.refs_2_, bf16[4,96,512]{2,1,0:T(8,128)(2,1)} %collective-permute-done.27.refs_3_, ...), custom_call_target="tpu_custom_call" | custom-call | flops 99999997952 | bytes 200000000 | tf_op jit(solution)/shard_map/pallas_call | solution.py:561
  154.1 3.7 %all-to-all-start.2 = ((bf16[4,96,512]{2,1,0:T(8,128)(2,1)}), bf16[4,96,512]{2,1,0:T(8,128)(2,1)S(1)}, u32[]{:S(2)}, u32[]{:S(2)}) async-start(bf16[4,96,512]{2,1,0:T(8,128)(2,1)} %shard_map.151.refs_14_), calls=%async_computation.2 | async-start | bytes 786432 | tf_op jit(solution)/shard_map/all_to_all | solution.py:575
  159.2 13.3 %shard_map.152 = (bf16[768,1536]{1,0:T(8,128)(2,1)}, bf16[768,1536]{1,0:T(8,128)(2,1)}, f32[8,1536]{1,0:T(8,128)S(1)}) custom-call(s32[4]{0:T(128)S(1)} %pad_add_fusion.refs_0_.idx, bf16[768,1536]{1,0:T(8,128)(2,1)} %bitcast.24, bf16[768,1536]{1,0:T(8,128)(2,1)} %bitcast.30, f32[1536,128]{1,0:T(8,128)S(1)} %broadcast_in_dim.2.refs_13_.refs_3_, ...), custom_call_target="tpu_custom_call" | custom-call | flops 99999997952 | bytes 200000000 | tf_op jit(solution)/shard_map/pallas_call | solution.py:680
  172.5 1.5 collective-permute-start.36
  174.6 1.5 collective-permute-start.32
  176.1 1.4 collective-permute-start.33
  178.8 1.6 collective-permute-start.37
  180.4 2.6 %collective-permute-done.31.refs_1_ = bf16[2,96,512]{2,1,0:T(8,128)(2,1)S(1)} collective-permute-done((bf16[2,96,512]{2,1,0:T(8,128)(2,1)S(1)}, bf16[2,96,512]{2,1,0:T(8,128)(2,1)S(1)}, u32[]{:S(2)}, u32[]{:S(2)}) %collective-permute-start.31) | collective-permute-done | bytes 196640 | tf_op jit(solution)/shard_map/ppermute | solution.py:387
  183.0 4.3 %collective-permute-done.33.refs_3_ = bf16[2,96,512]{2,1,0:T(8,128)(2,1)S(1)} collective-permute-done((bf16[2,96,512]{2,1,0:T(8,128)(2,1)S(1)}, bf16[2,96,512]{2,1,0:T(8,128)(2,1)S(1)}, u32[]{:S(2)}, u32[]{:S(2)}) %collective-permute-start.33) | collective-permute-done | bytes 196640 | tf_op jit(solution)/shard_map/ppermute | solution.py:387
  187.8 1.8 collective-permute-start.38
  189.7 1.5 collective-permute-start.28
  191.2 1.5 collective-permute-start.29
  193.3 2.7 %collective-permute-start.39 = (f32[33,768]{1,0:T(8,128)S(1)}, f32[33,768]{1,0:T(8,128)S(1)}, u32[]{:S(2)}, u32[]{:S(2)}) collective-permute-start(f32[33,768]{1,0:T(8,128)S(1)} %add.53), channel_id=1, source_target_pairs={{0,2},{1,3},{2,0},{3,1},{4,6},{5,7},{6,4},{7,5},{8,10},{9,11},{10,... | collective-permute-start | bytes 304136 | tf_op jit(solution)/shard_map/ppermute | solution.py:737
  196.0 3.8 %shard_map.155.refs_4_.rest_0_ = f32[384,3072]{1,0:T(8,128)} custom-call(s32[4]{0:T(128)S(1)} %pad_add_fusion.refs_0_.idx, bf16[4,2,96,512]{3,2,1,0:T(8,128)(2,1)S(1)} %shard_map.154.mine, bf16[4,2,96,512]{3,2,1,0:T(8,128)(2,1)S(1)} %collective-permute-done.34.sib), custom_call_target="tpu_custom_call" | custom-call | flops 99999997952 | bytes 200000000 | tf_op jit(solution)/shard_map/pallas_call | solution.py:611
  199.8 2.3 %copy-done.2 = f32[384,3072]{1,0:T(8,128)S(1)} copy-done((f32[384,3072]{1,0:T(8,128)S(1)}, f32[384,3072]{1,0:T(8,128)}, u32[]{:S(2)}) %copy-start.2) | copy-done | bytes 4718616
  204.0 2.3 %shard_map.157 = f32[384,3072]{1,0:T(8,128)} custom-call(s32[4]{0:T(128)S(1)} %pad_add_fusion.refs_0_.idx, bf16[4,1,96,512]{3,2,1,0:T(8,128)(2,1)S(1)} %shard_map.156.mine, bf16[4,1,96,512]{3,2,1,0:T(8,128)(2,1)S(1)} %collective-permute-done.35.sib, f32[384,3072]{1,0:T(8,128)} %shard_map.155.refs_4_.rest_0_), custom_call_target="tpu_custom_call", output_to_operand_aliasing={{}: (3, {})} | custom-call | flops 1000000 | bytes 1000000 | tf_op jit(solution)/shard_map/pallas_call | solution.py:611
  (153 shorter events, 24.4 us)
Async XLA Ops:
  0.6 12.8 %collective-permute-start = (bf16[768,1536]{1,0:T(8,128)(2,1)}, bf16[768,1536]{1,0:T(8,128)(2,1)}, u32[]{:S(2)}, u32[]{:S(2)}) collective-permute-start(bf16[768,1536]{1,0:T(8,128)(2,1)} %bitcast.20), channel_id=1, source_target_pairs={{0,4},{4,0},{8,12},{12,8},{16,20},{20,16},{24,28},{28,24},{1,5},{5... | collective-permute-start | bytes 7077896 | tf_op jit(solution)/shard_map/ppermute | solution.py:384
  1.2 12.3 %collective-permute-start.1 = (bf16[768,1536]{1,0:T(8,128)(2,1)}, bf16[768,1536]{1,0:T(8,128)(2,1)}, u32[]{:S(2)}, u32[]{:S(2)}) collective-permute-start(bf16[768,1536]{1,0:T(8,128)(2,1)} %bitcast.26), channel_id=1, source_target_pairs={{0,4},{4,0},{8,12},{12,8},{16,20},{20,16},{24,28},{28,24},{1,5},{5... | collective-permute-start | bytes 7077896 | tf_op jit(solution)/shard_map/ppermute | solution.py:384
  3.6 19.9 %collective-permute-start.2 = (bf16[192,512]{1,0:T(8,128)(2,1)S(1)}, bf16[192,512]{1,0:T(8,128)(2,1)S(1)}, u32[]{:S(2)}, u32[]{:S(2)}) collective-permute-start(bf16[192,512]{1,0:T(8,128)(2,1)S(1)} %shard_map.137.refs_3_), channel_id=1, source_target_pairs={{0,1},{1,2},{2,3},{3,0},{4,5},{5,6},{6,7},{7,4},{8,9},{9,10},{10,1... | collective-permute-start | bytes 589832 | tf_op jit(solution)/shard_map/ppermute | solution.py:390
  6.6 16.9 %collective-permute-start.3 = (bf16[192,512]{1,0:T(8,128)(2,1)S(1)}, bf16[192,512]{1,0:T(8,128)(2,1)S(1)}, u32[]{:S(2)}, u32[]{:S(2)}) collective-permute-start(bf16[192,512]{1,0:T(8,128)(2,1)S(1)} %shard_map.137.refs_3_), channel_id=1, source_target_pairs={{0,2},{1,3},{2,0},{3,1},{4,6},{5,7},{6,4},{7,5},{8,10},{9,11},{10,... | collective-permute-start | bytes 589832 | tf_op jit(solution)/shard_map/ppermute | solution.py:390
  9.2 14.3 %collective-permute-start.4 = (bf16[192,512]{1,0:T(8,128)(2,1)S(1)}, bf16[192,512]{1,0:T(8,128)(2,1)S(1)}, u32[]{:S(2)}, u32[]{:S(2)}) collective-permute-start(bf16[192,512]{1,0:T(8,128)(2,1)S(1)} %shard_map.137.refs_3_), channel_id=1, source_target_pairs={{0,3},{1,0},{2,1},{3,2},{4,7},{5,4},{6,5},{7,6},{8,11},{9,8},{10,9... | collective-permute-start | bytes 589832 | tf_op jit(solution)/shard_map/ppermute | solution.py:390
  24.1 10.5 %collective-permute-start.7 = (bf16[192,512]{1,0:T(8,128)(2,1)S(1)}, bf16[192,512]{1,0:T(8,128)(2,1)S(1)}, u32[]{:S(2)}, u32[]{:S(2)}) collective-permute-start(bf16[192,512]{1,0:T(8,128)(2,1)S(1)} %shard_map.140.refs_18_), channel_id=1, source_target_pairs={{0,1},{1,2},{2,3},{3,0},{4,5},{5,6},{6,7},{7,4},{8,9},{9,10},{10,1... | collective-permute-start | bytes 589832 | tf_op jit(solution)/shard_map/ppermute | solution.py:390
  27.7 13.9 %collective-permute-start.8 = (bf16[192,512]{1,0:T(8,128)(2,1)S(1)}, bf16[192,512]{1,0:T(8,128)(2,1)S(1)}, u32[]{:S(2)}, u32[]{:S(2)}) collective-permute-start(bf16[192,512]{1,0:T(8,128)(2,1)S(1)} %shard_map.140.refs_18_), channel_id=1, source_target_pairs={{0,2},{1,3},{2,0},{3,1},{4,6},{5,7},{6,4},{7,5},{8,10},{9,11},{10,... | collective-permute-start | bytes 589832 | tf_op jit(solution)/shard_map/ppermute | solution.py:390
  29.3 12.3 %collective-permute-start.9 = (bf16[192,512]{1,0:T(8,128)(2,1)S(1)}, bf16[192,512]{1,0:T(8,128)(2,1)S(1)}, u32[]{:S(2)}, u32[]{:S(2)}) collective-permute-start(bf16[192,512]{1,0:T(8,128)(2,1)S(1)} %shard_map.140.refs_18_), channel_id=1, source_target_pairs={{0,3},{1,0},{2,1},{3,2},{4,7},{5,4},{6,5},{7,6},{8,11},{9,8},{10,9... | collective-permute-start | bytes 589832 | tf_op jit(solution)/shard_map/ppermute | solution.py:390
  30.2 20.3 %collective-permute-start.5 = (bf16[3,192,256]{2,1,0:T(8,128)(2,1)S(1)}, bf16[3,192,256]{2,1,0:T(8,128)(2,1)S(1)}, u32[]{:S(2)}, u32[]{:S(2)}) collective-permute-start(bf16[3,192,256]{2,1,0:T(8,128)(2,1)S(1)} %get-tuple-element.45), channel_id=1, source_target_pairs={{0,8},{4,12},{8,0},{12,4},{16,24},{20,28},{24,16},{28,20},{1,9},{5... | collective-permute-start | bytes 884744 | tf_op jit(solution)/shard_map/ppermute | solution.py:387
  31.7 18.8 %collective-permute-start.6 = (bf16[3,192,256]{2,1,0:T(8,128)(2,1)S(1)}, bf16[3,192,256]{2,1,0:T(8,128)(2,1)S(1)}, u32[]{:S(2)}, u32[]{:S(2)}) collective-permute-start(bf16[3,192,256]{2,1,0:T(8,128)(2,1)S(1)} %get-tuple-element.46), channel_id=1, source_target_pairs={{0,16},{4,20},{8,24},{12,28},{16,0},{20,4},{24,8},{28,12},{1,17},{... | collective-permute-start | bytes 884744 | tf_op jit(solution)/shard_map/ppermute | solution.py:387
  42.8 29.2 %collective-permute-start.12 = (bf16[192,512]{1,0:T(8,128)(2,1)}, bf16[192,512]{1,0:T(8,128)(2,1)}, u32[]{:S(2)}, u32[]{:S(2)}) collective-permute-start(bf16[192,512]{1,0:T(8,128)(2,1)} %shard_map.142.refs_19_), channel_id=1, source_target_pairs={{0,1},{1,2},{2,3},{3,0},{4,5},{5,6},{6,7},{7,4},{8,9},{9,10},{10,1... | collective-permute-start | bytes 589832 | tf_op jit(solution)/shard_map/ppermute | solution.py:390
  47.5 25.1 %collective-permute-start.13 = (bf16[192,512]{1,0:T(8,128)(2,1)}, bf16[192,512]{1,0:T(8,128)(2,1)}, u32[]{:S(2)}, u32[]{:S(2)}) collective-permute-start(bf16[192,512]{1,0:T(8,128)(2,1)} %shard_map.142.refs_19_), channel_id=1, source_target_pairs={{0,2},{1,3},{2,0},{3,1},{4,6},{5,7},{6,4},{7,5},{8,10},{9,11},{10,... | collective-permute-start | bytes 589832 | tf_op jit(solution)/shard_map/ppermute | solution.py:390
  49.6 23.5 %collective-permute-start.14 = (bf16[192,512]{1,0:T(8,128)(2,1)}, bf16[192,512]{1,0:T(8,128)(2,1)}, u32[]{:S(2)}, u32[]{:S(2)}) collective-permute-start(bf16[192,512]{1,0:T(8,128)(2,1)} %shard_map.142.refs_19_), channel_id=1, source_target_pairs={{0,3},{1,0},{2,1},{3,2},{4,7},{5,4},{6,5},{7,6},{8,11},{9,8},{10,9... | collective-permute-start | bytes 589832 | tf_op jit(solution)/shard_map/ppermute | solution.py:390
  51.4 26.2 %collective-permute-start.10 = (bf16[3,192,256]{2,1,0:T(8,128)(2,1)}, bf16[3,192,256]{2,1,0:T(8,128)(2,1)}, u32[]{:S(2)}, u32[]{:S(2)}) collective-permute-start(bf16[3,192,256]{2,1,0:T(8,128)(2,1)} %get-tuple-element.47.refs_17_), channel_id=1, source_target_pairs={{0,8},{4,12},{8,0},{12,4},{16,24},{20,28},{24,16},{28,20},{1,9},{5... | collective-permute-start | bytes 884744 | tf_op jit(solution)/shard_map/ppermute | solution.py:387
  52.9 25.3 %collective-permute-start.11 = (bf16[3,192,256]{2,1,0:T(8,128)(2,1)}, bf16[3,192,256]{2,1,0:T(8,128)(2,1)}, u32[]{:S(2)}, u32[]{:S(2)}) collective-permute-start(bf16[3,192,256]{2,1,0:T(8,128)(2,1)} %get-tuple-element.49), channel_id=1, source_target_pairs={{0,16},{4,20},{8,24},{12,28},{16,0},{20,4},{24,8},{28,12},{1,17},{... | collective-permute-start | bytes 884744 | tf_op jit(solution)/shard_map/ppermute | solution.py:387
  72.0 25.0 %collective-permute-start.17 = (bf16[4,96,512]{2,1,0:T(8,128)(2,1)}, bf16[4,96,512]{2,1,0:T(8,128)(2,1)}, u32[]{:S(2)}, u32[]{:S(2)}) collective-permute-start(bf16[4,96,512]{2,1,0:T(8,128)(2,1)} %get-tuple-element.59), channel_id=1, source_target_pairs={{0,8},{4,12},{8,0},{12,4},{16,24},{20,28},{24,16},{28,20},{1,9},{5... | collective-permute-start | bytes 1179656 | tf_op jit(solution)/shard_map/ppermute | solution.py:387
  72.6 25.9 %collective-permute-start.18 = (bf16[4,96,512]{2,1,0:T(8,128)(2,1)}, bf16[4,96,512]{2,1,0:T(8,128)(2,1)}, u32[]{:S(2)}, u32[]{:S(2)}) collective-permute-start(bf16[4,96,512]{2,1,0:T(8,128)(2,1)} %get-tuple-element.60), channel_id=1, source_target_pairs={{0,16},{4,20},{8,24},{12,28},{16,0},{20,4},{24,8},{28,12},{1,17},{... | collective-permute-start | bytes 1179656 | tf_op jit(solution)/shard_map/ppermute | solution.py:387
  73.1 26.9 %collective-permute-start.19 = (bf16[4,96,512]{2,1,0:T(8,128)(2,1)}, bf16[4,96,512]{2,1,0:T(8,128)(2,1)}, u32[]{:S(2)}, u32[]{:S(2)}) collective-permute-start(bf16[4,96,512]{2,1,0:T(8,128)(2,1)} %get-tuple-element.61), channel_id=1, source_target_pairs={{0,24},{4,28},{8,16},{12,20},{16,8},{20,12},{24,0},{28,4},{1,25},{... | collective-permute-start | bytes 1179656 | tf_op jit(solution)/shard_map/ppermute | solution.py:387
  77.6 29.4 %collective-permute-start.15 = (bf16[3,192,256]{2,1,0:T(8,128)(2,1)}, bf16[3,192,256]{2,1,0:T(8,128)(2,1)}, u32[]{:S(2)}, u32[]{:S(2)}) collective-permute-start(bf16[3,192,256]{2,1,0:T(8,128)(2,1)} %get-tuple-element.53.refs_19_), channel_id=1, source_target_pairs={{0,8},{4,12},{8,0},{12,4},{16,24},{20,28},{24,16},{28,20},{1,9},{5... | collective-permute-start | bytes 884744 | tf_op jit(solution)/shard_map/ppermute | solution.py:387
  78.2 28.9 %collective-permute-start.16 = (bf16[3,192,256]{2,1,0:T(8,128)(2,1)}, bf16[3,192,256]{2,1,0:T(8,128)(2,1)}, u32[]{:S(2)}, u32[]{:S(2)}) collective-permute-start(bf16[3,192,256]{2,1,0:T(8,128)(2,1)} %get-tuple-element.55), channel_id=1, source_target_pairs={{0,16},{4,20},{8,24},{12,28},{16,0},{20,4},{24,8},{28,12},{1,17},{... | collective-permute-start | bytes 884744 | tf_op jit(solution)/shard_map/ppermute | solution.py:387
  97.0 31.8 %collective-permute-start.20 = (bf16[4,96,512]{2,1,0:T(8,128)(2,1)}, bf16[4,96,512]{2,1,0:T(8,128)(2,1)}, u32[]{:S(2)}, u32[]{:S(2)}) collective-permute-start(bf16[4,96,512]{2,1,0:T(8,128)(2,1)} %get-tuple-element.69), channel_id=1, source_target_pairs={{0,8},{4,12},{8,0},{12,4},{16,24},{20,28},{24,16},{28,20},{1,9},{5... | collective-permute-start | bytes 1179656 | tf_op jit(solution)/shard_map/ppermute | solution.py:387
  98.5 30.8 %collective-permute-start.21 = (bf16[4,96,512]{2,1,0:T(8,128)(2,1)}, bf16[4,96,512]{2,1,0:T(8,128)(2,1)}, u32[]{:S(2)}, u32[]{:S(2)}) collective-permute-start(bf16[4,96,512]{2,1,0:T(8,128)(2,1)} %get-tuple-element.70), channel_id=1, source_target_pairs={{0,16},{4,20},{8,24},{12,28},{16,0},{20,4},{24,8},{28,12},{1,17},{... | collective-permute-start | bytes 1179656 | tf_op jit(solution)/shard_map/ppermute | solution.py:387
  100.0 29.3 %collective-permute-start.22 = (bf16[4,96,512]{2,1,0:T(8,128)(2,1)}, bf16[4,96,512]{2,1,0:T(8,128)(2,1)}, u32[]{:S(2)}, u32[]{:S(2)}) collective-permute-start(bf16[4,96,512]{2,1,0:T(8,128)(2,1)} %get-tuple-element.71), channel_id=1, source_target_pairs={{0,24},{4,28},{8,16},{12,20},{16,8},{20,12},{24,0},{28,4},{1,25},{... | collective-permute-start | bytes 1179656 | tf_op jit(solution)/shard_map/ppermute | solution.py:387
  102.7 28.9 %all-to-all-start = ((bf16[4,96,512]{2,1,0:T(8,128)(2,1)}), bf16[4,96,512]{2,1,0:T(8,128)(2,1)}, u32[]{:S(2)}, u32[]{:S(2)}) async-start(bf16[4,96,512]{2,1,0:T(8,128)(2,1)} %shard_map.146.refs_19_), calls=%async_computation | async-start | bytes 786432 | tf_op jit(solution)/shard_map/all_to_all | solution.py:575
  107.0 20.8 %copy-start.4 = (f32[96,256]{1,0:T(8,128)S(1)}, f32[96,256]{1,0:T(8,128)}, u32[]{:S(2)}) copy-start(f32[96,256]{1,0:T(8,128)} %copy-done.3) | copy-start | bytes 294916
  107.0 20.8 %copy-start.32 = (f32[31,96]{1,0:T(8,128)S(1)}, f32[31,96]{1,0:T(8,128)}, u32[]{:S(2)}) copy-start(f32[31,96]{1,0:T(8,128)} %constant.71.clone) | copy-start | bytes 35716
  107.0 22.2 %copy-start.28 = (bf16[4,96,512]{2,1,0:T(8,128)(2,1)S(1)}, bf16[4,96,512]{2,1,0:T(8,128)(2,1)}, u32[]{:S(2)}) copy-start(bf16[4,96,512]{2,1,0:T(8,128)(2,1)} %copy-done.27) | copy-start | bytes 1179652
  124.8 27.0 %collective-permute-start.25 = (bf16[4,96,512]{2,1,0:T(8,128)(2,1)}, bf16[4,96,512]{2,1,0:T(8,128)(2,1)}, u32[]{:S(2)}, u32[]{:S(2)}) collective-permute-start(bf16[4,96,512]{2,1,0:T(8,128)(2,1)} %get-tuple-element.75), channel_id=1, source_target_pairs={{0,8},{4,12},{8,0},{12,4},{16,24},{20,28},{24,16},{28,20},{1,9},{5... | collective-permute-start | bytes 1179656 | tf_op jit(solution)/shard_map/ppermute | solution.py:387
  126.3 25.5 %collective-permute-start.26 = (bf16[4,96,512]{2,1,0:T(8,128)(2,1)}, bf16[4,96,512]{2,1,0:T(8,128)(2,1)}, u32[]{:S(2)}, u32[]{:S(2)}) collective-permute-start(bf16[4,96,512]{2,1,0:T(8,128)(2,1)} %get-tuple-element.76), channel_id=1, source_target_pairs={{0,16},{4,20},{8,24},{12,28},{16,0},{20,4},{24,8},{28,12},{1,17},{... | collective-permute-start | bytes 1179656 | tf_op jit(solution)/shard_map/ppermute | solution.py:387
  128.8 23.0 %collective-permute-start.27 = (bf16[4,96,512]{2,1,0:T(8,128)(2,1)}, bf16[4,96,512]{2,1,0:T(8,128)(2,1)}, u32[]{:S(2)}, u32[]{:S(2)}) collective-permute-start(bf16[4,96,512]{2,1,0:T(8,128)(2,1)} %get-tuple-element.77), channel_id=1, source_target_pairs={{0,24},{4,28},{8,16},{12,20},{16,8},{20,12},{24,0},{28,4},{1,25},{... | collective-permute-start | bytes 1179656 | tf_op jit(solution)/shard_map/ppermute | solution.py:387
  129.3 28.6 %collective-permute-start.24 = (bf16[768,768]{1,0:T(8,128)(2,1)}, bf16[768,768]{1,0:T(8,128)(2,1)}, u32[]{:S(2)}, u32[]{:S(2)}) collective-permute-start(bf16[768,768]{1,0:T(8,128)(2,1)} %get-tuple-element.73), channel_id=1, source_target_pairs={{0,4},{4,0},{8,12},{12,8},{16,20},{20,16},{24,28},{28,24},{1,5},{5... | collective-permute-start | bytes 3538952 | tf_op jit(solution)/shard_map/ppermute | solution.py:384
  131.6 17.4 %all-to-all-start.1 = ((bf16[4,96,512]{2,1,0:T(8,128)(2,1)}), bf16[4,96,512]{2,1,0:T(8,128)(2,1)S(1)}, u32[]{:S(2)}, u32[]{:S(2)}) async-start(bf16[4,96,512]{2,1,0:T(8,128)(2,1)} %shard_map.148.refs_7_), calls=%async_computation.1 | async-start | bytes 786432 | tf_op jit(solution)/shard_map/all_to_all | solution.py:575
  147.2 10.7 %collective-permute-start.23 = (bf16[768,1536]{1,0:T(8,128)(2,1)}, bf16[768,1536]{1,0:T(8,128)(2,1)}, u32[]{:S(2)}, u32[]{:S(2)}) collective-permute-start(bf16[768,1536]{1,0:T(8,128)(2,1)} %shard_map.149.refs_3_), channel_id=1, source_target_pairs={{0,4},{4,0},{8,12},{12,8},{16,20},{20,16},{24,28},{28,24},{1,5},{5... | collective-permute-start | bytes 7077896 | tf_op jit(solution)/shard_map/ppermute | solution.py:384
  154.1 35.5 %all-to-all-start.2 = ((bf16[4,96,512]{2,1,0:T(8,128)(2,1)}), bf16[4,96,512]{2,1,0:T(8,128)(2,1)S(1)}, u32[]{:S(2)}, u32[]{:S(2)}) async-start(bf16[4,96,512]{2,1,0:T(8,128)(2,1)} %shard_map.151.refs_14_), calls=%async_computation.2 | async-start | bytes 786432 | tf_op jit(solution)/shard_map/all_to_all | solution.py:575
  159.2 13.3 %copy-start.29 = (f32[31,768]{1,0:T(8,128)S(1)}, f32[31,768]{1,0:T(8,128)}, u32[]{:S(2)}) copy-start(f32[31,768]{1,0:T(8,128)} %fusion) | copy-start | bytes 285700
  172.5 6.2 %collective-permute-start.36 = (f32[33,768]{1,0:T(8,128)S(1)}, f32[33,768]{1,0:T(8,128)S(1)}, u32[]{:S(2)}, u32[]{:S(2)}) collective-permute-start(f32[33,768]{1,0:T(8,128)S(1)} %pad_maximum_fusion.1), channel_id=1, source_target_pairs={{0,8},{4,12},{8,0},{12,4},{16,24},{20,28},{24,16},{28,20},{1,9},{5... | collective-permute-start | bytes 304136 | tf_op jit(solution)/shard_map/ppermute | solution.py:387
  174.0 8.9 %collective-permute-start.31 = (bf16[2,96,512]{2,1,0:T(8,128)(2,1)S(1)}, bf16[2,96,512]{2,1,0:T(8,128)(2,1)S(1)}, u32[]{:S(2)}, u32[]{:S(2)}) collective-permute-start(bf16[2,96,512]{2,1,0:T(8,128)(2,1)S(1)} %shard_map.150.refs_4_.refs_0_), channel_id=1, source_target_pairs={{0,8},{4,12},{8,0},{12,4},{16,24},{20,28},{24,16},{28,20},{1,9},{5... | collective-permute-start | bytes 589832 | tf_op jit(solution)/shard_map/ppermute | solution.py:387
  174.6 8.4 %collective-permute-start.32 = (bf16[2,96,512]{2,1,0:T(8,128)(2,1)S(1)}, bf16[2,96,512]{2,1,0:T(8,128)(2,1)S(1)}, u32[]{:S(2)}, u32[]{:S(2)}) collective-permute-start(bf16[2,96,512]{2,1,0:T(8,128)(2,1)S(1)} %shard_map.150.refs_4_.refs_0_), channel_id=1, source_target_pairs={{0,16},{4,20},{8,24},{12,28},{16,0},{20,4},{24,8},{28,12},{1,17},{... | collective-permute-start | bytes 589832 | tf_op jit(solution)/shard_map/ppermute | solution.py:387
  176.1 11.2 %collective-permute-start.33 = (bf16[2,96,512]{2,1,0:T(8,128)(2,1)S(1)}, bf16[2,96,512]{2,1,0:T(8,128)(2,1)S(1)}, u32[]{:S(2)}, u32[]{:S(2)}) collective-permute-start(bf16[2,96,512]{2,1,0:T(8,128)(2,1)S(1)} %shard_map.150.refs_4_.refs_0_), channel_id=1, source_target_pairs={{0,24},{4,28},{8,16},{12,20},{16,8},{20,12},{24,0},{28,4},{1,25},{... | collective-permute-start | bytes 589832 | tf_op jit(solution)/shard_map/ppermute | solution.py:387
  178.8 9.0 %collective-permute-start.37 = (f32[33,768]{1,0:T(8,128)S(1)}, f32[33,768]{1,0:T(8,128)S(1)}, u32[]{:S(2)}, u32[]{:S(2)}) collective-permute-start(f32[33,768]{1,0:T(8,128)S(1)} %fusion.7), channel_id=1, source_target_pairs={{0,16},{4,20},{8,24},{12,28},{16,0},{20,4},{24,8},{28,12},{1,17},{... | collective-permute-start | bytes 304136 | tf_op jit(solution)/shard_map/ppermute | solution.py:387
  187.4 8.6 %collective-permute-start.34 = (bf16[4,2,96,512]{3,2,1,0:T(8,128)(2,1)S(1)}, bf16[4,2,96,512]{3,2,1,0:T(8,128)(2,1)S(1)}, u32[]{:S(2)}, u32[]{:S(2)}) collective-permute-start(bf16[4,2,96,512]{3,2,1,0:T(8,128)(2,1)S(1)} %shard_map.154.mine), channel_id=1, source_target_pairs={{0,4},{4,0},{8,12},{12,8},{16,20},{20,16},{24,28},{28,24},{1,5},{5... | collective-permute-start | bytes 2359304 | tf_op jit(solution)/shard_map/ppermute | solution.py:384
  187.8 5.5 %collective-permute-start.38 = (f32[33,768]{1,0:T(8,128)S(1)}, f32[33,768]{1,0:T(8,128)S(1)}, u32[]{:S(2)}, u32[]{:S(2)}) collective-permute-start(f32[33,768]{1,0:T(8,128)S(1)} %add.52), channel_id=1, source_target_pairs={{0,1},{1,0},{2,3},{3,2},{4,5},{5,4},{6,7},{7,6},{8,9},{9,8},{10,11... | collective-permute-start | bytes 304136 | tf_op jit(solution)/shard_map/ppermute | solution.py:737
  189.7 10.2 %collective-permute-start.28 = (bf16[1,96,512]{2,1,0:T(8,128)(2,1)S(1)}, bf16[1,96,512]{2,1,0:T(8,128)(2,1)S(1)}, u32[]{:S(2)}, u32[]{:S(2)}) collective-permute-start(bf16[1,96,512]{2,1,0:T(8,128)(2,1)S(1)} %shard_map.153.refs_0_), channel_id=1, source_target_pairs={{0,8},{4,12},{8,0},{12,4},{16,24},{20,28},{24,16},{28,20},{1,9},{5... | collective-permute-start | bytes 294920 | tf_op jit(solution)/shard_map/ppermute | solution.py:387
  191.2 8.6 %collective-permute-start.29 = (bf16[1,96,512]{2,1,0:T(8,128)(2,1)S(1)}, bf16[1,96,512]{2,1,0:T(8,128)(2,1)S(1)}, u32[]{:S(2)}, u32[]{:S(2)}) collective-permute-start(bf16[1,96,512]{2,1,0:T(8,128)(2,1)S(1)} %shard_map.153.refs_0_), channel_id=1, source_target_pairs={{0,16},{4,20},{8,24},{12,28},{16,0},{20,4},{24,8},{28,12},{1,17},{... | collective-permute-start | bytes 294920 | tf_op jit(solution)/shard_map/ppermute | solution.py:387
  192.7 7.1 %collective-permute-start.30 = (bf16[1,96,512]{2,1,0:T(8,128)(2,1)S(1)}, bf16[1,96,512]{2,1,0:T(8,128)(2,1)S(1)}, u32[]{:S(2)}, u32[]{:S(2)}) collective-permute-start(bf16[1,96,512]{2,1,0:T(8,128)(2,1)S(1)} %shard_map.153.refs_0_), channel_id=1, source_target_pairs={{0,24},{4,28},{8,16},{12,20},{16,8},{20,12},{24,0},{28,4},{1,25},{... | collective-permute-start | bytes 294920 | tf_op jit(solution)/shard_map/ppermute | solution.py:387
  193.3 9.0 %collective-permute-start.39 = (f32[33,768]{1,0:T(8,128)S(1)}, f32[33,768]{1,0:T(8,128)S(1)}, u32[]{:S(2)}, u32[]{:S(2)}) collective-permute-start(f32[33,768]{1,0:T(8,128)S(1)} %add.53), channel_id=1, source_target_pairs={{0,2},{1,3},{2,0},{3,1},{4,6},{5,7},{6,4},{7,5},{8,10},{9,11},{10,... | collective-permute-start | bytes 304136 | tf_op jit(solution)/shard_map/ppermute | solution.py:737
  202.2 1.8 collective-permute-start.35
  202.3 3.9 %collective-permute-start.40 = (f32[33,768]{1,0:T(8,128)S(1)}, f32[33,768]{1,0:T(8,128)S(1)}, u32[]{:S(2)}, u32[]{:S(2)}) collective-permute-start(f32[33,768]{1,0:T(8,128)S(1)} %add_multiply_fusion), channel_id=1, source_target_pairs={{0,4},{4,0},{8,12},{12,8},{16,20},{20,16},{24,28},{28,24},{1,5},{5... | collective-permute-start | bytes 304136 | tf_op jit(solution)/shard_map/ppermute | solution.py:384
  (31 other events, 210.7 us)

commit v4 on v3

--- a/solution.py
+++ b/solution.py
@@ -619,7 +619,7 @@
                     lambda k, c, h, idx: (0, near_column + k + c * columns + h * 2 * columns),
                 ),
             ),
-            out_shape=jax.ShapeDtypeStruct((block, 2 * model_width), jnp.float32),
+            out_shape=pltpu.HBM((block, 2 * model_width), jnp.float32),
             input_output_aliases={3: 0} if has_out else {},
             compiler_params=params(),
             cost_estimate=estimate,
@@ -668,7 +668,7 @@
         + w_specs
         + [ANY] * len(deps),
         out_specs=whole((own_rows, model_width)),
-        out_shape=jax.ShapeDtypeStruct((own_rows, model_width), jnp.bfloat16),
+        out_shape=pltpu.HBM((own_rows, model_width), jnp.bfloat16),
         compiler_params=params(),
         cost_estimate=LONG,
     )(*ghs, *ws, *deps)

time: 212 us -> 212 us (level)
  no operation moved by 1% of the time
where the time goes in v4:
time: 212 us; the launch traced here: 208 us
  Pallas kernels  101 us (48%)
  starting transfers between devices  67.7 us (32%)
  waiting for transfers between devices  19.7 us (9%)
  local copies, waits for them, and re-layouts  14.1 us (7%)
  between operations  2.17 us (1%)
    pallas_call x3, Pallas kernels, middle(): pl.pallas_call(ordered(functools.partial(chunk_kernel, red_size, length,...  52.5 us
    ppermute x23, starting transfers between devices, to_quarter(): return lax.ppermute(x, 'dp', [(i, i ^ 2 * r) for i in range(dp_size)])  27.9 us
    ppermute x9, starting transfers between devices, shift_red(): lax.ppermute(x, 'red', [(i, (i + s) % red_size) for i in range(red_size)])  20.6 us
    pallas_call x1, Pallas kernels, local(): pl.pallas_call(ordered(functools.partial(frame_kernel, n_chunks), 8 + 2 *...  13.3 us
    all_to_all x3, starting transfers between devices, send_line(): return lax.all_to_all(parts, 'red', 0, 0, tiled=True)  13.1 us
    unnamed x70, local copies, waits for them, and re-layouts  12.5 us
    ppermute x23, waiting for transfers between devices, to_quarter(): return lax.ppermute(x, 'dp', [(i, i ^ 2 * r) for i in range(dp_size)])  8.5 us
    ppermute x9, waiting for transfers between devices, shift_red(): lax.ppermute(x, 'red', [(i, (i + s) % red_size) for i in range(red_size)])  8.32 us
  transfers between devices with their start and end apart: 44, of which 9 were waited for; matrix products, arithmetic and copies ran while one was open for 2% of the time, Pallas kernels for 48%

profile of v4, /device:TPU:0, one launch (start us, length us, event | category | flops | bytes accessed | tf_op | source)
XLA Modules:
  0.0 207.8 jit_solution(4628208092160435119)
XLA Ops:
  1.3 1.7 copy-done.7
  3.6 3.1 %collective-permute-start.2 = (bf16[192,512]{1,0:T(8,128)(2,1)S(1)}, bf16[192,512]{1,0:T(8,128)(2,1)S(1)}, u32[]{:S(2)}, u32[]{:S(2)}) collective-permute-start(bf16[192,512]{1,0:T(8,128)(2,1)S(1)} %shard_map.137.refs_3_), channel_id=1, source_target_pairs={{0,1},{1,2},{2,3},{3,0},{4,5},{5,6},{6,7},{7,4},{8,9},{9,10},{10,1... | collective-permute-start | bytes 589832 | tf_op jit(solution)/shard_map/ppermute | solution.py:390
  6.6 2.6 %collective-permute-start.3 = (bf16[192,512]{1,0:T(8,128)(2,1)S(1)}, bf16[192,512]{1,0:T(8,128)(2,1)S(1)}, u32[]{:S(2)}, u32[]{:S(2)}) collective-permute-start(bf16[192,512]{1,0:T(8,128)(2,1)S(1)} %shard_map.137.refs_3_), channel_id=1, source_target_pairs={{0,2},{1,3},{2,0},{3,1},{4,6},{5,7},{6,4},{7,5},{8,10},{9,11},{10,... | collective-permute-start | bytes 589832 | tf_op jit(solution)/shard_map/ppermute | solution.py:390
  13.5 1.8 copy-done.9
  15.3 8.2 %shard_map.138 = (bf16[1536,1536]{1,0:T(8,128)(2,1)}, bf16[1536,1536]{1,0:T(8,128)(2,1)}) custom-call(bf16[768,1536]{1,0:T(8,128)(2,1)S(1)} %bitcast.25, bf16[768,1536]{1,0:T(8,128)(2,1)} %collective-permute-done.refs_1_.refs_10_, f32[1,1536]{1,0:T(1,128)S(1)} %reshape.131.refs_2_.refs_4_, bf16[192,512]{1,0:T(8,128)(2,1)S(1)} %shard_map.137.refs_3_, ...), custom_call_target="tpu_custom_call" | custom-call | flops 99999997952 | bytes 200000000 | tf_op jit(solution)/shard_map/pallas_call | solution.py:452
  24.1 3.5 %collective-permute-start.7 = (bf16[192,512]{1,0:T(8,128)(2,1)S(1)}, bf16[192,512]{1,0:T(8,128)(2,1)S(1)}, u32[]{:S(2)}, u32[]{:S(2)}) collective-permute-start(bf16[192,512]{1,0:T(8,128)(2,1)S(1)} %shard_map.140.refs_18_), channel_id=1, source_target_pairs={{0,1},{1,2},{2,3},{3,0},{4,5},{5,6},{6,7},{7,4},{8,9},{9,10},{10,1... | collective-permute-start | bytes 589832 | tf_op jit(solution)/shard_map/ppermute | solution.py:390
  27.7 1.6 collective-permute-start.8
  30.2 1.5 collective-permute-start.5
  31.7 1.5 collective-permute-start.6
  34.6 6.9 %collective-permute-done.8.refs_1_.refs_4_.refs_5_ = bf16[192,512]{1,0:T(8,128)(2,1)S(1)} collective-permute-done((bf16[192,512]{1,0:T(8,128)(2,1)S(1)}, bf16[192,512]{1,0:T(8,128)(2,1)S(1)}, u32[]{:S(2)}, u32[]{:S(2)}) %collective-permute-start.8) | collective-permute-done | bytes 196640 | tf_op jit(solution)/shard_map/ppermute | solution.py:390
  42.8 4.7 %collective-permute-start.12 = (bf16[192,512]{1,0:T(8,128)(2,1)}, bf16[192,512]{1,0:T(8,128)(2,1)}, u32[]{:S(2)}, u32[]{:S(2)}) collective-permute-start(bf16[192,512]{1,0:T(8,128)(2,1)} %shard_map.142.refs_19_), channel_id=1, source_target_pairs={{0,1},{1,2},{2,3},{3,0},{4,5},{5,6},{6,7},{7,4},{8,9},{9,10},{10,1... | collective-permute-start | bytes 589832 | tf_op jit(solution)/shard_map/ppermute | solution.py:390
  47.5 2.1 %collective-permute-start.13 = (bf16[192,512]{1,0:T(8,128)(2,1)}, bf16[192,512]{1,0:T(8,128)(2,1)}, u32[]{:S(2)}, u32[]{:S(2)}) collective-permute-start(bf16[192,512]{1,0:T(8,128)(2,1)} %shard_map.142.refs_19_), channel_id=1, source_target_pairs={{0,2},{1,3},{2,0},{3,1},{4,6},{5,7},{6,4},{7,5},{8,10},{9,11},{10,... | collective-permute-start | bytes 589832 | tf_op jit(solution)/shard_map/ppermute | solution.py:390
  51.4 1.5 collective-permute-start.10
  52.9 1.5 collective-permute-start.11
  54.7 17.3 %shard_map.143 = (bf16[768,768]{1,0:T(8,128)(2,1)}, bf16[768,768]{1,0:T(8,128)(2,1)}, bf16[4,96,512]{2,1,0:T(8,128)(2,1)S(1)}, bf16[4,96,512]{2,1,0:T(8,128)(2,1...) custom-call(s32[4]{0:T(128)S(1)} %pad_add_fusion.refs_0_.idx, ...), custom_call_target="tpu_custom_call" | custom-call | flops 99999997952 | bytes 200000000 | tf_op jit(solution)/shard_map/pallas_call | solution.py:520
  73.1 2.4 %collective-permute-start.19 = (bf16[4,96,512]{2,1,0:T(8,128)(2,1)}, bf16[4,96,512]{2,1,0:T(8,128)(2,1)}, u32[]{:S(2)}, u32[]{:S(2)}) collective-permute-start(bf16[4,96,512]{2,1,0:T(8,128)(2,1)} %get-tuple-element.61), channel_id=1, source_target_pairs={{0,24},{4,28},{8,16},{12,20},{16,8},{20,12},{24,0},{28,4},{1,25},{... | collective-permute-start | bytes 1179656 | tf_op jit(solution)/shard_map/ppermute | solution.py:387
  75.6 2.0 shard_map.144
  78.7 17.5 %shard_map.145 = (bf16[768,768]{1,0:T(8,128)(2,1)}, bf16[768,768]{1,0:T(8,128)(2,1)}, bf16[4,96,512]{2,1,0:T(8,128)(2,1)S(1)}, bf16[4,96,512]{2,1,0:T(8,128)(2,1...) custom-call(s32[4]{0:T(128)S(1)} %pad_add_fusion.refs_0_.idx, ...), custom_call_target="tpu_custom_call", output_to_operand_aliasing={{0}: (17, {}), {1}: (18, {})} | custom-call | flops 99999997952 | bytes 200000000 | tf_op jit(solution)/shard_map/pallas_call | solution.py:520
  97.0 1.5 collective-permute-start.20
  98.5 1.5 collective-permute-start.21
  100.5 2.2 %shard_map.146.refs_19_ = bf16[4,96,512]{2,1,0:T(8,128)(2,1)} custom-call(bf16[4,96,512]{2,1,0:T(8,128)(2,1)S(1)} %get-tuple-element.58.refs_0_, bf16[4,96,512]{2,1,0:T(8,128)(2,1)} %collective-permute-done.17.refs_1_, bf16[4,96,512]{2,1,0:T(8,128)(2,1)} %collective-permute-done.18.refs_2_, bf16[4,96,512]{2,1,0:T(8,128)(2,1)} %collective-permute-done.19.refs_3_, ...), custom_call_target="tpu_custom_call" | custom-call | flops 99999997952 | bytes 200000000 | tf_op jit(solution)/shard_map/pallas_call | solution.py:561
  102.7 4.3 %all-to-all-start = ((bf16[4,96,512]{2,1,0:T(8,128)(2,1)}), bf16[4,96,512]{2,1,0:T(8,128)(2,1)}, u32[]{:S(2)}, u32[]{:S(2)}) async-start(bf16[4,96,512]{2,1,0:T(8,128)(2,1)} %shard_map.146.refs_19_), calls=%async_computation | async-start | bytes 786432 | tf_op jit(solution)/shard_map/all_to_all | solution.py:575
  107.0 17.7 %shard_map.147 = (bf16[768,768]{1,0:T(8,128)(2,1)}, bf16[768,768]{1,0:T(8,128)(2,1)}, bf16[4,96,512]{2,1,0:T(8,128)(2,1)S(1)}, bf16[4,96,512]{2,1,0:T(8,128)(2,1...) custom-call(s32[4]{0:T(128)S(1)} %pad_add_fusion.refs_0_.idx, ...), custom_call_target="tpu_custom_call", output_to_operand_aliasing={{0}: (17, {}), {1}: (18, {})} | custom-call | flops 99999997952 | bytes 200000000 | tf_op jit(solution)/shard_map/pallas_call | solution.py:520
  124.8 1.6 collective-permute-start.25
  126.3 1.5 collective-permute-start.26
  129.3 2.3 %shard_map.148.refs_7_ = bf16[4,96,512]{2,1,0:T(8,128)(2,1)} custom-call(bf16[4,96,512]{2,1,0:T(8,128)(2,1)S(1)} %copy-done.28, bf16[4,96,512]{2,1,0:T(8,128)(2,1)} %collective-permute-done.20.refs_1_, bf16[4,96,512]{2,1,0:T(8,128)(2,1)} %collective-permute-done.21.refs_2_, bf16[4,96,512]{2,1,0:T(8,128)(2,1)} %collective-permute-done.22.refs_3_, ...), custom_call_target="tpu_custom_call" | custom-call | flops 99999997952 | bytes 200000000 | tf_op jit(solution)/shard_map/pallas_call | solution.py:561
  131.6 5.1 %all-to-all-start.1 = ((bf16[4,96,512]{2,1,0:T(8,128)(2,1)}), bf16[4,96,512]{2,1,0:T(8,128)(2,1)S(1)}, u32[]{:S(2)}, u32[]{:S(2)}) async-start(bf16[4,96,512]{2,1,0:T(8,128)(2,1)} %shard_map.148.refs_7_), calls=%async_computation.1 | async-start | bytes 786432 | tf_op jit(solution)/shard_map/all_to_all | solution.py:575
  136.7 1.4 copy-done.23
  138.1 1.4 copy-done.24
  139.5 7.7 %shard_map.149.refs_3_ = bf16[768,1536]{1,0:T(8,128)(2,1)} custom-call(bf16[1536,512]{1,0:T(8,128)(2,1)S(1)} %copy-done.24, bf16[1536,512]{1,0:T(8,128)(2,1)S(1)} %copy-done.23, bf16[1536,512]{1,0:T(8,128)(2,1)S(1)} %copy-done.22, bf16[1536,512]{1,0:T(8,128)(2,1)} %get-tuple-element.64.refs_3_.refs_11_, ...), custom_call_target="tpu_custom_call" | custom-call | flops 99999997952 | bytes 200000000 | tf_op jit(solution)/shard_map/pallas_call | solution.py:664
  147.4 1.6 all-to-all-done.1.refs_2_
  149.0 1.7 copy-done.10
  151.8 2.3 %shard_map.151.refs_14_ = bf16[4,96,512]{2,1,0:T(8,128)(2,1)} custom-call(bf16[4,96,512]{2,1,0:T(8,128)(2,1)S(1)} %get-tuple-element.74.refs_0_, bf16[4,96,512]{2,1,0:T(8,128)(2,1)} %collective-permute-done.25.refs_1_, bf16[4,96,512]{2,1,0:T(8,128)(2,1)} %collective-permute-done.26.refs_2_, bf16[4,96,512]{2,1,0:T(8,128)(2,1)} %collective-permute-done.27.refs_3_, ...), custom_call_target="tpu_custom_call" | custom-call | flops 99999997952 | bytes 200000000 | tf_op jit(solution)/shard_map/pallas_call | solution.py:561
  154.1 3.7 %all-to-all-start.2 = ((bf16[4,96,512]{2,1,0:T(8,128)(2,1)}), bf16[4,96,512]{2,1,0:T(8,128)(2,1)S(1)}, u32[]{:S(2)}, u32[]{:S(2)}) async-start(bf16[4,96,512]{2,1,0:T(8,128)(2,1)} %shard_map.151.refs_14_), calls=%async_computation.2 | async-start | bytes 786432 | tf_op jit(solution)/shard_map/all_to_all | solution.py:575
  159.2 13.3 %shard_map.152 = (bf16[768,1536]{1,0:T(8,128)(2,1)}, bf16[768,1536]{1,0:T(8,128)(2,1)}, f32[8,1536]{1,0:T(8,128)S(1)}) custom-call(s32[4]{0:T(128)S(1)} %pad_add_fusion.refs_0_.idx, bf16[768,1536]{1,0:T(8,128)(2,1)} %bitcast.24, bf16[768,1536]{1,0:T(8,128)(2,1)} %bitcast.30, f32[1536,128]{1,0:T(8,128)S(1)} %broadcast_in_dim.2.refs_13_.refs_3_, ...), custom_call_target="tpu_custom_call" | custom-call | flops 99999997952 | bytes 200000000 | tf_op jit(solution)/shard_map/pallas_call | solution.py:680
  172.5 1.5 collective-permute-start.36
  174.6 1.5 collective-permute-start.32
  176.1 1.4 collective-permute-start.33
  178.8 1.6 collective-permute-start.37
  180.4 2.6 %collective-permute-done.31.refs_1_ = bf16[2,96,512]{2,1,0:T(8,128)(2,1)S(1)} collective-permute-done((bf16[2,96,512]{2,1,0:T(8,128)(2,1)S(1)}, bf16[2,96,512]{2,1,0:T(8,128)(2,1)S(1)}, u32[]{:S(2)}, u32[]{:S(2)}) %collective-permute-start.31) | collective-permute-done | bytes 196640 | tf_op jit(solution)/shard_map/ppermute | solution.py:387
  183.0 4.3 %collective-permute-done.33.refs_3_ = bf16[2,96,512]{2,1,0:T(8,128)(2,1)S(1)} collective-permute-done((bf16[2,96,512]{2,1,0:T(8,128)(2,1)S(1)}, bf16[2,96,512]{2,1,0:T(8,128)(2,1)S(1)}, u32[]{:S(2)}, u32[]{:S(2)}) %collective-permute-start.33) | collective-permute-done | bytes 196640 | tf_op jit(solution)/shard_map/ppermute | solution.py:387
  187.8 1.8 collective-permute-start.38
  189.7 1.5 collective-permute-start.28
  191.2 1.5 collective-permute-start.29
  193.3 2.7 %collective-permute-start.39 = (f32[33,768]{1,0:T(8,128)S(1)}, f32[33,768]{1,0:T(8,128)S(1)}, u32[]{:S(2)}, u32[]{:S(2)}) collective-permute-start(f32[33,768]{1,0:T(8,128)S(1)} %add.53), channel_id=1, source_target_pairs={{0,2},{1,3},{2,0},{3,1},{4,6},{5,7},{6,4},{7,5},{8,10},{9,11},{10,... | collective-permute-start | bytes 304136 | tf_op jit(solution)/shard_map/ppermute | solution.py:737
  196.0 3.8 %shard_map.155.refs_4_.rest_0_ = f32[384,3072]{1,0:T(8,128)} custom-call(s32[4]{0:T(128)S(1)} %pad_add_fusion.refs_0_.idx, bf16[4,2,96,512]{3,2,1,0:T(8,128)(2,1)S(1)} %shard_map.154.mine, bf16[4,2,96,512]{3,2,1,0:T(8,128)(2,1)S(1)} %collective-permute-done.34.sib), custom_call_target="tpu_custom_call" | custom-call | flops 99999997952 | bytes 200000000 | tf_op jit(solution)/shard_map/pallas_call | solution.py:611
  199.8 2.3 %copy-done.2 = f32[384,3072]{1,0:T(8,128)S(1)} copy-done((f32[384,3072]{1,0:T(8,128)S(1)}, f32[384,3072]{1,0:T(8,128)}, u32[]{:S(2)}) %copy-start.2) | copy-done | bytes 4718616
  204.0 2.3 %shard_map.157 = f32[384,3072]{1,0:T(8,128)} custom-call(s32[4]{0:T(128)S(1)} %pad_add_fusion.refs_0_.idx, bf16[4,1,96,512]{3,2,1,0:T(8,128)(2,1)S(1)} %shard_map.156.mine, bf16[4,1,96,512]{3,2,1,0:T(8,128)(2,1)S(1)} %collective-permute-done.35.sib, f32[384,3072]{1,0:T(8,128)} %shard_map.155.refs_4_.rest_0_), custom_call_target="tpu_custom_call", output_to_operand_aliasing={{}: (3, {})} | custom-call | flops 1000000 | bytes 1000000 | tf_op jit(solution)/shard_map/pallas_call | solution.py:611
  (153 shorter events, 24.4 us)
Async XLA Ops:
  0.6 12.8 %collective-permute-start = (bf16[768,1536]{1,0:T(8,128)(2,1)}, bf16[768,1536]{1,0:T(8,128)(2,1)}, u32[]{:S(2)}, u32[]{:S(2)}) collective-permute-start(bf16[768,1536]{1,0:T(8,128)(2,1)} %bitcast.20), channel_id=1, source_target_pairs={{0,4},{4,0},{8,12},{12,8},{16,20},{20,16},{24,28},{28,24},{1,5},{5... | collective-permute-start | bytes 7077896 | tf_op jit(solution)/shard_map/ppermute | solution.py:384
  1.2 12.3 %collective-permute-start.1 = (bf16[768,1536]{1,0:T(8,128)(2,1)}, bf16[768,1536]{1,0:T(8,128)(2,1)}, u32[]{:S(2)}, u32[]{:S(2)}) collective-permute-start(bf16[768,1536]{1,0:T(8,128)(2,1)} %bitcast.26), channel_id=1, source_target_pairs={{0,4},{4,0},{8,12},{12,8},{16,20},{20,16},{24,28},{28,24},{1,5},{5... | collective-permute-start | bytes 7077896 | tf_op jit(solution)/shard_map/ppermute | solution.py:384
  3.6 19.9 %collective-permute-start.2 = (bf16[192,512]{1,0:T(8,128)(2,1)S(1)}, bf16[192,512]{1,0:T(8,128)(2,1)S(1)}, u32[]{:S(2)}, u32[]{:S(2)}) collective-permute-start(bf16[192,512]{1,0:T(8,128)(2,1)S(1)} %shard_map.137.refs_3_), channel_id=1, source_target_pairs={{0,1},{1,2},{2,3},{3,0},{4,5},{5,6},{6,7},{7,4},{8,9},{9,10},{10,1... | collective-permute-start | bytes 589832 | tf_op jit(solution)/shard_map/ppermute | solution.py:390
  6.6 16.9 %collective-permute-start.3 = (bf16[192,512]{1,0:T(8,128)(2,1)S(1)}, bf16[192,512]{1,0:T(8,128)(2,1)S(1)}, u32[]{:S(2)}, u32[]{:S(2)}) collective-permute-start(bf16[192,512]{1,0:T(8,128)(2,1)S(1)} %shard_map.137.refs_3_), channel_id=1, source_target_pairs={{0,2},{1,3},{2,0},{3,1},{4,6},{5,7},{6,4},{7,5},{8,10},{9,11},{10,... | collective-permute-start | bytes 589832 | tf_op jit(solution)/shard_map/ppermute | solution.py:390
  9.2 14.3 %collective-permute-start.4 = (bf16[192,512]{1,0:T(8,128)(2,1)S(1)}, bf16[192,512]{1,0:T(8,128)(2,1)S(1)}, u32[]{:S(2)}, u32[]{:S(2)}) collective-permute-start(bf16[192,512]{1,0:T(8,128)(2,1)S(1)} %shard_map.137.refs_3_), channel_id=1, source_target_pairs={{0,3},{1,0},{2,1},{3,2},{4,7},{5,4},{6,5},{7,6},{8,11},{9,8},{10,9... | collective-permute-start | bytes 589832 | tf_op jit(solution)/shard_map/ppermute | solution.py:390
  24.1 10.5 %collective-permute-start.7 = (bf16[192,512]{1,0:T(8,128)(2,1)S(1)}, bf16[192,512]{1,0:T(8,128)(2,1)S(1)}, u32[]{:S(2)}, u32[]{:S(2)}) collective-permute-start(bf16[192,512]{1,0:T(8,128)(2,1)S(1)} %shard_map.140.refs_18_), channel_id=1, source_target_pairs={{0,1},{1,2},{2,3},{3,0},{4,5},{5,6},{6,7},{7,4},{8,9},{9,10},{10,1... | collective-permute-start | bytes 589832 | tf_op jit(solution)/shard_map/ppermute | solution.py:390
  27.7 13.9 %collective-permute-start.8 = (bf16[192,512]{1,0:T(8,128)(2,1)S(1)}, bf16[192,512]{1,0:T(8,128)(2,1)S(1)}, u32[]{:S(2)}, u32[]{:S(2)}) collective-permute-start(bf16[192,512]{1,0:T(8,128)(2,1)S(1)} %shard_map.140.refs_18_), channel_id=1, source_target_pairs={{0,2},{1,3},{2,0},{3,1},{4,6},{5,7},{6,4},{7,5},{8,10},{9,11},{10,... | collective-permute-start | bytes 589832 | tf_op jit(solution)/shard_map/ppermute | solution.py:390
  29.3 12.3 %collective-permute-start.9 = (bf16[192,512]{1,0:T(8,128)(2,1)S(1)}, bf16[192,512]{1,0:T(8,128)(2,1)S(1)}, u32[]{:S(2)}, u32[]{:S(2)}) collective-permute-start(bf16[192,512]{1,0:T(8,128)(2,1)S(1)} %shard_map.140.refs_18_), channel_id=1, source_target_pairs={{0,3},{1,0},{2,1},{3,2},{4,7},{5,4},{6,5},{7,6},{8,11},{9,8},{10,9... | collective-permute-start | bytes 589832 | tf_op jit(solution)/shard_map/ppermute | solution.py:390
  30.2 20.3 %collective-permute-start.5 = (bf16[3,192,256]{2,1,0:T(8,128)(2,1)S(1)}, bf16[3,192,256]{2,1,0:T(8,128)(2,1)S(1)}, u32[]{:S(2)}, u32[]{:S(2)}) collective-permute-start(bf16[3,192,256]{2,1,0:T(8,128)(2,1)S(1)} %get-tuple-element.45), channel_id=1, source_target_pairs={{0,8},{4,12},{8,0},{12,4},{16,24},{20,28},{24,16},{28,20},{1,9},{5... | collective-permute-start | bytes 884744 | tf_op jit(solution)/shard_map/ppermute | solution.py:387
  31.7 18.8 %collective-permute-start.6 = (bf16[3,192,256]{2,1,0:T(8,128)(2,1)S(1)}, bf16[3,192,256]{2,1,0:T(8,128)(2,1)S(1)}, u32[]{:S(2)}, u32[]{:S(2)}) collective-permute-start(bf16[3,192,256]{2,1,0:T(8,128)(2,1)S(1)} %get-tuple-element.46), channel_id=1, source_target_pairs={{0,16},{4,20},{8,24},{12,28},{16,0},{20,4},{24,8},{28,12},{1,17},{... | collective-permute-start | bytes 884744 | tf_op jit(solution)/shard_map/ppermute | solution.py:387
  42.8 29.2 %collective-permute-start.12 = (bf16[192,512]{1,0:T(8,128)(2,1)}, bf16[192,512]{1,0:T(8,128)(2,1)}, u32[]{:S(2)}, u32[]{:S(2)}) collective-permute-start(bf16[192,512]{1,0:T(8,128)(2,1)} %shard_map.142.refs_19_), channel_id=1, source_target_pairs={{0,1},{1,2},{2,3},{3,0},{4,5},{5,6},{6,7},{7,4},{8,9},{9,10},{10,1... | collective-permute-start | bytes 589832 | tf_op jit(solution)/shard_map/ppermute | solution.py:390
  47.5 25.1 %collective-permute-start.13 = (bf16[192,512]{1,0:T(8,128)(2,1)}, bf16[192,512]{1,0:T(8,128)(2,1)}, u32[]{:S(2)}, u32[]{:S(2)}) collective-permute-start(bf16[192,512]{1,0:T(8,128)(2,1)} %shard_map.142.refs_19_), channel_id=1, source_target_pairs={{0,2},{1,3},{2,0},{3,1},{4,6},{5,7},{6,4},{7,5},{8,10},{9,11},{10,... | collective-permute-start | bytes 589832 | tf_op jit(solution)/shard_map/ppermute | solution.py:390
  49.6 23.5 %collective-permute-start.14 = (bf16[192,512]{1,0:T(8,128)(2,1)}, bf16[192,512]{1,0:T(8,128)(2,1)}, u32[]{:S(2)}, u32[]{:S(2)}) collective-permute-start(bf16[192,512]{1,0:T(8,128)(2,1)} %shard_map.142.refs_19_), channel_id=1, source_target_pairs={{0,3},{1,0},{2,1},{3,2},{4,7},{5,4},{6,5},{7,6},{8,11},{9,8},{10,9... | collective-permute-start | bytes 589832 | tf_op jit(solution)/shard_map/ppermute | solution.py:390
  51.4 26.2 %collective-permute-start.10 = (bf16[3,192,256]{2,1,0:T(8,128)(2,1)}, bf16[3,192,256]{2,1,0:T(8,128)(2,1)}, u32[]{:S(2)}, u32[]{:S(2)}) collective-permute-start(bf16[3,192,256]{2,1,0:T(8,128)(2,1)} %get-tuple-element.47.refs_17_), channel_id=1, source_target_pairs={{0,8},{4,12},{8,0},{12,4},{16,24},{20,28},{24,16},{28,20},{1,9},{5... | collective-permute-start | bytes 884744 | tf_op jit(solution)/shard_map/ppermute | solution.py:387
  52.9 25.3 %collective-permute-start.11 = (bf16[3,192,256]{2,1,0:T(8,128)(2,1)}, bf16[3,192,256]{2,1,0:T(8,128)(2,1)}, u32[]{:S(2)}, u32[]{:S(2)}) collective-permute-start(bf16[3,192,256]{2,1,0:T(8,128)(2,1)} %get-tuple-element.49), channel_id=1, source_target_pairs={{0,16},{4,20},{8,24},{12,28},{16,0},{20,4},{24,8},{28,12},{1,17},{... | collective-permute-start | bytes 884744 | tf_op jit(solution)/shard_map/ppermute | solution.py:387
  72.0 25.0 %collective-permute-start.17 = (bf16[4,96,512]{2,1,0:T(8,128)(2,1)}, bf16[4,96,512]{2,1,0:T(8,128)(2,1)}, u32[]{:S(2)}, u32[]{:S(2)}) collective-permute-start(bf16[4,96,512]{2,1,0:T(8,128)(2,1)} %get-tuple-element.59), channel_id=1, source_target_pairs={{0,8},{4,12},{8,0},{12,4},{16,24},{20,28},{24,16},{28,20},{1,9},{5... | collective-permute-start | bytes 1179656 | tf_op jit(solution)/shard_map/ppermute | solution.py:387
  72.6 25.9 %collective-permute-start.18 = (bf16[4,96,512]{2,1,0:T(8,128)(2,1)}, bf16[4,96,512]{2,1,0:T(8,128)(2,1)}, u32[]{:S(2)}, u32[]{:S(2)}) collective-permute-start(bf16[4,96,512]{2,1,0:T(8,128)(2,1)} %get-tuple-element.60), channel_id=1, source_target_pairs={{0,16},{4,20},{8,24},{12,28},{16,0},{20,4},{24,8},{28,12},{1,17},{... | collective-permute-start | bytes 1179656 | tf_op jit(solution)/shard_map/ppermute | solution.py:387
  73.1 26.9 %collective-permute-start.19 = (bf16[4,96,512]{2,1,0:T(8,128)(2,1)}, bf16[4,96,512]{2,1,0:T(8,128)(2,1)}, u32[]{:S(2)}, u32[]{:S(2)}) collective-permute-start(bf16[4,96,512]{2,1,0:T(8,128)(2,1)} %get-tuple-element.61), channel_id=1, source_target_pairs={{0,24},{4,28},{8,16},{12,20},{16,8},{20,12},{24,0},{28,4},{1,25},{... | collective-permute-start | bytes 1179656 | tf_op jit(solution)/shard_map/ppermute | solution.py:387
  77.6 29.4 %collective-permute-start.15 = (bf16[3,192,256]{2,1,0:T(8,128)(2,1)}, bf16[3,192,256]{2,1,0:T(8,128)(2,1)}, u32[]{:S(2)}, u32[]{:S(2)}) collective-permute-start(bf16[3,192,256]{2,1,0:T(8,128)(2,1)} %get-tuple-element.53.refs_19_), channel_id=1, source_target_pairs={{0,8},{4,12},{8,0},{12,4},{16,24},{20,28},{24,16},{28,20},{1,9},{5... | collective-permute-start | bytes 884744 | tf_op jit(solution)/shard_map/ppermute | solution.py:387
  78.2 28.9 %collective-permute-start.16 = (bf16[3,192,256]{2,1,0:T(8,128)(2,1)}, bf16[3,192,256]{2,1,0:T(8,128)(2,1)}, u32[]{:S(2)}, u32[]{:S(2)}) collective-permute-start(bf16[3,192,256]{2,1,0:T(8,128)(2,1)} %get-tuple-element.55), channel_id=1, source_target_pairs={{0,16},{4,20},{8,24},{12,28},{16,0},{20,4},{24,8},{28,12},{1,17},{... | collective-permute-start | bytes 884744 | tf_op jit(solution)/shard_map/ppermute | solution.py:387
  97.0 31.8 %collective-permute-start.20 = (bf16[4,96,512]{2,1,0:T(8,128)(2,1)}, bf16[4,96,512]{2,1,0:T(8,128)(2,1)}, u32[]{:S(2)}, u32[]{:S(2)}) collective-permute-start(bf16[4,96,512]{2,1,0:T(8,128)(2,1)} %get-tuple-element.69), channel_id=1, source_target_pairs={{0,8},{4,12},{8,0},{12,4},{16,24},{20,28},{24,16},{28,20},{1,9},{5... | collective-permute-start | bytes 1179656 | tf_op jit(solution)/shard_map/ppermute | solution.py:387
  98.5 30.8 %collective-permute-start.21 = (bf16[4,96,512]{2,1,0:T(8,128)(2,1)}, bf16[4,96,512]{2,1,0:T(8,128)(2,1)}, u32[]{:S(2)}, u32[]{:S(2)}) collective-permute-start(bf16[4,96,512]{2,1,0:T(8,128)(2,1)} %get-tuple-element.70), channel_id=1, source_target_pairs={{0,16},{4,20},{8,24},{12,28},{16,0},{20,4},{24,8},{28,12},{1,17},{... | collective-permute-start | bytes 1179656 | tf_op jit(solution)/shard_map/ppermute | solution.py:387
  100.0 29.3 %collective-permute-start.22 = (bf16[4,96,512]{2,1,0:T(8,128)(2,1)}, bf16[4,96,512]{2,1,0:T(8,128)(2,1)}, u32[]{:S(2)}, u32[]{:S(2)}) collective-permute-start(bf16[4,96,512]{2,1,0:T(8,128)(2,1)} %get-tuple-element.71), channel_id=1, source_target_pairs={{0,24},{4,28},{8,16},{12,20},{16,8},{20,12},{24,0},{28,4},{1,25},{... | collective-permute-start | bytes 1179656 | tf_op jit(solution)/shard_map/ppermute | solution.py:387
  102.7 28.9 %all-to-all-start = ((bf16[4,96,512]{2,1,0:T(8,128)(2,1)}), bf16[4,96,512]{2,1,0:T(8,128)(2,1)}, u32[]{:S(2)}, u32[]{:S(2)}) async-start(bf16[4,96,512]{2,1,0:T(8,128)(2,1)} %shard_map.146.refs_19_), calls=%async_computation | async-start | bytes 786432 | tf_op jit(solution)/shard_map/all_to_all | solution.py:575
  107.0 20.8 %copy-start.4 = (f32[96,256]{1,0:T(8,128)S(1)}, f32[96,256]{1,0:T(8,128)}, u32[]{:S(2)}) copy-start(f32[96,256]{1,0:T(8,128)} %copy-done.3) | copy-start | bytes 294916
  107.0 20.8 %copy-start.32 = (f32[31,96]{1,0:T(8,128)S(1)}, f32[31,96]{1,0:T(8,128)}, u32[]{:S(2)}) copy-start(f32[31,96]{1,0:T(8,128)} %constant.71.clone) | copy-start | bytes 35716
  107.0 22.2 %copy-start.28 = (bf16[4,96,512]{2,1,0:T(8,128)(2,1)S(1)}, bf16[4,96,512]{2,1,0:T(8,128)(2,1)}, u32[]{:S(2)}) copy-start(bf16[4,96,512]{2,1,0:T(8,128)(2,1)} %copy-done.27) | copy-start | bytes 1179652
  124.8 27.0 %collective-permute-start.25 = (bf16[4,96,512]{2,1,0:T(8,128)(2,1)}, bf16[4,96,512]{2,1,0:T(8,128)(2,1)}, u32[]{:S(2)}, u32[]{:S(2)}) collective-permute-start(bf16[4,96,512]{2,1,0:T(8,128)(2,1)} %get-tuple-element.75), channel_id=1, source_target_pairs={{0,8},{4,12},{8,0},{12,4},{16,24},{20,28},{24,16},{28,20},{1,9},{5... | collective-permute-start | bytes 1179656 | tf_op jit(solution)/shard_map/ppermute | solution.py:387
  126.3 25.5 %collective-permute-start.26 = (bf16[4,96,512]{2,1,0:T(8,128)(2,1)}, bf16[4,96,512]{2,1,0:T(8,128)(2,1)}, u32[]{:S(2)}, u32[]{:S(2)}) collective-permute-start(bf16[4,96,512]{2,1,0:T(8,128)(2,1)} %get-tuple-element.76), channel_id=1, source_target_pairs={{0,16},{4,20},{8,24},{12,28},{16,0},{20,4},{24,8},{28,12},{1,17},{... | collective-permute-start | bytes 1179656 | tf_op jit(solution)/shard_map/ppermute | solution.py:387
  128.8 23.0 %collective-permute-start.27 = (bf16[4,96,512]{2,1,0:T(8,128)(2,1)}, bf16[4,96,512]{2,1,0:T(8,128)(2,1)}, u32[]{:S(2)}, u32[]{:S(2)}) collective-permute-start(bf16[4,96,512]{2,1,0:T(8,128)(2,1)} %get-tuple-element.77), channel_id=1, source_target_pairs={{0,24},{4,28},{8,16},{12,20},{16,8},{20,12},{24,0},{28,4},{1,25},{... | collective-permute-start | bytes 1179656 | tf_op jit(solution)/shard_map/ppermute | solution.py:387
  129.3 28.6 %collective-permute-start.24 = (bf16[768,768]{1,0:T(8,128)(2,1)}, bf16[768,768]{1,0:T(8,128)(2,1)}, u32[]{:S(2)}, u32[]{:S(2)}) collective-permute-start(bf16[768,768]{1,0:T(8,128)(2,1)} %get-tuple-element.73), channel_id=1, source_target_pairs={{0,4},{4,0},{8,12},{12,8},{16,20},{20,16},{24,28},{28,24},{1,5},{5... | collective-permute-start | bytes 3538952 | tf_op jit(solution)/shard_map/ppermute | solution.py:384
  131.6 17.4 %all-to-all-start.1 = ((bf16[4,96,512]{2,1,0:T(8,128)(2,1)}), bf16[4,96,512]{2,1,0:T(8,128)(2,1)S(1)}, u32[]{:S(2)}, u32[]{:S(2)}) async-start(bf16[4,96,512]{2,1,0:T(8,128)(2,1)} %shard_map.148.refs_7_), calls=%async_computation.1 | async-start | bytes 786432 | tf_op jit(solution)/shard_map/all_to_all | solution.py:575
  147.2 10.7 %collective-permute-start.23 = (bf16[768,1536]{1,0:T(8,128)(2,1)}, bf16[768,1536]{1,0:T(8,128)(2,1)}, u32[]{:S(2)}, u32[]{:S(2)}) collective-permute-start(bf16[768,1536]{1,0:T(8,128)(2,1)} %shard_map.149.refs_3_), channel_id=1, source_target_pairs={{0,4},{4,0},{8,12},{12,8},{16,20},{20,16},{24,28},{28,24},{1,5},{5... | collective-permute-start | bytes 7077896 | tf_op jit(solution)/shard_map/ppermute | solution.py:384
  154.1 35.5 %all-to-all-start.2 = ((bf16[4,96,512]{2,1,0:T(8,128)(2,1)}), bf16[4,96,512]{2,1,0:T(8,128)(2,1)S(1)}, u32[]{:S(2)}, u32[]{:S(2)}) async-start(bf16[4,96,512]{2,1,0:T(8,128)(2,1)} %shard_map.151.refs_14_), calls=%async_computation.2 | async-start | bytes 786432 | tf_op jit(solution)/shard_map/all_to_all | solution.py:575
  159.2 13.3 %copy-start.29 = (f32[31,768]{1,0:T(8,128)S(1)}, f32[31,768]{1,0:T(8,128)}, u32[]{:S(2)}) copy-start(f32[31,768]{1,0:T(8,128)} %fusion) | copy-start | bytes 285700
  172.5 6.2 %collective-permute-start.36 = (f32[33,768]{1,0:T(8,128)S(1)}, f32[33,768]{1,0:T(8,128)S(1)}, u32[]{:S(2)}, u32[]{:S(2)}) collective-permute-start(f32[33,768]{1,0:T(8,128)S(1)} %pad_maximum_fusion.1), channel_id=1, source_target_pairs={{0,8},{4,12},{8,0},{12,4},{16,24},{20,28},{24,16},{28,20},{1,9},{5... | collective-permute-start | bytes 304136 | tf_op jit(solution)/shard_map/ppermute | solution.py:387
  174.0 8.9 %collective-permute-start.31 = (bf16[2,96,512]{2,1,0:T(8,128)(2,1)S(1)}, bf16[2,96,512]{2,1,0:T(8,128)(2,1)S(1)}, u32[]{:S(2)}, u32[]{:S(2)}) collective-permute-start(bf16[2,96,512]{2,1,0:T(8,128)(2,1)S(1)} %shard_map.150.refs_4_.refs_0_), channel_id=1, source_target_pairs={{0,8},{4,12},{8,0},{12,4},{16,24},{20,28},{24,16},{28,20},{1,9},{5... | collective-permute-start | bytes 589832 | tf_op jit(solution)/shard_map/ppermute | solution.py:387
  174.6 8.4 %collective-permute-start.32 = (bf16[2,96,512]{2,1,0:T(8,128)(2,1)S(1)}, bf16[2,96,512]{2,1,0:T(8,128)(2,1)S(1)}, u32[]{:S(2)}, u32[]{:S(2)}) collective-permute-start(bf16[2,96,512]{2,1,0:T(8,128)(2,1)S(1)} %shard_map.150.refs_4_.refs_0_), channel_id=1, source_target_pairs={{0,16},{4,20},{8,24},{12,28},{16,0},{20,4},{24,8},{28,12},{1,17},{... | collective-permute-start | bytes 589832 | tf_op jit(solution)/shard_map/ppermute | solution.py:387
  176.1 11.2 %collective-permute-start.33 = (bf16[2,96,512]{2,1,0:T(8,128)(2,1)S(1)}, bf16[2,96,512]{2,1,0:T(8,128)(2,1)S(1)}, u32[]{:S(2)}, u32[]{:S(2)}) collective-permute-start(bf16[2,96,512]{2,1,0:T(8,128)(2,1)S(1)} %shard_map.150.refs_4_.refs_0_), channel_id=1, source_target_pairs={{0,24},{4,28},{8,16},{12,20},{16,8},{20,12},{24,0},{28,4},{1,25},{... | collective-permute-start | bytes 589832 | tf_op jit(solution)/shard_map/ppermute | solution.py:387
  178.8 9.0 %collective-permute-start.37 = (f32[33,768]{1,0:T(8,128)S(1)}, f32[33,768]{1,0:T(8,128)S(1)}, u32[]{:S(2)}, u32[]{:S(2)}) collective-permute-start(f32[33,768]{1,0:T(8,128)S(1)} %fusion.7), channel_id=1, source_target_pairs={{0,16},{4,20},{8,24},{12,28},{16,0},{20,4},{24,8},{28,12},{1,17},{... | collective-permute-start | bytes 304136 | tf_op jit(solution)/shard_map/ppermute | solution.py:387
  187.4 8.6 %collective-permute-start.34 = (bf16[4,2,96,512]{3,2,1,0:T(8,128)(2,1)S(1)}, bf16[4,2,96,512]{3,2,1,0:T(8,128)(2,1)S(1)}, u32[]{:S(2)}, u32[]{:S(2)}) collective-permute-start(bf16[4,2,96,512]{3,2,1,0:T(8,128)(2,1)S(1)} %shard_map.154.mine), channel_id=1, source_target_pairs={{0,4},{4,0},{8,12},{12,8},{16,20},{20,16},{24,28},{28,24},{1,5},{5... | collective-permute-start | bytes 2359304 | tf_op jit(solution)/shard_map/ppermute | solution.py:384
  187.8 5.5 %collective-permute-start.38 = (f32[33,768]{1,0:T(8,128)S(1)}, f32[33,768]{1,0:T(8,128)S(1)}, u32[]{:S(2)}, u32[]{:S(2)}) collective-permute-start(f32[33,768]{1,0:T(8,128)S(1)} %add.52), channel_id=1, source_target_pairs={{0,1},{1,0},{2,3},{3,2},{4,5},{5,4},{6,7},{7,6},{8,9},{9,8},{10,11... | collective-permute-start | bytes 304136 | tf_op jit(solution)/shard_map/ppermute | solution.py:737
  189.7 10.2 %collective-permute-start.28 = (bf16[1,96,512]{2,1,0:T(8,128)(2,1)S(1)}, bf16[1,96,512]{2,1,0:T(8,128)(2,1)S(1)}, u32[]{:S(2)}, u32[]{:S(2)}) collective-permute-start(bf16[1,96,512]{2,1,0:T(8,128)(2,1)S(1)} %shard_map.153.refs_0_), channel_id=1, source_target_pairs={{0,8},{4,12},{8,0},{12,4},{16,24},{20,28},{24,16},{28,20},{1,9},{5... | collective-permute-start | bytes 294920 | tf_op jit(solution)/shard_map/ppermute | solution.py:387
  191.2 8.6 %collective-permute-start.29 = (bf16[1,96,512]{2,1,0:T(8,128)(2,1)S(1)}, bf16[1,96,512]{2,1,0:T(8,128)(2,1)S(1)}, u32[]{:S(2)}, u32[]{:S(2)}) collective-permute-start(bf16[1,96,512]{2,1,0:T(8,128)(2,1)S(1)} %shard_map.153.refs_0_), channel_id=1, source_target_pairs={{0,16},{4,20},{8,24},{12,28},{16,0},{20,4},{24,8},{28,12},{1,17},{... | collective-permute-start | bytes 294920 | tf_op jit(solution)/shard_map/ppermute | solution.py:387
  192.7 7.1 %collective-permute-start.30 = (bf16[1,96,512]{2,1,0:T(8,128)(2,1)S(1)}, bf16[1,96,512]{2,1,0:T(8,128)(2,1)S(1)}, u32[]{:S(2)}, u32[]{:S(2)}) collective-permute-start(bf16[1,96,512]{2,1,0:T(8,128)(2,1)S(1)} %shard_map.153.refs_0_), channel_id=1, source_target_pairs={{0,24},{4,28},{8,16},{12,20},{16,8},{20,12},{24,0},{28,4},{1,25},{... | collective-permute-start | bytes 294920 | tf_op jit(solution)/shard_map/ppermute | solution.py:387
  193.3 9.0 %collective-permute-start.39 = (f32[33,768]{1,0:T(8,128)S(1)}, f32[33,768]{1,0:T(8,128)S(1)}, u32[]{:S(2)}, u32[]{:S(2)}) collective-permute-start(f32[33,768]{1,0:T(8,128)S(1)} %add.53), channel_id=1, source_target_pairs={{0,2},{1,3},{2,0},{3,1},{4,6},{5,7},{6,4},{7,5},{8,10},{9,11},{10,... | collective-permute-start | bytes 304136 | tf_op jit(solution)/shard_map/ppermute | solution.py:737
  202.2 1.8 collective-permute-start.35
  202.3 3.9 %collective-permute-start.40 = (f32[33,768]{1,0:T(8,128)S(1)}, f32[33,768]{1,0:T(8,128)S(1)}, u32[]{:S(2)}, u32[]{:S(2)}) collective-permute-start(f32[33,768]{1,0:T(8,128)S(1)} %add_multiply_fusion), channel_id=1, source_target_pairs={{0,4},{4,0},{8,12},{12,8},{16,20},{20,16},{24,28},{28,24},{1,5},{5... | collective-permute-start | bytes 304136 | tf_op jit(solution)/shard_map/ppermute | solution.py:384
  (31 other events, 210.7 us)
